TPU v7x, 32 devices: a whole 2x2x4 slice. The times are simulated.
32 devices in a mesh: dp: 8 (over z, y), heads: 4 (over x, core).
Axes of the slice: x: 2, y: 2, z: 4, core: 2. Of those that a mesh axis runs over, the one named last changes fastest.
Arguments:
- tokens: bfloat16 [8192, 768], P('dp'), may hold values from -6 to 6
- cotangent: bfloat16 [8192, 768], P('dp'), as said below
- clip_ids: int32 [8, 1024], P('dp'), may hold values from 0 to 3, as said below
- frame_ids: int32 [8, 1024], P('dp'), may hold values from -1 to 21, as said below
- patch_ids: int32 [8, 1024], P('dp'), may hold values from -1 to 63, as said below
- weights: float32 [768, 13056], P('dp', 'heads'), as said below
- weights_m: float32 [768, 13056], P('dp', 'heads'), may hold values from -3 to 3
- weights_v: float32 [768, 13056], P('dp', 'heads'), may hold values from 0.25 to 1
- weights_ema: float32 [768, 13056], P('dp', 'heads'), as said below
- vectors: float32 [10, 768], P(None, 'dp'), as said below
- vectors_m: float32 [10, 768], P(None, 'dp'), may hold values from -9 to 9
- vectors_v: float32 [10, 768], P(None, 'dp'), may hold values from 2.25 to 9
- vectors_ema: float32 [10, 768], P(None, 'dp'), as said below
Outputs:
- layer_out: float32 [8192, 768], P('dp')
- input_grad: float32 [8192, 768], P('dp')
- weight_grad: float32 [768, 13056], P('dp', 'heads')
- vector_grad: float32 [10, 768], P(None, 'dp')
- grad_norm: float32 [], replicated
- weights_new: float32 [768, 13056], P('dp', 'heads')
- weights_m_new: float32 [768, 13056], P('dp', 'heads')
- weights_v_new: float32 [768, 13056], P('dp', 'heads')
- weights_ema_new: float32 [768, 13056], P('dp', 'heads')
- vectors_new: float32 [10, 768], P(None, 'dp')
- vectors_m_new: float32 [10, 768], P(None, 'dp')
- vectors_v_new: float32 [10, 768], P(None, 'dp')
- vectors_ema_new: float32 [10, 768], P(None, 'dp')
Inputs may be any that keep to these rules, and one draw needn't show every extreme that they name: `clip_ids`: within a sequence clip ids never fall and start at 0 on the first row; each clip begins with its class row (frame and patch id -1). `frame_ids`: after its class row a clip holds frames of one patch count between 24 and 64 in order; its last frame may be short. `patch_ids`: patch ids count from 0 within each frame. `cotangent`: entries of order one. `weights`: matrices scaled by their fan-in. `weights_ema`: of the size of weights. `vectors`: gains near one and small biases. `vectors_ema`: of the size of vectors.
All inputs are finite; a program needn't handle non-finite values.
Results may differ from a plain program's by a relative error of at most 0.02.
The roundings to bfloat16 on the way count: a program that leaves them out, or rounds other values in their place, can miss the bound.
Values may be sent and summed in bfloat16 or wider, within the bound.
No kernel may reach another device: no remote copies, remote signals or barrier semaphores. Data moves between devices by JAX's collectives and lax.ppermute only.
A program may use at most 192 MiB of HBM per device.

v0:
```python
import math
from functools import partial

import jax
import jax.numpy as jnp
from jax import lax
from jax.experimental import pallas as pl
from jax.experimental.pallas import tpu as pltpu
from jax.sharding import PartitionSpec as P

HEAD_DIM = 64
STEP = 5
NPARAM = 10034688
VECTORS = 10

NORM_EPS = 1e-06
BETA_FIRST = 0.5
BETA_SECOND = 0.5
AVERAGE_RATE = 0.5
MATRIX_RATE = 0.03
VECTOR_RATE = 0.3
MATRIX_DECAY = 0.05
ADAM_EPS = 1e-08
MASKED = -1e30
SCALE = HEAD_DIM ** (-0.5)
F32 = jnp.float32
BF16 = jnp.bfloat16

BLOCK = 128
WINDOW = 256
CLASSES = 8
CHUNK = 256
LONG = 40_000_000_000

VMEM = pl.BlockSpec(memory_space=pltpu.VMEM)
SMEM = pl.BlockSpec(memory_space=pltpu.SMEM)


def core_swap(value):
    return lax.ppermute(value, "heads", [(i, i ^ 1) for i in range(4)])


def x_swap(value):
    return lax.ppermute(value, "heads", [(i, i ^ 2) for i in range(4)])


def dp_swap(value, mask):
    count = lax.axis_size("dp")
    return lax.ppermute(value, "dp", [(i, i ^ mask) for i in range(count)])


def after(value, *others):
    return lax.optimization_barrier((value, *others))[0]


def together(*groups):
    flat = lax.optimization_barrier([one for group in groups for one in group])
    split, at = [], 0
    for group in groups:
        split.append(list(flat[at : at + len(group)]))
        at += len(group)
    return split


def shaped(shape, dtype):
    return jax.ShapeDtypeStruct(shape, dtype)


def local_call(name, kernel, outs, *operands, scratch=(), smem=(), extra=6, flops=0):
    held = sum(math.prod(one.shape) * jnp.dtype(one.dtype).itemsize for one in scratch)
    return pl.pallas_call(
        kernel,
        name=name,
        out_shape=list(outs),
        in_specs=[SMEM if i in smem else VMEM for i in range(len(operands))],
        out_specs=[VMEM] * len(outs),
        scratch_shapes=list(scratch),
        compiler_params=pltpu.CompilerParams(
            vmem_limit_bytes=held + extra * 2**20
        ),
        cost_estimate=pl.CostEstimate(flops=flops, bytes_accessed=0, transcendentals=0),
    )(*operands)


def dot(left, right):
    return jnp.dot(left, right, preferred_element_type=F32)


def dot_nt(left, right):
    return lax.dot_general(left, right, (((1,), (1,)), ((), ())), preferred_element_type=F32)


def dot_tn(left, right):
    return lax.dot_general(left, right, (((0,), (0,)), ((), ())), preferred_element_type=F32)


def dot_tn_exact(left, right):
    return lax.dot_general(
        left, right, (((0,), (0,)), ((), ())), preferred_element_type=F32, precision=lax.Precision.HIGHEST
    )


def chunk_loop(rows, body, size=CHUNK):
    def step(i, carry):
        body(pl.ds(pl.multiple_of(i * size, size), size))
        return carry

    lax.fori_loop(0, rows // size, step, 0)


def normed(stream):
    center = stream - jnp.mean(stream, -1, keepdims=True)
    factor = lax.rsqrt(jnp.mean(center * center, -1, keepdims=True) + NORM_EPS)
    return center * factor, factor


def norm_grad(hat, factor, gain, grad):
    scaled = grad * gain
    return factor * (
        scaled - jnp.mean(scaled, -1, keepdims=True) - hat * jnp.mean(scaled * hat, -1, keepdims=True)
    )


def column_sum(value):
    return jnp.sum(value, 0, keepdims=True)


def z_blocks(piece):
    return [piece] + [dp_swap(piece, 2 * k) for k in range(1, lax.axis_size("dp") // 2)]


def y_blocks(mine, fine=False):
    return [dp_swap(one, 1) for one in mine] if fine else [dp_swap(jnp.stack(mine), 1)]


def assemble(name, mine, other):
    half, count, fine = len(mine), lax.axis_size("dp"), len(other) > 1
    rows, columns = mine[0].shape

    def kernel(place_ref, *refs):
        out_ref = refs[-1]
        z, y = place_ref[0], place_ref[1]
        for k in range(half):
            out_ref[(z ^ k) * 2 + y] = refs[k][...]
            out_ref[(z ^ k) * 2 + (1 - y)] = refs[half + k][...] if fine else refs[half][k]

    (out,) = local_call(
        name, kernel, [shaped((count, rows, columns), mine[0].dtype)], places(), *mine, *other, smem=(0,)
    )
    return out.reshape(count * rows, columns)


def places():
    dp, heads = lax.axis_index("dp"), lax.axis_index("heads")
    return jnp.stack([dp // 2, dp % 2, heads, heads % 2]).astype(jnp.int32)


def split_rows(name, totals, fine=False):
    count = lax.axis_size("dp")
    half = count // 2
    operands, columns = [], 0
    for own, received in totals:
        rows = own.shape[0] // count
        operands += [one.reshape(count, rows, own.shape[1]) for one in (own, received) if one is not None]
        columns += own.shape[1]

    def kernel(place_ref, *refs):
        ins, outs = refs[: len(operands)], refs[len(operands) :]
        z, y = place_ref[0], place_ref[1]
        for k in range(half):
            for side in range(2):
                block = (z ^ k) * 2 + (1 - y if side == 0 else y)
                at, column = 0, 0
                for own, received in totals:
                    value = ins[at][block].astype(F32)
                    at += 1
                    if received is not None:
                        value = value + ins[at][block].astype(F32)
                        at += 1
                    part = slice(column, column + own.shape[1])
                    column += own.shape[1]
                    if side == 1:
                        outs[-1][k, :, part] = value
                    elif fine:
                        outs[k][:, part] = value.astype(BF16)
                    else:
                        outs[0][k, :, part] = value.astype(BF16)

    sends = [shaped((rows, columns), BF16)] * half if fine else [shaped((half, rows, columns), BF16)]
    outs = local_call(
        name, kernel, [*sends, shaped((half, rows, columns), F32)], places(), *operands, smem=(0,)
    )
    return outs[:-1], outs[-1]


def y_sums(keep, arrived):
    half = keep.shape[0]
    arrived = arrived if len(arrived) > 1 else [arrived[0][k] for k in range(half)]
    return [keep[k] + arrived[k].astype(F32) for k in range(half)]


def z_swaps(summed):
    return [dp_swap(summed[k].astype(BF16), 2 * k) for k in range(1, len(summed))]


def head_parts(width):
    parts = []
    for head in range(width // HEAD_DIM):
        start = head // 2 * 2 * HEAD_DIM
        stop = min(start + 2 * HEAD_DIM, width)
        parts.append((start, stop, head % 2 if stop - start == 2 * HEAD_DIM else None))
    return parts


def half_only(value, half):
    if half is None:
        return value
    lane = lax.broadcasted_iota(jnp.int32, value.shape, 1)
    return jnp.where((lane >= HEAD_DIM) == bool(half), value, jnp.zeros_like(value))


def softmax_columns(score_parts):
    top = jnp.max(score_parts[0], 0, keepdims=True)
    for one in score_parts[1:]:
        top = jnp.maximum(top, jnp.max(one, 0, keepdims=True))
    exps = [jnp.exp(one - top) for one in score_parts]
    total = sum(jnp.sum(one, 0, keepdims=True) for one in exps)
    return exps, top, total


def masked_bias(allowed):
    return jnp.where(allowed, 0.0, MASKED).astype(F32)


def head_forward(q, half, key_parts, value_parts, biases):
    q = half_only(q, half)
    scores = [dot_nt(k, q) + bias for k, bias in zip(key_parts, biases)]
    exps, top, total = softmax_columns(scores)
    out = sum(dot_tn(v, e.astype(BF16)) for v, e in zip(value_parts, exps)) / total
    if half is not None:
        out = out[half * HEAD_DIM : (half + 1) * HEAD_DIM]
    return out, top + jnp.log(total)


def head_backward(q, grad, half, key_parts, value_parts, biases, log_row):
    q, grad = half_only(q, half), half_only(grad, half)
    probs = [jnp.exp(dot_nt(k, q) + bias - log_row) for k, bias in zip(key_parts, biases)]
    grad_probs = [dot_nt(v, grad) for v in value_parts]
    delta = sum(jnp.sum(p * d, 0, keepdims=True) for p, d in zip(probs, grad_probs))
    grad_scores = [(p * (d - delta)).astype(BF16) for p, d in zip(probs, grad_probs)]
    grad_q = sum(dot_tn(k, s) for k, s in zip(key_parts, grad_scores))
    if half is not None:
        grad_q = grad_q[half * HEAD_DIM : (half + 1) * HEAD_DIM]
    grad_k = [dot(s, q) for s in grad_scores]
    grad_v = [dot(p.astype(BF16), grad) for p in probs]
    return grad_q * SCALE, grad_k, grad_v


def sort_kernel(col_ref, row_ref, tokens_ref, sorted_ref, order_ref, back_ref, code_col_ref, code_row_ref):
    count = tokens_ref.shape[0]
    key_row = (row_ref[0:1] * 128 + row_ref[2:3] + 1) * 64 + row_ref[1:2] + 1
    key_col = (col_ref[:, 0:1] * 128 + col_ref[:, 2:3] + 1) * 64 + col_ref[:, 1:2] + 1
    rank_row = jnp.zeros((1, count), jnp.int32)
    for i in range(0, count, CHUNK):
        smaller = key_col[i : i + CHUNK] < key_row
        rank_row = rank_row + jnp.sum(smaller.astype(jnp.int32), 0, keepdims=True)
    for i in range(0, count, CHUNK):
        at = slice(i, i + CHUNK)
        place = lax.broadcasted_iota(jnp.int32, (CHUNK, count), 0) + i
        order = (place == rank_row).astype(F32).astype(BF16)
        order_ref[at, :] = order
        rank_col = jnp.sum((key_row < key_col[at]).astype(jnp.int32), 1, keepdims=True)
        place = lax.broadcasted_iota(jnp.int32, (CHUNK, count), 1)
        back_ref[at, :] = (place == rank_col).astype(F32).astype(BF16)
        sorted_ref[at, :] = dot(order, tokens_ref[...]).astype(BF16)
        cols = dot(order, col_ref[...].astype(F32).astype(BF16))
        code_col_ref[at, :] = cols
        code_row_ref[:, at] = dot_nt(row_ref[...].astype(F32).astype(BF16), order)


def same_clip_patch(col_ref, row_ref, keys, queries):
    key = col_ref[keys, :]
    query = row_ref[:, queries]
    return (key[:, 0:1] * 128 + key[:, 2:3]) == (query[0:1] * 128 + query[2:3])


def temporal_window(i, count):
    first = i * BLOCK
    start = jnp.clip(first - (WINDOW - BLOCK) // 2, 0, count - WINDOW)
    return (
        pl.ds(pl.multiple_of(first, BLOCK), BLOCK),
        pl.ds(pl.multiple_of(start, (WINDOW - BLOCK) // 2), WINDOW),
    )


def time_forward_kernel(
    maps_ref, tokens_ref, back_ref, col_ref, row_ref,
    vec_ref, first_ref, inputs_ref, own_ref, far_ref, log_ref, heads_ref,
):
    count, width = tokens_ref.shape[0], own_ref.shape[1]
    columns = maps_ref.shape[1]
    lanes = maps_ref[:, columns - 128 :].astype(F32).T
    offset = 3 * width - (columns - 128)
    vec_ref[...] = lanes[offset : offset + 16]
    gain, shift = vec_ref[0:1], vec_ref[1:2]

    def project(at):
        hat, _ = normed(tokens_ref[at, :].astype(F32))
        first = (hat * gain + shift).astype(BF16)
        first_ref[at, :] = first
        inputs_ref[at, :] = dot(first, maps_ref[:, : 3 * width]).astype(BF16)

    chunk_loop(count, project)

    def step(i, carry):
        queries, keys = temporal_window(i, count)
        bias = masked_bias(same_clip_patch(col_ref, row_ref, keys, queries))
        outs, logs = [], []
        for start, stop, half in head_parts(width):
            q = inputs_ref[queries, start:stop] * BF16(SCALE)
            k = inputs_ref[keys, width + start : width + stop]
            v = inputs_ref[keys, 2 * width + start : 2 * width + stop]
            out, log = head_forward(q, half, [k], [v], [bias])
            outs.append(out)
            logs.append(log)
        heads_ref[queries, :] = jnp.concatenate(outs, 0).T.astype(BF16)
        log_ref[:, queries] = jnp.concatenate(logs + [logs[0]] * (8 - len(logs)), 0)
        return carry

    lax.fori_loop(0, count // BLOCK, step, 0)
    rows = count // 2
    for i in range(0, rows, CHUNK):
        own_ref[i : i + CHUNK, :] = dot(back_ref[i : i + CHUNK, :], heads_ref[...]).astype(BF16)
        far_ref[i : i + CHUNK, :] = dot(back_ref[rows + i : rows + i + CHUNK, :], heads_ref[...]).astype(BF16)


def time_backward_kernel(
    own_ref, far_ref, order_ref, inputs_ref, log_ref, col_ref, row_ref,
    out_ref, grad_ref, sum_ref,
):
    count, width = inputs_ref.shape[0], own_ref.shape[1]
    rows = count // 2
    for i in range(0, count, CHUNK):
        grad_ref[i : i + CHUNK, :] = (
            dot(order_ref[i : i + CHUNK, :rows], own_ref[...]) + dot(order_ref[i : i + CHUNK, rows:], far_ref[...])
        ).astype(BF16)
    sum_ref[...] = jnp.zeros_like(sum_ref)

    def step(i, carry):
        queries, keys = temporal_window(i, count)
        bias = masked_bias(same_clip_patch(col_ref, row_ref, keys, queries))
        grad_qs, pairs = [], {}
        for head, (start, stop, half) in enumerate(head_parts(width)):
            q = inputs_ref[queries, start:stop] * BF16(SCALE)
            k = inputs_ref[keys, width + start : width + stop]
            v = inputs_ref[keys, 2 * width + start : 2 * width + stop]
            grad_q, grad_k, grad_v = head_backward(
                q, grad_ref[queries, start:stop], half, [k], [v], [bias], log_ref[head : head + 1, queries]
            )
            grad_qs.append(grad_q)
            before = pairs.get((start, stop))
            pairs[start, stop] = (
                (grad_k[0], grad_v[0]) if before is None else (before[0] + grad_k[0], before[1] + grad_v[0])
            )
        out_ref[queries, :width] = jnp.concatenate(grad_qs, 0).T.astype(BF16)
        for (start, stop), (grad_k, grad_v) in pairs.items():
            sum_ref[keys, start:stop] += grad_k
            sum_ref[keys, width + start : width + stop] += grad_v
        return carry

    lax.fori_loop(0, count // BLOCK, step, 0)

    def store(at):
        out_ref[at, width:] = sum_ref[at, :].astype(BF16)

    chunk_loop(count, store)


def space_window(i, core, rows):
    first = core * rows + i * BLOCK
    start = jnp.clip(first - (WINDOW - BLOCK) // 2, 0, 2 * rows - WINDOW)
    return (
        pl.ds(pl.multiple_of(i * BLOCK, BLOCK), BLOCK),
        pl.ds(pl.multiple_of(first, BLOCK), BLOCK),
        pl.ds(pl.multiple_of(start, (WINDOW - BLOCK) // 2), WINDOW),
    )


def whole_pairs(core, pairs_ref, got_ref, whole_ref):
    rows, width = pairs_ref.shape[0], pairs_ref.shape[1] // 4
    whole_ref[pl.ds(pl.multiple_of(core * rows, rows), rows), :] = pairs_ref[...]
    there = pl.ds(pl.multiple_of((1 - core) * rows, rows), rows)
    for i, j in enumerate((1, 0, 3, 2)):
        whole_ref[there, i * width : (i + 1) * width] = got_ref[:, j * width : (j + 1) * width]


def class_rows(row):
    number = lax.broadcasted_iota(jnp.int32, (CLASSES, row.shape[1]), 0)
    return (row[0:1] == number) & (row[1:2] < 0)


def space_biases(col_ref, row_ref, queries, keys):
    key, query = col_ref[keys, :], row_ref[:, queries]
    frame = jnp.where(key[:, 1:2] < 0, -1, key[:, 0:1] * 128 + key[:, 1:2]) == query[0:1] * 128 + query[1:2]
    number = lax.broadcasted_iota(jnp.int32, (CLASSES, BLOCK), 0)
    return [masked_bias(frame & (query[1:2] >= 0)), masked_bias(number == query[0:1])]


def class_allowed(row_ref):
    number = lax.broadcasted_iota(jnp.int32, (CLASSES, row_ref.shape[1]), 0)
    return row_ref[0:1] == number


def space_forward_kernel(
    place_ref, q_ref, pairs_ref, got_ref, col_ref, row_ref, out_own_ref, out_far_ref,
    heads_ref, log_ref, class_log_ref, part_ref, whole_ref, class_ref,
):
    core = place_ref[3]
    rows, width = q_ref.shape
    whole_pairs(core, pairs_ref, got_ref, whole_ref)
    here = pl.ds(pl.multiple_of(core * rows, rows), rows)
    classes = class_rows(row_ref[...]).astype(F32).astype(BF16)
    own_classes = class_rows(row_ref[:, here]).astype(F32).astype(BF16)
    class_ref[...] = dot(classes, whole_ref[...]).astype(BF16)
    parts = head_parts(width)

    def step(i, carry):
        local, queries, keys = space_window(i, core, rows)
        biases = space_biases(col_ref, row_ref, queries, keys)
        outs, logs = [], []
        for start, stop, half in parts:
            out, log = head_forward(
                q_ref[local, start:stop] * BF16(SCALE),
                half,
                [whole_ref[keys, start:stop], class_ref[:, start:stop]],
                [whole_ref[keys, width + start : width + stop], class_ref[:, width + start : width + stop]],
                biases,
            )
            outs.append(out)
            logs.append(log)
        heads_ref[local, :] = jnp.concatenate(outs, 0).T.astype(BF16)
        log_ref[:, local] = jnp.concatenate(logs + [logs[0]] * (8 - len(logs)), 0)
        return carry

    lax.fori_loop(0, rows // BLOCK, step, 0)

    bias = masked_bias(class_allowed(row_ref))
    class_q = dot(own_classes, q_ref[...]).astype(BF16) * BF16(SCALE)
    outs, logs = [], []
    for start, stop, half in parts:
        scores = dot_nt(half_only(class_q[:, start:stop], half), whole_ref[:, start:stop]) + bias
        top = jnp.max(scores, 1, keepdims=True)
        exps = jnp.exp(scores - top)
        total = jnp.sum(exps, 1, keepdims=True)
        out = dot(exps.astype(BF16), whole_ref[:, width + start : width + stop]) / total
        if half:
            outs[-1] = jnp.where(lax.broadcasted_iota(jnp.int32, out.shape, 1) >= HEAD_DIM, out, outs[-1])
        else:
            outs.append(out)
        logs.append(top + jnp.log(total))
    class_log_ref[...] = jnp.concatenate(logs + [logs[0]] * (8 - len(logs)), 1)
    class_out = jnp.concatenate(outs, 1).astype(BF16)
    is_class = col_ref[here, 1:2] < 0

    def replace(at):
        back = dot_tn(own_classes, class_out).astype(BF16)
        heads_ref[...] = jnp.where(is_class, back, heads_ref[...])

    replace(None)
    group = width // 2

    def project(at):
        part_ref[at, :] = (
            dot_nt(heads_ref[at, :group], out_own_ref[:, 3 * group :])
            + dot_nt(heads_ref[at, group:], out_far_ref[:, 3 * group :])
        ).astype(BF16)

    chunk_loop(rows, project)


def space_back_in_kernel(
    part_ref, got_ref, stream_ref, vec_ref, dy_ref, out_own_ref, out_far_ref, grad_ref, low_ref, sums_ref, heads_ref
):
    group = heads_ref.shape[1] // 2
    gain = vec_ref[7:8]
    sums_ref[...] = jnp.zeros_like(sums_ref)

    def through_norm(at):
        grad = part_ref[at, :].astype(F32) + got_ref[at, :].astype(F32)
        hat, factor = normed(stream_ref[at, :])
        dy = dy_ref[at, :].astype(F32)
        dx = dy + norm_grad(hat, factor, gain, grad)
        grad_ref[at, :] = dx
        low = dx.astype(BF16)
        low_ref[at, :] = low
        heads_ref[at, :group] = dot(low, out_own_ref[:, 3 * group :]).astype(BF16)
        heads_ref[at, group:] = dot(low, out_far_ref[:, 3 * group :]).astype(BF16)
        sums_ref[0:4] += jnp.concatenate(
            [column_sum(dx), column_sum(grad * hat), column_sum(grad), column_sum(dy)], 0
        )

    chunk_loop(grad_ref.shape[0], through_norm)


def space_backward_kernel(
    place_ref, heads_ref, q_ref, pairs_ref, got_ref, log_ref, class_log_ref, col_ref, row_ref,
    dq_ref, keep_ref, send_ref,
    whole_ref, class_ref, total_ref, class_total_ref, class_dq_ref,
):
    core = place_ref[3]
    rows, width = q_ref.shape
    whole_pairs(core, pairs_ref, got_ref, whole_ref)
    here = pl.ds(pl.multiple_of(core * rows, rows), rows)
    there = pl.ds(pl.multiple_of((1 - core) * rows, rows), rows)
    classes = class_rows(row_ref[...]).astype(F32)
    own_classes = class_rows(row_ref[:, here]).astype(F32).astype(BF16)
    class_ref[...] = dot(classes.astype(BF16), whole_ref[...]).astype(BF16)
    class_total_ref[...] = jnp.zeros_like(class_total_ref)
    parts = head_parts(width)
    is_class_row = row_ref[1:2, here] < 0

    bias = masked_bias(class_allowed(row_ref))
    class_q = dot(own_classes, q_ref[...]).astype(BF16) * BF16(SCALE)
    class_g = dot(own_classes, heads_ref[...]).astype(BF16)
    for head, (start, stop, half) in enumerate(parts):
        keys, values = whole_ref[:, start:stop], whole_ref[:, width + start : width + stop]
        q, grad = half_only(class_q[:, start:stop], half), half_only(class_g[:, start:stop], half)
        probs = jnp.exp(dot_nt(q, keys) + bias - class_log_ref[:, head : head + 1])
        grad_probs = dot_nt(grad, values)
        grad_scores = (probs * (grad_probs - jnp.sum(probs * grad_probs, 1, keepdims=True))).astype(BF16)
        grad_q = half_only(dot(grad_scores, keys) * SCALE, half).astype(BF16)
        grad_k, grad_v = dot_tn(grad_scores, q), dot_tn(probs.astype(BF16), grad)
        if half:
            class_dq_ref[:, start:stop] += grad_q
            total_ref[:, start:stop] += grad_k
            total_ref[:, width + start : width + stop] += grad_v
        else:
            class_dq_ref[:, start:stop] = grad_q
            total_ref[:, start:stop] = grad_k
            total_ref[:, width + start : width + stop] = grad_v

    def step(i, carry):
        local, queries, keys = space_window(i, core, rows)
        biases = space_biases(col_ref, row_ref, queries, keys)
        is_class = row_ref[1:2, queries] < 0
        grad_qs, pairs = [], {}
        for head, (start, stop, half) in enumerate(parts):
            log_row = jnp.where(is_class, -MASKED, log_ref[head : head + 1, local])
            grad_q, grad_k, grad_v = head_backward(
                q_ref[local, start:stop] * BF16(SCALE),
                heads_ref[local, start:stop],
                half,
                [whole_ref[keys, start:stop], class_ref[:, start:stop]],
                [whole_ref[keys, width + start : width + stop], class_ref[:, width + start : width + stop]],
                biases,
                log_row,
            )
            grad_qs.append(grad_q)
            new = grad_k + grad_v
            before = pairs.get((start, stop))
            pairs[start, stop] = new if before is None else [a + b for a, b in zip(before, new)]
        dq_ref[local, :] = jnp.concatenate(grad_qs, 0).T.astype(BF16)
        for (start, stop), (frame_k, class_k, frame_v, class_v) in pairs.items():
            total_ref[keys, start:stop] += frame_k
            total_ref[keys, width + start : width + stop] += frame_v
            class_total_ref[:, start:stop] += class_k
            class_total_ref[:, width + start : width + stop] += class_v
        return carry

    lax.fori_loop(0, rows // BLOCK, step, 0)
    dq_ref[...] = jnp.where(
        col_ref[here, 1:2] < 0, dot_tn(own_classes, class_dq_ref[...]).astype(BF16), dq_ref[...]
    )
    total_ref[...] += dot_tn_exact(classes, class_total_ref[...])
    keep_ref[...] = total_ref[here, :]
    send_ref[...] = total_ref[there, :].astype(BF16)


def mix_kernel(place_ref, out_ref, own_ref, x_ref, core_ref, vec_ref, mix_ref, fused_ref, bias_ref):
    place = place_ref[2]
    width = out_ref.shape[1]
    mix_ref[0] = own_ref[...]
    mix_ref[1] = core_ref[:, :width]
    mix_ref[2] = x_ref[...]
    mix_ref[3] = core_ref[:, width:]
    total, bias = 0.0, 0.0
    low = vec_ref[...].astype(BF16)
    for j in range(4):
        block = mix_ref[place ^ j]
        total = total + dot(block, out_ref[j * width : (j + 1) * width, :])
        bias = bias + dot_nt(low[:, j * width : (j + 1) * width], block)
    fused_ref[...] = total.astype(BF16)
    bias_ref[...] = bias[2:3] + vec_ref[3:4]


def time_out_kernel(own_ref, got_ref, fused_ref, far_ref, part_ref):
    def project(at):
        part_ref[at, :] = (dot_nt(own_ref[at, :], fused_ref[...]) + dot_nt(got_ref[at, :], far_ref[...])).astype(BF16)

    chunk_loop(part_ref.shape[0], project)


def norm_in_kernel(gain_row, before_ref, part_ref, got_ref, shift_ref, vec_ref, stream_ref, normed_ref):
    gain, shift = vec_ref[gain_row : gain_row + 1], vec_ref[gain_row + 1 : gain_row + 2]

    def body(at):
        stream = (
            before_ref[at, :].astype(F32)
            + (part_ref[at, :].astype(F32) + got_ref[at, :].astype(F32))
            + shift_ref[0:1]
        )
        stream_ref[at, :] = stream
        hat, _ = normed(stream)
        normed_ref[at, :] = (hat * gain + shift).astype(BF16)

    chunk_loop(stream_ref.shape[0], body)


def space_in_kernel(second_ref, own_ref, far_ref, q_ref, pairs_ref):
    width = q_ref.shape[1] // 2

    def project(at):
        for g, maps_ref in enumerate((own_ref, far_ref)):
            inputs = dot(second_ref[at, :], maps_ref[:, : 3 * width]).astype(BF16)
            q_ref[at, g * width : (g + 1) * width] = inputs[:, :width]
            pairs_ref[at, g * width : (g + 1) * width] = inputs[:, width : 2 * width]
            pairs_ref[at, (2 + g) * width : (3 + g) * width] = inputs[:, 2 * width :]

    chunk_loop(q_ref.shape[0], project)


def gelu_parts(pre):
    cdf = 0.5 * (1.0 + lax.erf(pre * (0.5**0.5)))
    slope = cdf + pre * jnp.exp(-0.5 * pre * pre) * (1.0 / math.sqrt(2.0 * math.pi))
    return pre * cdf, slope


def feed_kernel(
    third_ref, dy_ref, up_ref, up_far_ref, down_ref, down_far_ref, activ_ref, grad_ref, back_ref
):
    hidden = activ_ref.shape[1] // 2

    def project(at):
        back = 0.0
        for g, (ups_ref, downs_ref) in enumerate(((up_ref, down_ref), (up_far_ref, down_far_ref))):
            act, slope = gelu_parts(dot(third_ref[at, :], ups_ref[...]))
            part = slice(g * hidden, (g + 1) * hidden)
            activ_ref[at, part] = act.astype(BF16)
            grad = (dot(dy_ref[at, :], downs_ref[...]) * slope).astype(BF16)
            grad_ref[at, part] = grad
            back = back + dot_nt(grad, ups_ref[...])
        back_ref[at, :] = back.astype(BF16)

    chunk_loop(third_ref.shape[0], project)


def feed_out_kernel(activ_ref, own_ref, far_ref, part_ref):
    hidden = activ_ref.shape[1] // 2

    def project(at):
        part_ref[at, :] = (
            dot_nt(activ_ref[at, :hidden], own_ref[...]) + dot_nt(activ_ref[at, hidden:], far_ref[...])
        ).astype(BF16)

    chunk_loop(part_ref.shape[0], project)


def outer_kernel(left_ref, right_ref, own_ref, far_ref):
    hidden = own_ref.shape[1]
    for g, ref in ((1, far_ref), (0, own_ref)):
        ref[...] = dot_tn(left_ref[...], right_ref[:, g * hidden : (g + 1) * hidden]).astype(BF16)


def space_back_kernel(dq_ref, keep_ref, got_ref, own_ref, far_ref, grad_own_ref, grad_far_ref, part_ref):
    width = dq_ref.shape[1] // 2

    def project(at):
        total = 0.0
        for g, (maps_ref, grad_ref) in enumerate(((own_ref, grad_own_ref), (far_ref, grad_far_ref))):
            grad_ref[at, :width] = dq_ref[at, g * width : (g + 1) * width]
            for i in (1, 2):
                mine = slice((2 * i - 2 + g) * width, (2 * i - 1 + g) * width)
                theirs = slice((2 * i - 1 - g) * width, (2 * i - g) * width)
                grad_ref[at, i * width : (i + 1) * width] = (
                    keep_ref[at, mine] + got_ref[at, theirs].astype(F32)
                ).astype(BF16)
            total = total + dot_nt(grad_ref[at, :], maps_ref[:, : 3 * width])
        part_ref[at, :] = total.astype(BF16)

    chunk_loop(part_ref.shape[0], project)


def space_grads_kernel(second_ref, own_grad_ref, far_grad_ref, low_ref, heads_ref, own_ref, far_ref):
    width = heads_ref.shape[1] // 2
    for g, grad_ref, ref in ((1, far_grad_ref, far_ref), (0, own_grad_ref, own_ref)):
        ref[:, : 3 * width] = dot_tn(second_ref[...], grad_ref[...]).astype(BF16)
        ref[:, 3 * width :] = dot_tn(low_ref[...], heads_ref[:, g * width : (g + 1) * width]).astype(BF16)


def time_back_in_kernel(
    part_ref, got_ref, stream_ref, vec_ref, before_ref, fused_ref, far_ref,
    grad_ref, low_ref, sums_ref, own_ref, send_ref,
):
    gain = vec_ref[4:5]
    sums_ref[...] = jnp.zeros_like(sums_ref)

    def through_norm(at):
        grad = part_ref[at, :].astype(F32) + got_ref[at, :].astype(F32)
        hat, factor = normed(stream_ref[at, :])
        dx = before_ref[at, :] + norm_grad(hat, factor, gain, grad)
        grad_ref[at, :] = dx
        low = dx.astype(BF16)
        low_ref[at, :] = low
        own_ref[at, :] = dot(low, fused_ref[...]).astype(BF16)
        send_ref[at, :] = dot(low, far_ref[...]).astype(BF16)
        sums_ref[0:4] += jnp.concatenate(
            [column_sum(low.astype(F32)), column_sum(dx), column_sum(grad * hat), column_sum(grad)], 0
        )

    chunk_loop(grad_ref.shape[0], through_norm)


def time_grads_kernel(place_ref, first_ref, grad_ref, *refs):
    sends, keep_ref, total_ref = refs[:-2], refs[-2], refs[-1]
    half, rows, columns = keep_ref.shape
    z, y = place_ref[0], place_ref[1]
    total_ref[...] = dot_tn(first_ref[...], grad_ref[...])
    for k in range(half):
        mine = pl.ds(pl.multiple_of(((z ^ k) * 2 + y) * rows, 8), rows)
        theirs = pl.ds(pl.multiple_of(((z ^ k) * 2 + (1 - y)) * rows, 8), rows)
        sends[k][...] = total_ref[theirs, :].astype(BF16)
        keep_ref[k] = total_ref[mine, :]


def time_back_kernel(
    grad_ref, maps_ref, tokens_ref, back_ref, bias_ref, one_ref, two_ref, own_ref, far_ref, sums_ref, sorted_ref
):
    count, width = tokens_ref.shape[0], grad_ref.shape[1] // 3
    sums_ref[...] = jnp.zeros_like(sums_ref)
    sums_ref[2:3] = 0.5 * bias_ref[0:1]
    sums_ref[3:6] = 0.5 * one_ref[1:4]
    sums_ref[6:10] = 0.5 * two_ref[0:4]
    sums_ref[10:11] = 0.5 * one_ref[0:1]

    def project(at):
        grad = dot_nt(grad_ref[at, :], maps_ref[:, : 3 * width])
        hat, _ = normed(tokens_ref[at, :].astype(F32))
        sums_ref[0:2] += jnp.concatenate([column_sum(grad * hat), column_sum(grad)], 0)
        sorted_ref[at, :] = grad.astype(BF16)

    chunk_loop(count, project)
    rows = count // 2
    for i in range(0, rows, CHUNK):
        far_ref[i : i + CHUNK, :] = dot(back_ref[rows + i : rows + i + CHUNK, :], sorted_ref[...]).astype(BF16)
    for i in range(0, rows, CHUNK):
        own_ref[i : i + CHUNK, :] = dot(back_ref[i : i + CHUNK, :], sorted_ref[...]).astype(BF16)


def input_grad_kernel(part_ref, got_ref, tokens_ref, vec_ref, before_ref, out_ref):
    gain = vec_ref[0:1]

    def through_norm(at):
        grad = part_ref[at, :].astype(F32) + got_ref[at, :].astype(F32)
        hat, factor = normed(tokens_ref[at, :].astype(F32))
        out_ref[at, :] = before_ref[at, :] + norm_grad(hat, factor, gain, grad)

    chunk_loop(out_ref.shape[0], through_norm)


def layer_out_kernel(stream_ref, part_ref, got_ref, vec_ref, out_ref):
    out_ref[...] = stream_ref[...] + (part_ref[...].astype(F32) + got_ref[...].astype(F32)) + vec_ref[9:10]


def whole_rows_kernel(place_ref, own_ref, got_ref, out_ref):
    core = place_ref[3]
    rows = own_ref.shape[0]
    out_ref[pl.ds(pl.multiple_of(core * rows, rows), rows), :] = own_ref[...]
    out_ref[pl.ds(pl.multiple_of((1 - core) * rows, rows), rows), :] = got_ref[...]


def fused_grads_kernel(low_ref, heads_ref, got_heads_ref, own_ref, far_ref):
    far_ref[...] = dot_tn(low_ref[...], got_heads_ref[...]).astype(BF16)
    own_ref[...] = dot_tn(low_ref[...], heads_ref[...])


def mix_grads_kernel(
    place_ref, fused_ref, got_ref, mix_ref, sums_ref, grad_out_ref, total_ref, bias_ref
):
    place = place_ref[2]
    width = fused_ref.shape[1]
    fused = (fused_ref[...] + got_ref[...].astype(F32)).astype(BF16)
    total_ref[...] = fused
    for j in range(4):
        block = mix_ref[place ^ j]
        grad_out_ref[j * width : (j + 1) * width, :] = dot_tn(block, fused).astype(BF16)
        bias_ref[:, j * width : (j + 1) * width] = dot(sums_ref[...].astype(BF16), block)


def mix_shard_kernel(place_ref, fused_ref, out_ref, keep_ref, send_ref):
    place = place_ref[2]
    width = out_ref.shape[1]
    fused = fused_ref[...].astype(BF16)
    for m in range(4):
        rows = out_ref[pl.ds(pl.multiple_of((place ^ m) * width, width), width), :]
        part = dot_nt(fused, rows)
        ref = send_ref if m % 2 else keep_ref
        ref[:, m // 2 * width : (m // 2 + 1) * width] = part.astype(ref.dtype)


def whole_grad_kernel(counts, *refs):
    out_ref, square_ref = refs[-2:]
    at, column, square = 0, 0, 0.0
    for count in counts:
        value = refs[at][...].astype(F32)
        for ref in refs[at + 1 : at + count]:
            value = value + ref[...].astype(F32)
        at += count
        out_ref[:, column : column + value.shape[1]] = value
        column += value.shape[1]
        square = square + jnp.sum(value * value)
    square_ref[...] = jnp.full(square_ref.shape, square, F32)


def adam_update(master, first_moment, second_moment, average, gradient, factor, rate, decay):
    clipped = gradient * factor
    first_new = BETA_FIRST * first_moment + (1.0 - BETA_FIRST) * clipped
    second_new = BETA_SECOND * second_moment + (1.0 - BETA_SECOND) * clipped * clipped
    first_hat = first_new / (1.0 - BETA_FIRST**STEP)
    second_hat = second_new / (1.0 - BETA_SECOND**STEP)
    master_new = master - rate * (first_hat / (jnp.sqrt(second_hat) + ADAM_EPS) + decay * master)
    average_new = AVERAGE_RATE * average + (1.0 - AVERAGE_RATE) * master_new
    return (master_new, first_new, second_new, average_new)


def local(
    tokens,
    cotangent,
    clip_ids,
    frame_ids,
    patch_ids,
    weights,
    weights_m,
    weights_v,
    weights_ema,
    vectors,
    vectors_m,
    vectors_v,
    vectors_ema,
):
    group_count = lax.axis_size("heads")
    core = lax.axis_index("heads") % 2
    place = places()
    count, features = tokens.shape
    width = features // group_count
    hidden = (weights.shape[1] - 9 * width) // 2
    rows = count // 2
    half = lax.axis_size("dp") // 2
    shard = weights.shape[0]

    def in_order(value):
        return jnp.concatenate(
            [lax.dynamic_slice_in_dim(value, (core ^ k) * rows, rows, 0) for k in range(2)], 0
        )

    def id_arrays(values):
        return jnp.stack(values + [values[0]] * 5, 1), jnp.stack(values + [values[0]] * 5, 0)

    ids = [one[0] for one in (clip_ids, frame_ids, patch_ids)]
    space_ids = id_arrays(ids)
    order_col, order_row = id_arrays([in_order(one) for one in ids])
    tokens_all = in_order(tokens)
    tokens_own = tokens_all[:rows]
    dy = lax.dynamic_slice_in_dim(cotangent, core * rows, rows, 0)

    wide = lambda n, dtype: shaped((rows, n), dtype)
    tokens_sorted, order, back, time_col, time_row = local_call(
        "sort_rows",
        sort_kernel,
        [
            shaped((count, features), BF16),
            shaped((count, count), BF16),
            shaped((count, count), BF16),
            shaped((count, 8), F32),
            shaped((8, count), F32),
        ],
        order_col, order_row, tokens_all,
    )

    low = weights.astype(BF16)
    spare = jnp.zeros((shard, -(-(3 * width + 16) // 128) * 128 - 3 * width - VECTORS), BF16)
    mix_z = z_blocks(low[:, 4 * width : 5 * width])
    time_z = z_blocks(jnp.concatenate([low[:, : 3 * width], vectors.astype(BF16).T, spare], 1))
    mix_y = y_blocks(mix_z)
    time_z, mix_y, (space_col, space_row, _) = together(time_z, mix_y, [*space_ids, tokens_sorted])
    mix_map = assemble("gather_mix", mix_z, mix_y)
    mix_x = x_swap(mix_map)
    time_y = y_blocks(time_z, True)
    out_z = z_blocks(after(low[:, 3 * width : 4 * width], *time_z))
    time_y, out_z, (mix_map, mix_x) = together(time_y, out_z, [mix_map, mix_x])
    time_maps = assemble("gather_time", time_z, time_y)
    mix_core = core_swap(jnp.concatenate([mix_map, mix_x], 1))
    out_y = y_blocks(out_z)
    space_z = z_blocks(after(low[:, 5 * width : 9 * width], *out_z))

    vec, first, time_inputs, time_own, time_send, time_logs = local_call(
        "time_forward",
        time_forward_kernel,
        [
            shaped((16, features), F32),
            shaped((count, features), BF16),
            shaped((count, 3 * width), BF16),
            wide(width, BF16),
            wide(width, BF16),
            shaped((8, count), F32),
        ],
        time_maps, tokens_sorted, back, time_col, time_row,
        scratch=[pltpu.VMEM((count, width), BF16)],
    )
    out_y, space_z, (mix_core, time_send) = together(out_y, space_z, [mix_core, time_send])
    time_got = core_swap(time_send)
    out_map = assemble("gather_out", out_z, out_y)

    mix_blocks, fused, mix_bias = local_call(
        "mix_maps",
        mix_kernel,
        [
            shaped((group_count, features, width), BF16),
            shaped((features, width), BF16),
            shaped((1, features), F32),
        ],
        place, out_map, mix_map, mix_x, mix_core, vec,
        smem=(0,),
    )
    fused_far = core_swap(fused)
    space_y = y_blocks(space_z)
    up_z = z_blocks(after(low[:, 9 * width : 9 * width + hidden], *space_z))
    (time_part,) = local_call("time_out", time_out_kernel, [wide(features, BF16)], time_own, time_got, fused, fused_far)
    stream_one, second = local_call(
        "space_norm",
        partial(norm_in_kernel, 4),
        [wide(features, F32), wide(features, BF16)],
        tokens_own, time_part, x_swap(time_part), mix_bias, vec,
        flops=LONG,
    )

    space_own = assemble("gather_space", space_z, space_y)
    space_far = core_swap(space_own)
    space_q, space_pairs = local_call(
        "space_in",
        space_in_kernel,
        [wide(2 * width, BF16), wide(4 * width, BF16)],
        second, space_own, space_far,
    )
    up_z, (space_q, space_pairs) = together(up_z, [space_q, space_pairs])
    up_y = y_blocks(up_z)
    down_z = z_blocks(after(low[:, 9 * width + hidden :], *up_z))
    space_got = core_swap(space_pairs)
    space_heads, space_logs, class_logs, space_part = local_call(
        "space_forward",
        space_forward_kernel,
        [wide(2 * width, BF16), shaped((8, rows), F32), shaped((8, CLASSES), F32), wide(features, BF16)],
        place, space_q, space_pairs, space_got, space_col, space_row, space_own, space_far,
        smem=(0,),
        scratch=[pltpu.VMEM((count, 4 * width), BF16), pltpu.VMEM((CLASSES, 4 * width), BF16)],
    )
    up_y, down_z, (space_part,) = together(up_y, down_z, [space_part])
    stream_two, third = local_call(
        "feed_norm",
        partial(norm_in_kernel, 7),
        [wide(features, F32), wide(features, BF16)],
        stream_one, space_part, x_swap(space_part), vec[6:8], vec,
        flops=LONG,
    )

    up_own = assemble("gather_up", up_z, up_y)
    up_far = core_swap(up_own)
    down_own = assemble("gather_down", down_z, y_blocks(down_z))
    down_far = core_swap(down_own)
    activ, grad_pre, third_part = local_call(
        "feed",
        feed_kernel,
        [wide(2 * hidden, BF16), wide(2 * hidden, BF16), wide(features, BF16)],
        third, dy, up_own, up_far, down_own, down_far,
    )
    third_part_got = x_swap(third_part)
    outer = [shaped((features, hidden), BF16)] * 2
    up_grad, up_grad_far = local_call("up_grads", outer_kernel, outer, third, grad_pre)
    down_grad, down_grad_far = local_call("down_grads", outer_kernel, outer, dy, activ)
    (feed_part,) = local_call("feed_out", feed_out_kernel, [wide(features, BF16)], activ, down_own, down_far)
    up_sends, up_keep = split_rows("split_up", [(up_grad, core_swap(up_grad_far))])
    down_sends, down_keep = split_rows("split_down", [(down_grad, core_swap(down_grad_far))])

    grad_two, grad_two_low, sums_two, space_grad_heads = local_call(
        "space_back_in",
        space_back_in_kernel,
        [wide(features, F32), wide(features, BF16), shaped((8, features), F32), wide(2 * width, BF16)],
        third_part, third_part_got, stream_two, vec, dy, space_own, space_far,
        flops=LONG,
    )
    up_sends, down_sends, (space_grad_heads, feed_part) = together(
        up_sends, down_sends, [space_grad_heads, feed_part]
    )
    up_y = [dp_swap(one, 1) for one in up_sends]
    space_dq, space_keep, space_send = local_call(
        "space_backward",
        space_backward_kernel,
        [wide(2 * width, BF16), wide(4 * width, F32), wide(4 * width, BF16)],
        place, space_grad_heads, space_q, space_pairs, space_got, space_logs, class_logs, space_col, space_row,
        smem=(0,),
        scratch=[
            pltpu.VMEM((count, 4 * width), BF16),
            pltpu.VMEM((CLASSES, 4 * width), BF16),
            pltpu.VMEM((count, 4 * width), F32),
            pltpu.VMEM((CLASSES, 4 * width), F32),
            pltpu.VMEM((CLASSES, 2 * width), BF16),
        ],
    )
    up_y, (space_send,) = together(up_y, [space_send])
    space_got_grads = core_swap(space_send)
    up_sums = y_sums(up_keep, up_y)
    up_shards = z_swaps(up_sums)
    down_y = [dp_swap(after(one, *up_y), 1) for one in down_sends]
    grad_space, grad_space_far, second_part = local_call(
        "space_back",
        space_back_kernel,
        [wide(3 * width, BF16), wide(3 * width, BF16), wide(features, BF16)],
        space_dq, space_keep, space_got_grads, space_own, space_far,
    )
    second_part_got = x_swap(second_part)
    space_grad, space_grad_far = local_call(
        "space_grads",
        space_grads_kernel,
        [shaped((features, 4 * width), BF16)] * 2,
        second, grad_space, grad_space_far, grad_two_low, space_heads,
    )
    space_sends, space_own_rows = split_rows("split_space", [(space_grad, core_swap(space_grad_far))])

    grad_one, grad_one_low, sums_one, time_grad_own, time_grad_send = local_call(
        "time_back_in",
        time_back_in_kernel,
        [
            wide(features, F32),
            wide(features, BF16),
            shaped((8, features), F32),
            wide(width, BF16),
            wide(width, BF16),
        ],
        second_part, second_part_got, stream_one, vec, grad_two, fused, fused_far,
    )
    down_y, up_shards, space_sends, (time_grad_own, time_grad_send, grad_one_low) = together(
        down_y, up_shards, space_sends, [time_grad_own, time_grad_send, grad_one_low]
    )
    down_sums = y_sums(down_keep, down_y)
    down_shards = z_swaps(down_sums)
    space_y = [dp_swap(one, 1) for one in space_sends]
    time_grad_got = core_swap(time_grad_send)
    fused_grad, fused_grad_far = local_call(
        "fused_grads",
        fused_grads_kernel,
        [shaped((features, width), F32), shaped((features, width), BF16)],
        grad_one_low, time_own, time_got,
    )
    fused_grad_got = core_swap(fused_grad_far)
    grad_time_out, fused_total, bias_grad = local_call(
        "mix_grads",
        mix_grads_kernel,
        [shaped((features, width), BF16), shaped((features, width), BF16), shaped((8, features), F32)],
        place, fused_grad, fused_grad_got, mix_blocks, sums_one,
        smem=(0,),
    )
    out_sends, out_keep = split_rows("split_out", [(grad_time_out, None), (fused_total, None)])
    out_sends, (time_grad_own, time_grad_got) = together(out_sends, [time_grad_own, time_grad_got])
    out_y = [dp_swap(one, 1) for one in out_sends]
    (grad_time,) = local_call(
        "time_backward",
        time_backward_kernel,
        [shaped((count, 3 * width), BF16)],
        time_grad_own, time_grad_got, order, time_inputs, time_logs, time_col, time_row,
        scratch=[pltpu.VMEM((count, width), BF16), pltpu.VMEM((count, 2 * width), F32)],
    )
    down_shards, space_y, out_y, (grad_time,) = together(down_shards, space_y, out_y, [grad_time])
    *time_sends, time_keep = local_call(
        "time_grads",
        time_grads_kernel,
        [shaped((shard, 3 * width), BF16)] * half + [shaped((half, shard, 3 * width), F32)],
        place, first, grad_time,
        smem=(0,),
        scratch=[pltpu.VMEM((features, 3 * width), F32)],
    )
    time_sends, (grad_time,) = together(time_sends, [grad_time])
    time_y = [dp_swap(one, 1) for one in time_sends]
    space_sums, out_sums = y_sums(space_own_rows, space_y), y_sums(out_keep, out_y)
    space_shards, out_shards = z_swaps(space_sums), z_swaps(out_sums)
    first_own, first_send, vector_sum = local_call(
        "time_back",
        time_back_kernel,
        [wide(features, BF16), wide(features, BF16), shaped((16, features), F32)],
        grad_time, time_maps, tokens_sorted, back, bias_grad, sums_one, sums_two,
        scratch=[pltpu.VMEM((count, features), BF16)],
    )
    time_y, (first_send, vector_sum) = together(time_y, [first_send, vector_sum])
    time_sums = y_sums(time_keep, time_y)
    time_shards = z_swaps(time_sums)
    first_part = (first_own.astype(F32) + core_swap(first_send).astype(F32)).astype(BF16)
    first_part_got = x_swap(first_part)
    feed_part_got = x_swap(after(feed_part, first_part_got))

    out_width = 2 * width
    out_total = sum([one.astype(F32) for one in out_shards], out_sums[0])
    mix_keep, mix_send = local_call(
        "mix_shard",
        mix_shard_kernel,
        [shaped((shard, out_width), F32), shaped((shard, out_width), BF16)],
        place, out_total[:, width:], out_map,
        smem=(0,),
    )
    mix_sum = mix_keep + core_swap(mix_send).astype(F32)
    mix_total = mix_sum[:, :width] + x_swap(mix_sum[:, width:].astype(BF16)).astype(F32)

    dp_count = lax.axis_size("dp")

    def dp_sum(value):
        step = 1
        while step < dp_count:
            value = value + dp_swap(value, step)
            step *= 2
        return value

    def heads_sum(value):
        value = value + core_swap(value)
        return value + x_swap(value)

    vector_whole = dp_sum(heads_sum(vector_sum))
    vector_all = vector_whole[:VECTORS]
    vector_part = lax.dynamic_slice_in_dim(vector_whole, lax.axis_index("dp") * shard, shard, 1)
    vector_grad, low_sum = vector_part[:VECTORS], vector_part[10]
    bias_part = lax.dynamic_slice_in_dim(vec[2], lax.axis_index("heads") * width, width, 0)
    mix_total = mix_total + low_sum[:, None] * bias_part[None, :]
    pieces = [
        [time_sums[0], *time_shards],
        [out_total[:, :width]],
        [mix_total],
        [space_sums[0], *space_shards],
        [up_sums[0], *up_shards],
        [down_sums[0], *down_shards],
    ]
    weight_grad, square = local_call(
        "whole_grad",
        partial(whole_grad_kernel, [len(one) for one in pieces]),
        [shaped(weights.shape, F32), shaped((8, 128), F32)],
        *[one for piece in pieces for one in piece],
    )
    square = dp_sum(heads_sum(square))[0, 0]
    grad_norm = jnp.sqrt(square + jnp.sum(vector_all * vector_all))
    limit = 0.5 * math.sqrt(NPARAM)
    factor = limit / jnp.maximum(grad_norm, limit)
    weights_out = adam_update(
        weights, weights_m, weights_v, weights_ema, weight_grad, factor, MATRIX_RATE, MATRIX_DECAY
    )
    vectors_out = adam_update(vectors, vectors_m, vectors_v, vectors_ema, vector_grad, factor, VECTOR_RATE, 0.0)

    def whole(name, value):
        (out,) = local_call(
            name, whole_rows_kernel, [shaped((count, features), F32)], place, value, core_swap(value), smem=(0,)
        )
        return out

    (layer_rows,) = local_call(
        "layer_out", layer_out_kernel, [wide(features, F32)], stream_two, feed_part, feed_part_got, vec
    )
    (grad_rows,) = local_call(
        "input_grad", input_grad_kernel, [wide(features, F32)], first_part, first_part_got, tokens_own, vec, grad_one
    )
    return (
        whole("layer_rows", layer_rows),
        whole("grad_rows", grad_rows),
        weight_grad,
        vector_grad,
        grad_norm,
        *weights_out,
        *vectors_out,
    )


def solution(mesh):
    rows, square, line = P("dp", None), P("dp", "heads"), P(None, "dp")
    placed = (rows,) * 5 + (square,) * 4 + (line,) * 4
    return jax.shard_map(
        local,
        mesh=mesh,
        in_specs=placed,
        out_specs=(rows, rows, square, line, P()) + (square,) * 4 + (line,) * 4,
        check_vma=False,
    )
```

profile of v0, /device:TPU:0, one launch (start us, length us, event | category | flops | bytes accessed | tf_op | source)
XLA Modules:
  0.0 354.4 jit_solution(16709344897601586771)
XLA Ops:
  3.2 5.1 %collective-permute-start.2 = (bf16[96,640]{1,0:T(8,128)(2,1)S(1)}, bf16[96,640]{1,0:T(8,128)(2,1)}, u32[]{:S(2)}, u32[]{:S(2)}) collective-permute-start(bf16[96,640]{1,0:T(8,128)(2,1)S(1)} %maximum_maximum_fusion.refs_0_), channel_id=1, source_target_pairs={{0,24},{4,28},{8,16},{12,20},{16,8},{20,12},{24,0},{28,4},{1,25},{... | collective-permute-start | bytes 368648 | tf_op jit(solution)/shard_map/ppermute | solution.py:49
  16.3 6.7 %collective-permute-start = (bf16[96,640]{1,0:T(8,128)(2,1)S(1)}, bf16[96,640]{1,0:T(8,128)(2,1)}, u32[]{:S(2)}, u32[]{:S(2)}) collective-permute-start(bf16[96,640]{1,0:T(8,128)(2,1)S(1)} %maximum_maximum_fusion.refs_0_), channel_id=1, source_target_pairs={{0,8},{4,12},{8,0},{12,4},{16,24},{20,28},{24,16},{28,20},{1,9},{5... | collective-permute-start | bytes 368648 | tf_op jit(solution)/shard_map/ppermute | solution.py:49
  28.3 4.5 %sort_rows.1 = (bf16[1024,768]{1,0:T(8,128)(2,1)S(1)}, bf16[1024,1024]{1,0:T(8,128)(2,1)S(1)}, bf16[1024,1024]{1,0:T(8,128)(2,1)S(1)}, f32[1024,8]{1,0:T(8,128)S(1)}, f32[8,1024]{1,0:T(8,128)S(1)}) custom-call(s32[1024,8]{1,0:T(8,128)S(1)} %copy.45.col_ref, s32[8,1024]{1,0:T(8,128)S(1)} %stack.99.row_ref, bf16[1024,768]{1,0:T(8,128)(2,1)S(1)} %copy-done.9), custom_call_target="tpu_custom_call" | custom-call | tf_op jit(solution)/shard_map/sort_rows/pallas_call | solution.py:71
  36.5 2.5 collective-permute-start.13
  53.1 2.5 collective-permute-start.18
  59.2 10.1 %time_forward.1 = (f32[16,768]{1,0:T(8,128)S(1)}, bf16[1024,768]{1,0:T(8,128)(2,1)S(1)}, bf16[1024,576]{1,0:T(8,128)(2,1)S(1)}, bf16[512,192]{1,0:T(8,128)(2,1)S...) custom-call(bf16[768,640]{1,0:T(8,128)(2,1)S(1)} %bitcast.117, ...), custom_call_target="tpu_custom_call" | custom-call | tf_op jit(solution)/shard_map/time_forward/pallas_call | solution.py:71
  79.2 2.5 collective-permute-start.25
  83.6 9.2 %collective-permute-done.26.refs_4_ = bf16[4,96,768]{2,1,0:T(8,128)(2,1)S(1)} collective-permute-done((bf16[4,96,768]{2,1,0:T(8,128)(2,1)S(1)}, bf16[4,96,768]{2,1,0:T(8,128)(2,1)S(1)}, u32[]{:S(2)}, u32[]{:S(2)}) %collective-permute-start.26) | collective-permute-done | bytes 589856 | tf_op jit(solution)/shard_map/ppermute | solution.py:49
  93.5 3.1 collective-permute-done.22.got_ref
  98.5 2.6 space_in.1
  104.4 2.5 collective-permute-start.31
  114.7 11.7 %space_forward.1 = (bf16[512,384]{1,0:T(8,128)(2,1)S(1)}, f32[8,512]{1,0:T(8,128)S(1)}, f32[8,8]{1,0:T(8,128)S(1)}, bf16[512,768]{1,0:T(8,128)(2,1)S(1)}) custom-call(s32[4]{0:T(128)S(1)} %pad_add_fusion.3.place_ref, bf16[512,384]{1,0:T(8,128)(2,1)S(1)} %copy-done.23, bf16[512,768]{1,0:T(8,128)(2,1)} %get-tuple-element.206.pairs_ref, ...), custom_call_target="tpu_custom_call" | custom-call | tf_op jit(solution)/shard_map/space_forward/pallas_call | solution.py:71
  130.3 12.4 %collective-permute-done.35.refs_4_ = bf16[4,96,768]{2,1,0:T(8,128)(2,1)S(1)} collective-permute-done((bf16[4,96,768]{2,1,0:T(8,128)(2,1)S(1)}, bf16[4,96,768]{2,1,0:T(8,128)(2,1)S(1)}, u32[]{:S(2)}, u32[]{:S(2)}) %collective-permute-start.35) | collective-permute-done | bytes 589856 | tf_op jit(solution)/shard_map/ppermute | solution.py:49
  146.9 5.0 %feed.1 = (bf16[512,1536]{1,0:T(8,128)(2,1)S(1)}, bf16[512,1536]{1,0:T(8,128)(2,1)S(1)}, bf16[512,768]{1,0:T(8,128)(2,1)S(1)}) custom-call(bf16[512,768]{1,0:T(8,128)(2,1)S(1)} %get-tuple-element.212.third_ref.left_ref, bf16[512,768]{1,0:T(8,128)(2,1)S(1)} %constant_dynamic-slice_fusion.2.dy_ref.left_ref, bf16[768,768]{1,0:T(8,128)(2,1)S(1)} %bitcast.120, ...), custom_call_target="tpu_custom_call" | custom-call | tf_op jit(solution)/shard_map/feed/pallas_call | solution.py:71
  157.0 2.5 feed_out.1.part_ref
  159.5 12.1 %collective-permute-done.39.got_ref = bf16[512,768]{1,0:T(8,128)(2,1)S(1)} collective-permute-done((bf16[512,768]{1,0:T(8,128)(2,1)S(1)}, bf16[512,768]{1,0:T(8,128)(2,1)S(1)}, u32[]{:S(2)}, u32[]{:S(2)}) %collective-permute-start.39) | collective-permute-done | bytes 786464 | tf_op jit(solution)/shard_map/ppermute | solution.py:44
  171.6 2.7 space_back_in.1
  176.5 16.3 %space_backward.1 = (bf16[512,384]{1,0:T(8,128)(2,1)S(1)}, f32[512,768]{1,0:T(8,128)S(1)}, bf16[512,768]{1,0:T(8,128)(2,1)S(1)}) custom-call(s32[4]{0:T(128)S(1)} %pad_add_fusion.3.place_ref, bf16[512,384]{1,0:T(8,128)(2,1)S(1)} %get-tuple-element.233.heads_ref, bf16[512,384]{1,0:T(8,128)(2,1)S(1)} %copy-done.24, ...), custom_call_target="tpu_custom_call" | custom-call | tf_op jit(solution)/shard_map/space_backward/pallas_call | solution.py:71
  202.6 2.5 collective-permute-start.44
  205.2 14.1 %collective-permute-done.47.got_ref = bf16[512,768]{1,0:T(8,128)(2,1)S(1)} collective-permute-done((bf16[512,768]{1,0:T(8,128)(2,1)S(1)}, bf16[512,768]{1,0:T(8,128)(2,1)S(1)}, u32[]{:S(2)}, u32[]{:S(2)}) %collective-permute-start.47) | collective-permute-done | bytes 786464 | tf_op jit(solution)/shard_map/ppermute | solution.py:44
  230.9 2.5 collective-permute-start.50
  235.4 10.2 %time_backward.1.grad_ref = bf16[1024,576]{1,0:T(8,128)(2,1)S(1)} custom-call(bf16[512,192]{1,0:T(8,128)(2,1)S(1)} %get-tuple-element.268.own_ref, bf16[512,192]{1,0:T(8,128)(2,1)S(1)} %collective-permute-done.53.far_ref, bf16[1024,1024]{1,0:T(8,128)(2,1)S(1)} %copy-done.21, bf16[1024,576]{1,0:T(8,128)(2,1)S(1)} %copy-done.42, f32[8,1024]{1,0:T(8,128)S(1)} %copy-done.81, ...), custom_call_target="tpu_custom_call" | custom-call | tf_op jit(solution)/shard_map/time_backward/pallas_call | solution.py:71
  253.8 4.4 %time_back.1 = (bf16[512,768]{1,0:T(8,128)(2,1)S(1)}, bf16[512,768]{1,0:T(8,128)(2,1)S(1)}, f32[16,768]{1,0:T(8,128)}) custom-call(bf16[1024,576]{1,0:T(8,128)(2,1)S(1)} %time_backward.1.grad_ref, bf16[768,640]{1,0:T(8,128)(2,1)S(1)} %bitcast.118, bf16[1024,768]{1,0:T(8,128)(2,1)S(1)} %copy-done.11, bf16[1024,1024]{1,0:T(8,128)(2,1)S(1)} %copy-done.8, ...), custom_call_target="tpu_custom_call" | custom-call | tf_op jit(solution)/shard_map/time_back/pallas_call | solution.py:71
  271.4 2.5 collective-permute-start.69
  280.1 7.1 %collective-permute-done.68 = bf16[96,384]{1,0:T(8,128)(2,1)S(1)} collective-permute-done((bf16[96,384]{1,0:T(8,128)(2,1)S(1)}, bf16[96,384]{1,0:T(8,128)(2,1)S(1)}, u32[]{:S(2)}, u32[]{:S(2)}) %collective-permute-start.68) | collective-permute-done | bytes 73760 | tf_op jit(solution)/shard_map/ppermute | solution.py:49
  299.2 3.4 collective-permute-done.76
  304.2 3.5 collective-permute-start.66
  307.6 5.2 %collective-permute-done.71 = bf16[96,192]{1,0:T(8,128)(2,1)S(1)} collective-permute-done((bf16[96,192]{1,0:T(8,128)(2,1)S(1)}, bf16[96,192]{1,0:T(8,128)(2,1)S(1)}, u32[]{:S(2)}, u32[]{:S(2)}) %collective-permute-start.71) | collective-permute-done | bytes 36896 | tf_op jit(solution)/shard_map/ppermute | solution.py:44
  314.9 2.9 collective-permute-done.64.refs_1_
  340.2 5.9 %add_multiply_fusion = (f32[96,3264]{1,0:T(8,128)}, f32[96,3264]{1,0:T(8,128)}, f32[96,3264]{1,0:T(8,128)}, f32[96,3264]{1,0:T(8,128)}) fusion(f32[96,3264]{1,0:T(8,128)} %param.21, f32[96,3264]{1,0:T(8,128)} %param.18, f32[96,3264]{1,0:T(8,128)} %get-tuple-element.151, f32[]{:T(128)S(6)} %div.42, f32[96,3264]{1,0:T(8,128)} %param.19, f32[96,3264]{1,0:T(8,128)} %param.20), kind=kLoop, calls=%fused_computation.5 | loop fusion | flops 5326848 | bytes 11280388 | tf_op jit(solution)/shard_map/add | solution.py:831
  346.1 3.3 grad_rows.1
  349.4 3.4 layer_rows.1
  (441 shorter events, 164.4 us)
Async XLA Ops:
  3.2 31.1 %collective-permute-start.2 = (bf16[96,640]{1,0:T(8,128)(2,1)S(1)}, bf16[96,640]{1,0:T(8,128)(2,1)}, u32[]{:S(2)}, u32[]{:S(2)}) collective-permute-start(bf16[96,640]{1,0:T(8,128)(2,1)S(1)} %maximum_maximum_fusion.refs_0_), channel_id=1, source_target_pairs={{0,24},{4,28},{8,16},{12,20},{16,8},{20,12},{24,0},{28,4},{1,25},{... | collective-permute-start | bytes 368648 | tf_op jit(solution)/shard_map/ppermute | solution.py:49
  8.3 26.0 %collective-permute-start.1 = (bf16[96,640]{1,0:T(8,128)(2,1)S(1)}, bf16[96,640]{1,0:T(8,128)(2,1)}, u32[]{:S(2)}, u32[]{:S(2)}) collective-permute-start(bf16[96,640]{1,0:T(8,128)(2,1)S(1)} %maximum_maximum_fusion.refs_0_), channel_id=1, source_target_pairs={{0,16},{4,20},{8,24},{12,28},{16,0},{20,4},{24,8},{28,12},{1,17},{... | collective-permute-start | bytes 368648 | tf_op jit(solution)/shard_map/ppermute | solution.py:49
  16.3 18.1 %collective-permute-start = (bf16[96,640]{1,0:T(8,128)(2,1)S(1)}, bf16[96,640]{1,0:T(8,128)(2,1)}, u32[]{:S(2)}, u32[]{:S(2)}) collective-permute-start(bf16[96,640]{1,0:T(8,128)(2,1)S(1)} %maximum_maximum_fusion.refs_0_), channel_id=1, source_target_pairs={{0,8},{4,12},{8,0},{12,4},{16,24},{20,28},{24,16},{28,20},{1,9},{5... | collective-permute-start | bytes 368648 | tf_op jit(solution)/shard_map/ppermute | solution.py:49
  34.9 17.0 %collective-permute-start.14 = (bf16[768,192]{1,0:T(8,128)(2,1)S(1)}, bf16[768,192]{1,0:T(8,128)(2,1)S(1)}, u32[]{:S(2)}, u32[]{:S(2)}) collective-permute-start(bf16[768,192]{1,0:T(8,128)(2,1)S(1)} %bitcast.123), channel_id=1, source_target_pairs={{0,2},{1,3},{2,0},{3,1},{4,6},{5,7},{6,4},{7,5},{8,10},{9,11},{10,... | collective-permute-start | bytes 884744 | tf_op jit(solution)/shard_map/ppermute | solution.py:44
  52.1 18.4 %collective-permute-start.19 = (bf16[768,384]{1,0:T(8,128)(2,1)S(1)}, bf16[768,384]{1,0:T(8,128)(2,1)S(1)}, u32[]{:S(2)}, u32[]{:S(2)}) collective-permute-start(bf16[768,384]{1,0:T(8,128)(2,1)S(1)} %pad_maximum_fusion.1), channel_id=1, source_target_pairs={{0,1},{1,0},{2,3},{3,2},{4,5},{5,4},{6,7},{7,6},{8,9},{9,8},{10,11... | collective-permute-start | bytes 1769480 | tf_op jit(solution)/shard_map/ppermute | solution.py:40
  53.1 17.4 %collective-permute-start.18 = (bf16[96,768]{1,0:T(8,128)(2,1)S(1)}, bf16[96,768]{1,0:T(8,128)(2,1)S(1)}, u32[]{:S(2)}, u32[]{:S(2)}) collective-permute-start(bf16[96,768]{1,0:T(8,128)(2,1)S(1)} %get-tuple-element.192.refs_0_), channel_id=1, source_target_pairs={{0,24},{4,28},{8,16},{12,20},{16,8},{20,12},{24,0},{28,4},{1,25},{... | collective-permute-start | bytes 442376 | tf_op jit(solution)/shard_map/ppermute | solution.py:49
  77.0 19.6 %collective-permute-start.22 = (bf16[512,768]{1,0:T(8,128)(2,1)S(1)}, bf16[512,768]{1,0:T(8,128)(2,1)S(1)}, u32[]{:S(2)}, u32[]{:S(2)}) collective-permute-start(bf16[512,768]{1,0:T(8,128)(2,1)S(1)} %time_out.1.part_ref), channel_id=1, source_target_pairs={{0,2},{1,3},{2,0},{3,1},{4,6},{5,7},{6,4},{7,5},{8,10},{9,11},{10,... | collective-permute-start | bytes 2359304 | tf_op jit(solution)/shard_map/ppermute | solution.py:44
  79.2 22.7 %collective-permute-start.25 = (bf16[96,768]{1,0:T(8,128)(2,1)S(1)}, bf16[96,768]{1,0:T(8,128)(2,1)S(1)}, u32[]{:S(2)}, u32[]{:S(2)}) collective-permute-start(bf16[96,768]{1,0:T(8,128)(2,1)S(1)} %get-tuple-element.200.refs_0_), channel_id=1, source_target_pairs={{0,24},{4,28},{8,16},{12,20},{16,8},{20,12},{24,0},{28,4},{1,25},{... | collective-permute-start | bytes 442376 | tf_op jit(solution)/shard_map/ppermute | solution.py:49
  81.7 20.2 %collective-permute-start.24 = (bf16[96,768]{1,0:T(8,128)(2,1)S(1)}, bf16[96,768]{1,0:T(8,128)(2,1)S(1)}, u32[]{:S(2)}, u32[]{:S(2)}) collective-permute-start(bf16[96,768]{1,0:T(8,128)(2,1)S(1)} %get-tuple-element.200.refs_0_), channel_id=1, source_target_pairs={{0,16},{4,20},{8,24},{12,28},{16,0},{20,4},{24,8},{28,12},{1,17},{... | collective-permute-start | bytes 442376 | tf_op jit(solution)/shard_map/ppermute | solution.py:49
  81.7 20.2 %collective-permute-start.23 = (bf16[96,768]{1,0:T(8,128)(2,1)S(1)}, bf16[96,768]{1,0:T(8,128)(2,1)S(1)}, u32[]{:S(2)}, u32[]{:S(2)}) collective-permute-start(bf16[96,768]{1,0:T(8,128)(2,1)S(1)} %get-tuple-element.200.refs_0_), channel_id=1, source_target_pairs={{0,8},{4,12},{8,0},{12,4},{16,24},{20,28},{24,16},{28,20},{1,9},{5... | collective-permute-start | bytes 442376 | tf_op jit(solution)/shard_map/ppermute | solution.py:49
  102.9 23.5 %collective-permute-start.28 = (bf16[4,96,768]{2,1,0:T(8,128)(2,1)}, bf16[4,96,768]{2,1,0:T(8,128)(2,1)}, u32[]{:S(2)}, u32[]{:S(2)}) collective-permute-start(bf16[4,96,768]{2,1,0:T(8,128)(2,1)} %pad_maximum_fusion.3), channel_id=1, source_target_pairs={{0,4},{4,0},{8,12},{12,8},{16,20},{20,16},{24,28},{28,24},{1,5},{5... | collective-permute-start | bytes 1769480 | tf_op jit(solution)/shard_map/ppermute | solution.py:49
  104.4 22.0 %collective-permute-start.31 = (bf16[96,768]{1,0:T(8,128)(2,1)}, bf16[96,768]{1,0:T(8,128)(2,1)}, u32[]{:S(2)}, u32[]{:S(2)}) collective-permute-start(bf16[96,768]{1,0:T(8,128)(2,1)} %get-tuple-element.214.refs_0_), channel_id=1, source_target_pairs={{0,24},{4,28},{8,16},{12,20},{16,8},{20,12},{24,0},{28,4},{1,25},{... | collective-permute-start | bytes 442376 | tf_op jit(solution)/shard_map/ppermute | solution.py:49
  106.9 19.5 %collective-permute-start.30 = (bf16[96,768]{1,0:T(8,128)(2,1)}, bf16[96,768]{1,0:T(8,128)(2,1)}, u32[]{:S(2)}, u32[]{:S(2)}) collective-permute-start(bf16[96,768]{1,0:T(8,128)(2,1)} %get-tuple-element.214.refs_0_), channel_id=1, source_target_pairs={{0,16},{4,20},{8,24},{12,28},{16,0},{20,4},{24,8},{28,12},{1,17},{... | collective-permute-start | bytes 442376 | tf_op jit(solution)/shard_map/ppermute | solution.py:49
  106.9 19.5 %collective-permute-start.29 = (bf16[96,768]{1,0:T(8,128)(2,1)}, bf16[96,768]{1,0:T(8,128)(2,1)}, u32[]{:S(2)}, u32[]{:S(2)}) collective-permute-start(bf16[96,768]{1,0:T(8,128)(2,1)} %get-tuple-element.214.refs_0_), channel_id=1, source_target_pairs={{0,8},{4,12},{8,0},{12,4},{16,24},{20,28},{24,16},{28,20},{1,9},{5... | collective-permute-start | bytes 442376 | tf_op jit(solution)/shard_map/ppermute | solution.py:49
  126.5 18.9 %collective-permute-start.33 = (bf16[512,768]{1,0:T(8,128)(2,1)S(1)}, bf16[512,768]{1,0:T(8,128)(2,1)S(1)}, u32[]{:S(2)}, u32[]{:S(2)}) collective-permute-start(bf16[512,768]{1,0:T(8,128)(2,1)S(1)} %get-tuple-element.210.part_ref), channel_id=1, source_target_pairs={{0,2},{1,3},{2,0},{3,1},{4,6},{5,7},{6,4},{7,5},{8,10},{9,11},{10,... | collective-permute-start | bytes 2359304 | tf_op jit(solution)/shard_map/ppermute | solution.py:44
  130.2 15.9 %collective-permute-start.34 = (bf16[768,768]{1,0:T(8,128)(2,1)S(1)}, bf16[768,768]{1,0:T(8,128)(2,1)S(1)}, u32[]{:S(2)}, u32[]{:S(2)}) collective-permute-start(bf16[768,768]{1,0:T(8,128)(2,1)S(1)} %bitcast.119), channel_id=1, source_target_pairs={{0,1},{1,0},{2,3},{3,2},{4,5},{5,4},{6,7},{7,6},{8,9},{9,8},{10,11... | collective-permute-start | bytes 3538952 | tf_op jit(solution)/shard_map/ppermute | solution.py:40
  151.9 19.6 %collective-permute-start.39 = (bf16[512,768]{1,0:T(8,128)(2,1)S(1)}, bf16[512,768]{1,0:T(8,128)(2,1)S(1)}, u32[]{:S(2)}, u32[]{:S(2)}) collective-permute-start(bf16[512,768]{1,0:T(8,128)(2,1)S(1)} %get-tuple-element.226.part_ref), channel_id=1, source_target_pairs={{0,2},{1,3},{2,0},{3,1},{4,6},{5,7},{6,4},{7,5},{8,10},{9,11},{10,... | collective-permute-start | bytes 2359304 | tf_op jit(solution)/shard_map/ppermute | solution.py:44
  154.9 19.4 %collective-permute-start.37 = (bf16[768,768]{1,0:T(8,128)(2,1)S(1)}, bf16[768,768]{1,0:T(8,128)(2,1)S(1)}, u32[]{:S(2)}, u32[]{:S(2)}) collective-permute-start(bf16[768,768]{1,0:T(8,128)(2,1)S(1)} %get-tuple-element.220), channel_id=1, source_target_pairs={{0,1},{1,0},{2,3},{3,2},{4,5},{5,4},{6,7},{7,6},{8,9},{9,8},{10,11... | collective-permute-start | bytes 3538952 | tf_op jit(solution)/shard_map/ppermute | solution.py:40
  156.4 18.8 %collective-permute-start.38 = (bf16[768,768]{1,0:T(8,128)(2,1)S(1)}, bf16[768,768]{1,0:T(8,128)(2,1)S(1)}, u32[]{:S(2)}, u32[]{:S(2)}) collective-permute-start(bf16[768,768]{1,0:T(8,128)(2,1)S(1)} %get-tuple-element.224), channel_id=1, source_target_pairs={{0,1},{1,0},{2,3},{3,2},{4,5},{5,4},{6,7},{7,6},{8,9},{9,8},{10,11... | collective-permute-start | bytes 3538952 | tf_op jit(solution)/shard_map/ppermute | solution.py:40
  176.0 16.8 %collective-permute-start.40 = (bf16[4,96,768]{2,1,0:T(8,128)(2,1)S(1)}, bf16[4,96,768]{2,1,0:T(8,128)(2,1)S(1)}, u32[]{:S(2)}, u32[]{:S(2)}) collective-permute-start(bf16[4,96,768]{2,1,0:T(8,128)(2,1)S(1)} %get-tuple-element.232), channel_id=1, source_target_pairs={{0,4},{4,0},{8,12},{12,8},{16,20},{20,16},{24,28},{28,24},{1,5},{5... | collective-permute-start | bytes 1769480 | tf_op jit(solution)/shard_map/ppermute | solution.py:49
  199.3 23.4 %collective-permute-start.46 = (bf16[768,768]{1,0:T(8,128)(2,1)S(1)}, bf16[768,768]{1,0:T(8,128)(2,1)S(1)}, u32[]{:S(2)}, u32[]{:S(2)}) collective-permute-start(bf16[768,768]{1,0:T(8,128)(2,1)S(1)} %get-tuple-element.248), channel_id=1, source_target_pairs={{0,1},{1,0},{2,3},{3,2},{4,5},{5,4},{6,7},{7,6},{8,9},{9,8},{10,11... | collective-permute-start | bytes 3538952 | tf_op jit(solution)/shard_map/ppermute | solution.py:40
  199.5 19.8 %collective-permute-start.47 = (bf16[512,768]{1,0:T(8,128)(2,1)S(1)}, bf16[512,768]{1,0:T(8,128)(2,1)S(1)}, u32[]{:S(2)}, u32[]{:S(2)}) collective-permute-start(bf16[512,768]{1,0:T(8,128)(2,1)S(1)} %get-tuple-element.250.part_ref), channel_id=1, source_target_pairs={{0,2},{1,3},{2,0},{3,1},{4,6},{5,7},{6,4},{7,5},{8,10},{9,11},{10,... | collective-permute-start | bytes 2359304 | tf_op jit(solution)/shard_map/ppermute | solution.py:44
  201.0 23.6 %collective-permute-start.41 = (bf16[4,96,768]{2,1,0:T(8,128)(2,1)S(1)}, bf16[4,96,768]{2,1,0:T(8,128)(2,1)S(1)}, u32[]{:S(2)}, u32[]{:S(2)}) collective-permute-start(bf16[4,96,768]{2,1,0:T(8,128)(2,1)S(1)} %get-tuple-element.238), channel_id=1, source_target_pairs={{0,4},{4,0},{8,12},{12,8},{16,20},{20,16},{24,28},{28,24},{1,5},{5... | collective-permute-start | bytes 1769480 | tf_op jit(solution)/shard_map/ppermute | solution.py:49
  202.6 22.0 %collective-permute-start.44 = (bf16[96,768]{1,0:T(8,128)(2,1)S(1)}, bf16[96,768]{1,0:T(8,128)(2,1)S(1)}, u32[]{:S(2)}, u32[]{:S(2)}) collective-permute-start(bf16[96,768]{1,0:T(8,128)(2,1)S(1)} %get-tuple-element.325), channel_id=1, source_target_pairs={{0,24},{4,28},{8,16},{12,20},{16,8},{20,12},{24,0},{28,4},{1,25},{... | collective-permute-start | bytes 442376 | tf_op jit(solution)/shard_map/ppermute | solution.py:49
  205.2 19.4 %collective-permute-start.43 = (bf16[96,768]{1,0:T(8,128)(2,1)S(1)}, bf16[96,768]{1,0:T(8,128)(2,1)S(1)}, u32[]{:S(2)}, u32[]{:S(2)}) collective-permute-start(bf16[96,768]{1,0:T(8,128)(2,1)S(1)} %get-tuple-element.326), channel_id=1, source_target_pairs={{0,16},{4,20},{8,24},{12,28},{16,0},{20,4},{24,8},{28,12},{1,17},{... | collective-permute-start | bytes 442376 | tf_op jit(solution)/shard_map/ppermute | solution.py:49
  225.9 21.6 %collective-permute-start.51 = (bf16[4,96,768]{2,1,0:T(8,128)(2,1)S(1)}, bf16[4,96,768]{2,1,0:T(8,128)(2,1)S(1)}, u32[]{:S(2)}, u32[]{:S(2)}) collective-permute-start(bf16[4,96,768]{2,1,0:T(8,128)(2,1)S(1)} %get-tuple-element.256), channel_id=1, source_target_pairs={{0,4},{4,0},{8,12},{12,8},{16,20},{20,16},{24,28},{28,24},{1,5},{5... | collective-permute-start | bytes 1769480 | tf_op jit(solution)/shard_map/ppermute | solution.py:49
  229.5 18.0 %collective-permute-start.54 = (bf16[4,96,384]{2,1,0:T(8,128)(2,1)S(1)}, bf16[4,96,384]{2,1,0:T(8,128)(2,1)S(1)}, u32[]{:S(2)}, u32[]{:S(2)}) collective-permute-start(bf16[4,96,384]{2,1,0:T(8,128)(2,1)S(1)} %get-tuple-element.267), channel_id=1, source_target_pairs={{0,4},{4,0},{8,12},{12,8},{16,20},{20,16},{24,28},{28,24},{1,5},{5... | collective-permute-start | bytes 884744 | tf_op jit(solution)/shard_map/ppermute | solution.py:49
  266.9 26.6 %collective-permute-start.60 = (bf16[512,768]{1,0:T(8,128)(2,1)S(1)}, bf16[512,768]{1,0:T(8,128)(2,1)S(1)}, u32[]{:S(2)}, u32[]{:S(2)}) collective-permute-start(bf16[512,768]{1,0:T(8,128)(2,1)S(1)} %add_convert_fusion.part_ref), channel_id=1, source_target_pairs={{0,2},{1,3},{2,0},{3,1},{4,6},{5,7},{6,4},{7,5},{8,10},{9,11},{10,... | collective-permute-start | bytes 2359304 | tf_op jit(solution)/shard_map/ppermute | solution.py:44
  275.3 28.9 %collective-permute-start.79 = (bf16[96,768]{1,0:T(8,128)(2,1)S(1)}, bf16[96,768]{1,0:T(8,128)(2,1)S(1)}, u32[]{:S(2)}, u32[]{:S(2)}) collective-permute-start(bf16[96,768]{1,0:T(8,128)(2,1)S(1)} %get-tuple-element.328), channel_id=1, source_target_pairs={{0,24},{4,28},{8,16},{12,20},{16,8},{20,12},{24,0},{28,4},{1,25},{... | collective-permute-start | bytes 442376 | tf_op jit(solution)/shard_map/ppermute | solution.py:49
  277.9 29.7 %collective-permute-start.78 = (bf16[96,768]{1,0:T(8,128)(2,1)S(1)}, bf16[96,768]{1,0:T(8,128)(2,1)S(1)}, u32[]{:S(2)}, u32[]{:S(2)}) collective-permute-start(bf16[96,768]{1,0:T(8,128)(2,1)S(1)} %get-tuple-element.329), channel_id=1, source_target_pairs={{0,16},{4,20},{8,24},{12,28},{16,0},{20,4},{24,8},{28,12},{1,17},{... | collective-permute-start | bytes 442376 | tf_op jit(solution)/shard_map/ppermute | solution.py:49
  293.4 40.8 %collective-permute-start.61 = (bf16[512,768]{1,0:T(8,128)(2,1)}, bf16[512,768]{1,0:T(8,128)(2,1)S(1)}, u32[]{:S(2)}, u32[]{:S(2)}) collective-permute-start(bf16[512,768]{1,0:T(8,128)(2,1)} %feed_out.1.part_ref), channel_id=1, source_target_pairs={{0,2},{1,3},{2,0},{3,1},{4,6},{5,7},{6,4},{7,5},{8,10},{9,11},{10,... | collective-permute-start | bytes 2359304 | tf_op jit(solution)/shard_map/ppermute | solution.py:44
  296.5 17.5 %collective-permute-start.77 = (bf16[96,768]{1,0:T(8,128)(2,1)S(1)}, bf16[96,768]{1,0:T(8,128)(2,1)S(1)}, u32[]{:S(2)}, u32[]{:S(2)}) collective-permute-start(bf16[96,768]{1,0:T(8,128)(2,1)S(1)} %get-tuple-element.330), channel_id=1, source_target_pairs={{0,8},{4,12},{8,0},{12,4},{16,24},{20,28},{24,16},{28,20},{1,9},{5... | collective-permute-start | bytes 442376 | tf_op jit(solution)/shard_map/ppermute | solution.py:49
  (156 other events, 1433.5 us)
where the time goes:
time: 361 us; the launch traced here: 354 us
  Pallas kernels  107 us (30%)
  waiting for transfers between devices  104 us (29%)
  starting transfers between devices  95.8 us (27%)
  local copies, waits for them, and re-layouts  22.7 us (6%)
  other arithmetic  20.2 us (6%)
  between operations  5.15 us (1%)
    pallas_call x38, Pallas kernels, local_call(): pl.pallas_call(kernel, name=name, out_shape=list(outs), in_specs=[SMEM if...  107 us
    ppermute x56, starting transfers between devices, dp_swap(): return lax.ppermute(value, 'dp', [(i, i ^ mask) for i in range(count)])  80.6 us
    ppermute x56, waiting for transfers between devices, dp_swap(): return lax.ppermute(value, 'dp', [(i, i ^ mask) for i in range(count)])  56.2 us
    ppermute x10, waiting for transfers between devices, x_swap(): return lax.ppermute(value, 'heads', [(i, i ^ 2) for i in range(4)])  38 us
    unnamed x206, local copies, waits for them, and re-layouts  15.2 us
    ppermute x10, starting transfers between devices, x_swap(): return lax.ppermute(value, 'heads', [(i, i ^ 2) for i in range(4)])  12.4 us
    ppermute x19, waiting for transfers between devices, core_swap(): return lax.ppermute(value, 'heads', [(i, i ^ 1) for i in range(4)])  9.37 us
    add x2, other arithmetic, adam_update(): average_new = AVERAGE_RATE * average + (1.0 - AVERAGE_RATE) * master_new  7.38 us
  transfers between devices with their start and end apart: 85, of which 33 were waited for; matrix products, arithmetic and copies ran while one was open for 7% of the time, Pallas kernels for 25%

commit v1 on v0

v1 whole, which is shorter than its diff:
```python
import math
from functools import partial

import jax
import jax.numpy as jnp
from jax import lax
from jax.experimental import pallas as pl
from jax.experimental.pallas import tpu as pltpu
from jax.sharding import PartitionSpec as P

HEAD_DIM = 64
STEP = 5
NPARAM = 10034688
VECTORS = 10

NORM_EPS = 1e-06
BETA_FIRST = 0.5
BETA_SECOND = 0.5
AVERAGE_RATE = 0.5
MATRIX_RATE = 0.03
VECTOR_RATE = 0.3
MATRIX_DECAY = 0.05
ADAM_EPS = 1e-08
MASKED = -1e30
SCALE = HEAD_DIM ** (-0.5)
F32 = jnp.float32
BF16 = jnp.bfloat16

BLOCK = 128
WINDOW = 256
CLASSES = 16
CHUNK = 256
UNROLL = 4
SPARE = 64
LONG = 40_000_000_000

VMEM = pl.BlockSpec(memory_space=pltpu.VMEM)
SMEM = pl.BlockSpec(memory_space=pltpu.SMEM)
ANY = pl.BlockSpec(memory_space=pl.ANY)


def core_swap(value):
    return lax.ppermute(value, "heads", [(i, i ^ 1) for i in range(4)])


def x_swap(value):
    return lax.ppermute(value, "heads", [(i, i ^ 2) for i in range(4)])


def dp_swap(value, mask):
    count = lax.axis_size("dp")
    return lax.ppermute(value, "dp", [(i, i ^ mask) for i in range(count)])


def all_sum(value):
    count = lax.axis_size("dp") * lax.axis_size("heads")
    value = value + core_swap(value)
    step = 2
    while step < count:
        masks = [step, 2 * step, 3 * step] if 2 * step < count else [step]
        got = [lax.ppermute(value, ("dp", "heads"), [(i, i ^ mask) for i in range(count)]) for mask in masks]
        value = value + got[0]
        if len(got) > 1:
            value = value + (got[1] + got[2])
        step *= 4
    return value


def after(value, *others):
    return lax.optimization_barrier((value, *others))[0]


def together(*groups):
    flat = lax.optimization_barrier([one for group in groups for one in group])
    split, at = [], 0
    for group in groups:
        split.append(list(flat[at : at + len(group)]))
        at += len(group)
    return split


def shaped(shape, dtype):
    return jax.ShapeDtypeStruct(shape, dtype)


def local_call(name, kernel, outs, *operands, scratch=(), smem=(), extra=6, flops=0, staged=False):
    spec = VMEM
    if staged:
        spec, inner, count = ANY, kernel, len(operands)
        moved = [i for i in range(count) if i not in smem]

        def kernel(*refs):
            ins, rest, held, sem = list(refs[:count]), refs[count : -1 - len(moved)], refs[-1 - len(moved) : -1], refs[-1]
            copies = [pltpu.make_async_copy(ins[i], ref, sem.at[j]) for j, (i, ref) in enumerate(zip(moved, held))]
            for copy in copies:
                copy.start()
            for copy, i, ref in zip(copies, moved, held):
                copy.wait()
                ins[i] = ref
            inner(*ins, *rest)

        scratch = [*scratch, *[pltpu.VMEM(operands[i].shape, operands[i].dtype) for i in moved]]
    held = sum(math.prod(one.shape) * jnp.dtype(one.dtype).itemsize for one in scratch)
    return pl.pallas_call(
        kernel,
        name=name,
        out_shape=list(outs),
        in_specs=[SMEM if i in smem else spec for i in range(len(operands))],
        out_specs=[VMEM] * len(outs),
        scratch_shapes=[*scratch, *([pltpu.SemaphoreType.DMA((len(moved),))] if staged else [])],
        compiler_params=pltpu.CompilerParams(
            vmem_limit_bytes=held + extra * 2**20
        ),
        cost_estimate=pl.CostEstimate(flops=flops, bytes_accessed=0, transcendentals=0),
    )(*operands)


def dot(left, right):
    return jnp.dot(left, right, preferred_element_type=F32)


def dot_nt(left, right):
    return lax.dot_general(left, right, (((1,), (1,)), ((), ())), preferred_element_type=F32)


def dot_tn(left, right):
    return lax.dot_general(left, right, (((0,), (0,)), ((), ())), preferred_element_type=F32)


def chunk_loop(rows, body, size=CHUNK):
    def step(i, carry):
        body(pl.ds(pl.multiple_of(i * size, size), size))
        return carry

    lax.fori_loop(0, rows // size, step, 0)


def normed(stream):
    center = stream - jnp.mean(stream, -1, keepdims=True)
    factor = lax.rsqrt(jnp.mean(center * center, -1, keepdims=True) + NORM_EPS)
    return center * factor, factor


def norm_grad(hat, factor, gain, grad):
    scaled = grad * gain
    return factor * (
        scaled - jnp.mean(scaled, -1, keepdims=True) - hat * jnp.mean(scaled * hat, -1, keepdims=True)
    )


def column_sum(value):
    return jnp.sum(value, 0, keepdims=True)


def z_blocks(piece):
    return [piece] + [dp_swap(piece, 2 * k) for k in range(1, lax.axis_size("dp") // 2)]


def y_blocks(mine, fine=False):
    return [dp_swap(one, 1) for one in mine] if fine else [dp_swap(jnp.stack(mine), 1)]


def assemble(name, mine, other, cuts=()):
    half, count, fine = len(mine), lax.axis_size("dp"), len(other) > 1
    rows, columns = mine[0].shape
    bounds = [0, *cuts, columns]
    parts = [slice(start, stop) for start, stop in zip(bounds, bounds[1:])]

    def kernel(place_ref, *refs):
        z, y = place_ref[0], place_ref[1]
        for out_ref, part in zip(refs[half + len(other) :], parts):
            for k in range(half):
                out_ref[(z ^ k) * 2 + y] = refs[k][:, part]
                out_ref[(z ^ k) * 2 + (1 - y)] = refs[half + k][:, part] if fine else refs[half][k, :, part]

    outs = local_call(
        name,
        kernel,
        [shaped((count, rows, part.stop - part.start), mine[0].dtype) for part in parts],
        places(), *mine, *other,
        smem=(0,),
    )
    outs = [one.reshape(count * rows, -1) for one in outs]
    return outs if cuts else outs[0]


def places():
    dp, heads = lax.axis_index("dp"), lax.axis_index("heads")
    return jnp.stack([dp // 2, dp % 2, heads, heads % 2]).astype(jnp.int32)


def split_rows(name, totals, cuts=()):
    count = lax.axis_size("dp")
    half = count // 2
    operands, columns = [], 0
    for own, received in totals:
        rows = own.shape[0] // count
        operands += [one.reshape(count, rows, own.shape[1]) for one in (own, received) if one is not None]
        columns += own.shape[1]
    bounds = [0, *cuts, columns]
    parts = list(zip(bounds, bounds[1:]))

    def kernel(place_ref, *refs):
        ins, outs = refs[: len(operands)], refs[len(operands) :]
        z, y = place_ref[0], place_ref[1]
        for k in range(half):
            for side in range(2):
                block = (z ^ k) * 2 + (1 - y if side == 0 else y)
                at, column = 0, 0
                for own, received in totals:
                    value = ins[at][block].astype(F32)
                    at += 1
                    if received is not None:
                        value = value + ins[at][block].astype(F32)
                        at += 1
                    for i, (start, stop) in enumerate(parts):
                        first, last = max(start, column), min(stop, column + own.shape[1])
                        if first < last:
                            ref = outs[2 * i + side]
                            ref[k, :, first - start : last - start] = value[:, first - column : last - column].astype(
                                ref.dtype
                            )
                    column += own.shape[1]

    outs = []
    for start, stop in parts:
        outs += [shaped((half, rows, stop - start), BF16), shaped((half, rows, stop - start), F32)]
    outs = local_call(name, kernel, outs, places(), *operands, smem=(0,))
    return list(zip(outs[::2], outs[1::2]))


def y_sums(name, pieces, flops=0):
    half, rows, _ = pieces[0][0].shape
    columns = [keep.shape[2] for keep, _ in pieces]
    fine = len(pieces[0][1]) > 1
    operands = [one for keep, arrived in pieces for one in (keep, *arrived)]
    step = 1 + len(pieces[0][1])

    def kernel(*refs):
        ins, outs = refs[: len(operands)], refs[len(operands) :]
        column = 0
        for i, width in enumerate(columns):
            part = slice(column, column + width)
            column += width
            for k in range(half):
                there = ins[i * step + 1 + k][...] if fine else ins[i * step + 1][k]
                value = ins[i * step][k] + there.astype(F32)
                outs[k][:, part] = value.astype(outs[k].dtype)

    outs = [shaped((rows, sum(columns)), F32)] + [shaped((rows, sum(columns)), BF16)] * (half - 1)
    return local_call(name, kernel, outs, *operands, flops=flops)


def z_swaps(summed):
    return [summed[0]] + [dp_swap(summed[k], 2 * k) for k in range(1, len(summed))]


def head_pairs(width):
    pair = 2 * HEAD_DIM
    return [(at, min(at + pair, width), min(2, (width - at) // HEAD_DIM)) for at in range(0, width, pair)]


def by_head(value, heads):
    if heads == 1:
        return value
    lane = lax.broadcasted_iota(jnp.int32, value.shape, 1)
    zero = jnp.zeros_like(value)
    return jnp.concatenate(
        [jnp.where(lane < HEAD_DIM, value, zero), jnp.where(lane < HEAD_DIM, zero, value)], 0
    )


def own_columns(value, heads):
    if heads == 1:
        return value
    count = value.shape[1] // 2
    return jnp.concatenate([value[:HEAD_DIM, :count], value[HEAD_DIM:, count:]], 0)


def own_rows(value, heads):
    if heads == 1:
        return value
    count = value.shape[0] // 2
    lane = lax.broadcasted_iota(jnp.int32, (count, value.shape[1]), 1)
    return jnp.where(lane < HEAD_DIM, value[:count], value[count:])


def masked_bias(allowed):
    return jnp.where(allowed, 0.0, MASKED).astype(F32)


def pair_forward(q, keys, values, bias, heads):
    scores = dot_nt(keys, by_head(q, heads)) + (bias if heads == 1 else jnp.concatenate([bias, bias], 1))
    top = jnp.max(scores, 0, keepdims=True)
    exps = jnp.exp(scores - top)
    total = jnp.sum(exps, 0, keepdims=True)
    out = dot_tn(values, exps.astype(BF16)) / total
    log = top + jnp.log(total)
    count = q.shape[0]
    return own_columns(out, heads), [log[:, h * count : (h + 1) * count] for h in range(heads)]


def pair_backward(q, grad, keys, values, bias, logs, heads):
    q, grad = by_head(q, heads), by_head(grad, heads)
    if heads > 1:
        bias, logs = jnp.concatenate([bias, bias], 1), [jnp.concatenate(logs, 1)]
    probs = jnp.exp(dot_nt(keys, q) + bias - logs[0])
    grad_probs = dot_nt(values, grad)
    delta = jnp.sum(probs * grad_probs, 0, keepdims=True)
    grad_scores = (probs * (grad_probs - delta)).astype(BF16)
    grad_q = own_columns(dot_tn(keys, grad_scores), heads) * SCALE
    return grad_q, dot(grad_scores, q), dot(probs.astype(BF16), grad)


def sort_kernel(
    place_ref, clip_ref, frame_ref, patch_ref, tokens_ref, dy_ref,
    sorted_ref, order_ref, back_ref, col_ref, row_ref, space_col_ref, space_row_ref, own_ref, own_dy_ref,
    all_ref,
):
    count = tokens_ref.shape[0]
    rows = count // 2
    core = place_ref[3]
    own = pl.ds(pl.multiple_of(core * rows, rows), rows)
    far = pl.ds(pl.multiple_of((1 - core) * rows, rows), rows)
    own_ref[...] = tokens_ref[own, :]
    own_dy_ref[...] = dy_ref[own, :]
    all_ref[:rows, :] = tokens_ref[own, :]
    all_ref[rows:, :] = tokens_ref[far, :]
    ids = [clip_ref, frame_ref, patch_ref]
    spare = jnp.zeros((5, count), jnp.int32)
    natural = jnp.concatenate([ref[...] for ref in ids] + [spare], 0)
    space_row_ref[...] = natural
    space_col_ref[...] = natural.astype(F32).T.astype(jnp.int32)
    ordered = jnp.concatenate(
        [jnp.concatenate([ref[:, own], ref[:, far]], 1) for ref in ids] + [spare], 0
    )
    ordered_col = ordered.astype(F32).T.astype(jnp.int32)
    key_row = (ordered[0:1] * 128 + ordered[2:3] + 1) * 64 + ordered[1:2] + 1
    key_col = (ordered_col[:, 0:1] * 128 + ordered_col[:, 2:3] + 1) * 64 + ordered_col[:, 1:2] + 1
    rank_row = jnp.zeros((1, count), jnp.int32)
    for i in range(0, count, CHUNK):
        smaller = key_col[i : i + CHUNK] < key_row
        rank_row = rank_row + jnp.sum(smaller.astype(jnp.int32), 0, keepdims=True)
    for i in range(0, count, CHUNK):
        at = slice(i, i + CHUNK)
        place = lax.broadcasted_iota(jnp.int32, (CHUNK, count), 0) + i
        order = (place == rank_row).astype(F32).astype(BF16)
        order_ref[at, :] = order
        rank_col = jnp.sum((key_row < key_col[at]).astype(jnp.int32), 1, keepdims=True)
        place = lax.broadcasted_iota(jnp.int32, (CHUNK, count), 1)
        back_ref[at, :] = (place == rank_col).astype(F32).astype(BF16)
        sorted_ref[at, :] = dot(order, all_ref[...]).astype(BF16)
        col_ref[at, :] = dot(order, ordered_col.astype(F32).astype(BF16))
        row_ref[:, at] = dot_nt(ordered.astype(F32).astype(BF16), order)


def pack_kernel(weights_ref, vectors_ref, head_ref, space_ref, up_ref, down_ref):
    width, hidden = space_ref.shape[1] // 4, up_ref.shape[1]
    rows = weights_ref.shape[0]
    start = head_ref.shape[1] - 2 * width
    unit = lax.broadcasted_iota(jnp.int32, (rows, rows), 0) == lax.broadcasted_iota(jnp.int32, (rows, rows), 1)
    vectors = jnp.concatenate([vectors_ref[...], jnp.zeros((16 - VECTORS, rows), F32)], 0).astype(BF16)
    head_ref[:, : 3 * width] = weights_ref[:, : 3 * width].astype(BF16)
    head_ref[:, 3 * width : start] = jnp.zeros((rows, start - 3 * width), BF16)
    head_ref[:, 3 * width : 3 * width + 16] = dot_nt(unit.astype(F32).astype(BF16), vectors).astype(BF16)
    head_ref[:, start : start + width] = weights_ref[:, 4 * width : 5 * width].astype(BF16)
    head_ref[:, start + width :] = weights_ref[:, 3 * width : 4 * width].astype(BF16)
    space_ref[...] = weights_ref[:, 5 * width : 9 * width].astype(BF16)
    up_ref[...] = weights_ref[:, 9 * width : 9 * width + hidden].astype(BF16)
    down_ref[...] = weights_ref[:, 9 * width + hidden :].astype(BF16)


def same_clip_patch(col_ref, row_ref, keys, queries):
    key = col_ref[keys, :]
    query = row_ref[:, queries]
    return (key[:, 0:1] * 128 + key[:, 2:3]) == (query[0:1] * 128 + query[2:3])


def temporal_window(i, count):
    first = i * BLOCK
    start = jnp.clip(first - (WINDOW - BLOCK) // 2, 0, count - WINDOW)
    return (
        pl.ds(pl.multiple_of(first, BLOCK), BLOCK),
        pl.ds(pl.multiple_of(start, (WINDOW - BLOCK) // 2), WINDOW),
    )


def time_forward_kernel(
    maps_ref, tokens_ref, back_ref, col_ref, row_ref,
    vec_ref, first_ref, inputs_ref, own_ref, far_ref, log_ref, heads_ref,
):
    count, width = tokens_ref.shape[0], own_ref.shape[1]
    columns = maps_ref.shape[1]
    lanes = maps_ref[:, columns - 128 :].astype(F32).T
    offset = 3 * width - (columns - 128)
    vec_ref[...] = lanes[offset : offset + 16]
    gain, shift = vec_ref[0:1], vec_ref[1:2]

    def project(at):
        hat, _ = normed(tokens_ref[at, :].astype(F32))
        first = (hat * gain + shift).astype(BF16)
        first_ref[at, :] = first
        inputs_ref[at, :] = dot(first, maps_ref[:, : 3 * width]).astype(BF16)

    chunk_loop(count, project)

    def step(i, carry):
        queries, keys = temporal_window(i, count)
        bias = masked_bias(same_clip_patch(col_ref, row_ref, keys, queries))
        outs, logs = [], []
        for start, stop, heads in head_pairs(width):
            out, log = pair_forward(
                inputs_ref[queries, start:stop] * BF16(SCALE),
                inputs_ref[keys, width + start : width + stop],
                inputs_ref[keys, 2 * width + start : 2 * width + stop],
                bias,
                heads,
            )
            outs.append(out)
            logs += log
        heads_ref[queries, :] = jnp.concatenate(outs, 0).T.astype(BF16)
        log_ref[:, queries] = jnp.concatenate(logs + [logs[0]] * (8 - len(logs)), 0)
        return carry

    lax.fori_loop(0, count // BLOCK, step, 0, unroll=8)
    rows = count // 2
    for i in range(0, rows, CHUNK):
        own_ref[i : i + CHUNK, :] = dot(back_ref[i : i + CHUNK, :], heads_ref[...]).astype(BF16)
        far_ref[i : i + CHUNK, :] = dot(back_ref[rows + i : rows + i + CHUNK, :], heads_ref[...]).astype(BF16)


def time_backward_kernel(
    own_ref, far_ref, order_ref, inputs_ref, log_ref, col_ref, row_ref,
    out_ref, grad_ref, sum_ref,
):
    count, width = inputs_ref.shape[0], own_ref.shape[1]
    rows = count // 2
    for i in range(0, count, CHUNK):
        grad_ref[i : i + CHUNK, :] = (
            dot(order_ref[i : i + CHUNK, :rows], own_ref[...]) + dot(order_ref[i : i + CHUNK, rows:], far_ref[...])
        ).astype(BF16)
    sum_ref[...] = jnp.zeros_like(sum_ref)

    def step(i, carry):
        queries, keys = temporal_window(i, count)
        bias = masked_bias(same_clip_patch(col_ref, row_ref, keys, queries))
        grad_qs, head = [], 0
        for start, stop, heads in head_pairs(width):
            grad_q, grad_k, grad_v = pair_backward(
                inputs_ref[queries, start:stop] * BF16(SCALE),
                grad_ref[queries, start:stop],
                inputs_ref[keys, width + start : width + stop],
                inputs_ref[keys, 2 * width + start : 2 * width + stop],
                bias,
                [log_ref[h : h + 1, queries] for h in range(head, head + heads)],
                heads,
            )
            head += heads
            grad_qs.append(grad_q)
            sum_ref[keys, start:stop] += grad_k
            sum_ref[keys, width + start : width + stop] += grad_v
        out_ref[queries, :width] = jnp.concatenate(grad_qs, 0).T.astype(BF16)
        return carry

    lax.fori_loop(0, count // BLOCK, step, 0, unroll=8)

    def store(at):
        out_ref[at, width:] = sum_ref[at, :].astype(BF16)

    chunk_loop(count, store)


def space_window(i, core, rows):
    first = core * rows + i * BLOCK
    start = jnp.clip(first - (WINDOW - BLOCK) // 2, 0, 2 * rows - WINDOW)
    return (
        pl.ds(pl.multiple_of(i * BLOCK, BLOCK), BLOCK),
        pl.ds(pl.multiple_of(first, BLOCK), BLOCK),
        pl.ds(pl.multiple_of(start, (WINDOW - BLOCK) // 2), WINDOW),
    )


def whole_pairs(core, pairs_ref, got_ref, whole_ref):
    rows, width = pairs_ref.shape[0], pairs_ref.shape[1] // 4
    whole_ref[pl.ds(pl.multiple_of(core * rows, rows), rows), :] = pairs_ref[...]
    there = pl.ds(pl.multiple_of((1 - core) * rows, rows), rows)
    for i, j in enumerate((1, 0, 3, 2)):
        whole_ref[there, i * width : (i + 1) * width] = got_ref[:, j * width : (j + 1) * width]


def class_rows(row):
    number = lax.broadcasted_iota(jnp.int32, (CLASSES, row.shape[1]), 0)
    return (row[0:1] == number) & (row[1:2] < 0)


def space_bias(col_ref, row_ref, queries, keys):
    key, query = col_ref[keys, :], row_ref[:, queries]
    frame = jnp.where(key[:, 1:2] < 0, -1, key[:, 0:1] * 128 + key[:, 1:2]) == query[0:1] * 128 + query[1:2]
    number = lax.broadcasted_iota(jnp.int32, (CLASSES, BLOCK), 0)
    return masked_bias(jnp.concatenate([frame & (query[1:2] >= 0), number == query[0:1]], 0))


def class_allowed(row_ref):
    number = lax.broadcasted_iota(jnp.int32, (CLASSES, row_ref.shape[1]), 0)
    return row_ref[0:1] == number


def space_forward_kernel(
    place_ref, q_ref, pairs_ref, got_ref, col_ref, row_ref, out_own_ref, out_far_ref,
    heads_ref, log_ref, class_log_ref, part_ref, whole_ref, class_ref,
):
    core = place_ref[3]
    rows, width = q_ref.shape
    whole_pairs(core, pairs_ref, got_ref, whole_ref)
    here = pl.ds(pl.multiple_of(core * rows, rows), rows)
    classes = class_rows(row_ref[...]).astype(F32).astype(BF16)
    own_classes = class_rows(row_ref[:, here]).astype(F32).astype(BF16)
    class_ref[...] = dot(classes, whole_ref[...]).astype(BF16)
    def both(keys, part):
        return jnp.concatenate([whole_ref[keys, part], class_ref[:, part]], 0)

    def step(i, carry):
        local, queries, keys = space_window(i, core, rows)
        bias = space_bias(col_ref, row_ref, queries, keys)
        outs, logs = [], []
        for start, stop, heads in head_pairs(width):
            out, log = pair_forward(
                q_ref[local, start:stop] * BF16(SCALE),
                both(keys, slice(start, stop)),
                both(keys, slice(width + start, width + stop)),
                bias,
                heads,
            )
            outs.append(out)
            logs += log
        heads_ref[local, :] = jnp.concatenate(outs, 0).T.astype(BF16)
        log_ref[:, local] = jnp.concatenate(logs + [logs[0]] * (8 - len(logs)), 0)
        return carry

    lax.fori_loop(0, rows // BLOCK, step, 0, unroll=UNROLL)

    bias = masked_bias(class_allowed(row_ref))
    class_q = dot(own_classes, q_ref[...]).astype(BF16) * BF16(SCALE)
    outs, logs = [], []
    for start, stop, heads in head_pairs(width):
        scores = dot_nt(by_head(class_q[:, start:stop], heads), whole_ref[:, start:stop])
        scores = scores + (bias if heads == 1 else jnp.concatenate([bias, bias], 0))
        top = jnp.max(scores, 1, keepdims=True)
        exps = jnp.exp(scores - top)
        total = jnp.sum(exps, 1, keepdims=True)
        outs.append(own_rows(dot(exps.astype(BF16), whole_ref[:, width + start : width + stop]) / total, heads))
        log = top + jnp.log(total)
        logs += [log[h * CLASSES : (h + 1) * CLASSES] for h in range(heads)]
    class_log_ref[...] = jnp.concatenate(logs + [logs[0]] * (8 - len(logs)), 1)
    class_out = jnp.concatenate(outs, 1).astype(BF16)
    is_class = col_ref[here, 1:2] < 0

    def replace(at):
        back = dot_tn(own_classes, class_out).astype(BF16)
        heads_ref[...] = jnp.where(is_class, back, heads_ref[...])

    replace(None)
    group = width // 2

    def project(at):
        part_ref[at, :] = (
            dot_nt(heads_ref[at, :group], out_own_ref[:, 3 * group :])
            + dot_nt(heads_ref[at, group:], out_far_ref[:, 3 * group :])
        ).astype(BF16)

    chunk_loop(rows, project)


def space_back_in_kernel(
    part_ref, got_ref, stream_ref, vec_ref, dy_ref, out_own_ref, out_far_ref,
    grad_ref, low_ref, sums_ref, heads_ref,
):
    group = heads_ref.shape[1] // 2
    gain = vec_ref[7:8]
    sums_ref[...] = jnp.zeros_like(sums_ref)

    def through_norm(at):
        grad = part_ref[at, :].astype(F32) + got_ref[at, :].astype(F32)
        hat, factor = normed(stream_ref[at, :])
        dy = dy_ref[at, :].astype(F32)
        dx = dy + norm_grad(hat, factor, gain, grad)
        grad_ref[at, :] = dx
        low = dx.astype(BF16)
        low_ref[at, :] = low
        heads_ref[at, :group] = dot(low, out_own_ref[:, 3 * group :]).astype(BF16)
        heads_ref[at, group:] = dot(low, out_far_ref[:, 3 * group :]).astype(BF16)
        sums_ref[0:4] += jnp.concatenate(
            [column_sum(dx), column_sum(grad * hat), column_sum(grad), column_sum(dy)], 0
        )

    chunk_loop(grad_ref.shape[0], through_norm)


def space_backward_kernel(
    place_ref, heads_ref, q_ref, pairs_ref, got_ref, log_ref, class_log_ref, col_ref, row_ref,
    dq_ref, keep_ref, send_ref,
    whole_ref, class_ref, total_ref, class_total_ref, class_dq_ref,
):
    core = place_ref[3]
    rows, width = q_ref.shape
    whole_pairs(core, pairs_ref, got_ref, whole_ref)
    here = pl.ds(pl.multiple_of(core * rows, rows), rows)
    there = pl.ds(pl.multiple_of((1 - core) * rows, rows), rows)
    classes = class_rows(row_ref[...]).astype(F32)
    own_classes = class_rows(row_ref[:, here]).astype(F32).astype(BF16)
    class_ref[...] = dot(classes.astype(BF16), whole_ref[...]).astype(BF16)
    class_total_ref[...] = jnp.zeros_like(class_total_ref)
    bias = masked_bias(class_allowed(row_ref))
    class_q = dot(own_classes, q_ref[...]).astype(BF16) * BF16(SCALE)
    class_g = dot(own_classes, heads_ref[...]).astype(BF16)
    head = 0
    for start, stop, heads in head_pairs(width):
        keys, values = whole_ref[:, start:stop], whole_ref[:, width + start : width + stop]
        q, grad = by_head(class_q[:, start:stop], heads), by_head(class_g[:, start:stop], heads)
        logs = [class_log_ref[:, h : h + 1] for h in range(head, head + heads)]
        head += heads
        scores = dot_nt(q, keys) + (bias if heads == 1 else jnp.concatenate([bias, bias], 0))
        probs = jnp.exp(scores - jnp.concatenate(logs, 0))
        grad_probs = dot_nt(grad, values)
        grad_scores = (probs * (grad_probs - jnp.sum(probs * grad_probs, 1, keepdims=True))).astype(BF16)
        class_dq_ref[:, start:stop] = own_rows(dot(grad_scores, keys) * SCALE, heads).astype(BF16)
        total_ref[:, start:stop] = dot_tn(grad_scores, q)
        total_ref[:, width + start : width + stop] = dot_tn(probs.astype(BF16), grad)

    def both(keys, part):
        return jnp.concatenate([whole_ref[keys, part], class_ref[:, part]], 0)

    def step(i, carry):
        local, queries, keys = space_window(i, core, rows)
        bias = space_bias(col_ref, row_ref, queries, keys)
        is_class = row_ref[1:2, queries] < 0
        grad_qs, head = [], 0
        for start, stop, heads in head_pairs(width):
            key_part, value_part = slice(start, stop), slice(width + start, width + stop)
            grad_q, grad_k, grad_v = pair_backward(
                q_ref[local, start:stop] * BF16(SCALE),
                heads_ref[local, start:stop],
                both(keys, key_part),
                both(keys, value_part),
                bias,
                [jnp.where(is_class, -MASKED, log_ref[h : h + 1, local]) for h in range(head, head + heads)],
                heads,
            )
            head += heads
            grad_qs.append(grad_q)
            total_ref[keys, key_part] += grad_k[:WINDOW]
            total_ref[keys, value_part] += grad_v[:WINDOW]
            class_total_ref[:, key_part] += grad_k[WINDOW:]
            class_total_ref[:, value_part] += grad_v[WINDOW:]
        dq_ref[local, :] = jnp.concatenate(grad_qs, 0).T.astype(BF16)
        return carry

    lax.fori_loop(0, rows // BLOCK, step, 0, unroll=UNROLL)
    dq_ref[...] = jnp.where(
        col_ref[here, 1:2] < 0, dot_tn(own_classes, class_dq_ref[...]).astype(BF16), dq_ref[...]
    )
    high = class_total_ref[...].astype(BF16)
    rest = (class_total_ref[...] - high.astype(F32)).astype(BF16)
    classes = classes.astype(BF16)
    total_ref[...] += dot_tn(jnp.concatenate([classes, classes], 0), jnp.concatenate([high, rest], 0))
    keep_ref[...] = total_ref[here, :]
    send_ref[...] = total_ref[there, :].astype(BF16)


def mix_kernel(place_ref, out_ref, own_ref, x_ref, core_ref, vec_ref, mix_ref, fused_ref, bias_ref):
    place = place_ref[2]
    width = out_ref.shape[1]
    mix_ref[0] = own_ref[...]
    mix_ref[1] = core_ref[:, :width]
    mix_ref[2] = x_ref[...]
    mix_ref[3] = core_ref[:, width:]
    total, bias = 0.0, 0.0
    low = vec_ref[...].astype(BF16)
    for j in range(4):
        block = mix_ref[place ^ j]
        total = total + dot(block, out_ref[j * width : (j + 1) * width, :])
        bias = bias + dot_nt(low[:, j * width : (j + 1) * width], block)
    fused_ref[...] = total.astype(BF16)
    bias_ref[...] = bias[2:3] + vec_ref[3:4]


def time_out_kernel(own_ref, got_ref, fused_ref, far_ref, part_ref):
    def project(at):
        part_ref[at, :] = (dot_nt(own_ref[at, :], fused_ref[...]) + dot_nt(got_ref[at, :], far_ref[...])).astype(BF16)

    chunk_loop(part_ref.shape[0], project)


def norm_in_kernel(gain_row, before_ref, part_ref, got_ref, shift_ref, vec_ref, stream_ref, normed_ref):
    gain, shift = vec_ref[gain_row : gain_row + 1], vec_ref[gain_row + 1 : gain_row + 2]

    def body(at):
        stream = (
            before_ref[at, :].astype(F32)
            + (part_ref[at, :].astype(F32) + got_ref[at, :].astype(F32))
            + shift_ref[0:1]
        )
        stream_ref[at, :] = stream
        hat, _ = normed(stream)
        normed_ref[at, :] = (hat * gain + shift).astype(BF16)

    chunk_loop(stream_ref.shape[0], body)


def space_in_kernel(second_ref, own_ref, far_ref, q_ref, pairs_ref):
    width = q_ref.shape[1] // 2

    def project(at):
        for g, maps_ref in enumerate((own_ref, far_ref)):
            inputs = dot(second_ref[at, :], maps_ref[:, : 3 * width]).astype(BF16)
            q_ref[at, g * width : (g + 1) * width] = inputs[:, :width]
            pairs_ref[at, g * width : (g + 1) * width] = inputs[:, width : 2 * width]
            pairs_ref[at, (2 + g) * width : (3 + g) * width] = inputs[:, 2 * width :]

    chunk_loop(q_ref.shape[0], project)


def gelu_parts(pre):
    cdf = 0.5 * (1.0 + lax.erf(pre * (0.5**0.5)))
    slope = cdf + pre * jnp.exp(-0.5 * pre * pre) * (1.0 / math.sqrt(2.0 * math.pi))
    return pre * cdf, slope


def feed_kernel(
    third_ref, dy_ref, up_ref, up_far_ref, down_ref, down_far_ref, activ_ref, grad_ref, back_ref
):
    hidden = activ_ref.shape[1] // 2

    def project(at):
        back = 0.0
        for g, (ups_ref, downs_ref) in enumerate(((up_ref, down_ref), (up_far_ref, down_far_ref))):
            act, slope = gelu_parts(dot(third_ref[at, :], ups_ref[...]))
            part = slice(g * hidden, (g + 1) * hidden)
            activ_ref[at, part] = act.astype(BF16)
            grad = (dot(dy_ref[at, :], downs_ref[...]) * slope).astype(BF16)
            grad_ref[at, part] = grad
            back = back + dot_nt(grad, ups_ref[...])
        back_ref[at, :] = back.astype(BF16)

    chunk_loop(third_ref.shape[0], project)


def feed_out_kernel(activ_ref, own_ref, far_ref, part_ref):
    hidden = activ_ref.shape[1] // 2

    def project(at):
        part_ref[at, :] = (
            dot_nt(activ_ref[at, :hidden], own_ref[...]) + dot_nt(activ_ref[at, hidden:], far_ref[...])
        ).astype(BF16)

    chunk_loop(part_ref.shape[0], project)


def feed_grads_kernel(group, third_ref, grad_ref, dy_ref, activ_ref, out_ref):
    hidden = out_ref.shape[1] // 2
    part = slice(group * hidden, (group + 1) * hidden)
    out_ref[:, :hidden] = dot_tn(third_ref[...], grad_ref[:, part]).astype(BF16)
    out_ref[:, hidden:] = dot_tn(dy_ref[...], activ_ref[:, part]).astype(BF16)


def space_back_kernel(
    dq_ref, keep_ref, got_ref, own_ref, far_ref, grad_own_ref, grad_far_ref, part_ref
):
    width = dq_ref.shape[1] // 2

    def project(at):
        total = 0.0
        for g, (maps_ref, grad_ref) in enumerate(((own_ref, grad_own_ref), (far_ref, grad_far_ref))):
            grad_ref[at, :width] = dq_ref[at, g * width : (g + 1) * width]
            for i in (1, 2):
                mine = slice((2 * i - 2 + g) * width, (2 * i - 1 + g) * width)
                theirs = slice((2 * i - 1 - g) * width, (2 * i - g) * width)
                grad_ref[at, i * width : (i + 1) * width] = (
                    keep_ref[at, mine] + got_ref[at, theirs].astype(F32)
                ).astype(BF16)
            total = total + dot_nt(grad_ref[at, :], maps_ref[:, : 3 * width])
        part_ref[at, :] = total.astype(BF16)

    chunk_loop(part_ref.shape[0], project)


def space_grads_kernel(group, second_ref, grad_ref, low_ref, heads_ref, out_ref):
    width = heads_ref.shape[1] // 2
    out_ref[:, : 3 * width] = dot_tn(second_ref[...], grad_ref[...]).astype(BF16)
    out_ref[:, 3 * width :] = dot_tn(low_ref[...], heads_ref[:, group * width : (group + 1) * width]).astype(BF16)


def time_back_in_kernel(
    part_ref, got_ref, stream_ref, vec_ref, before_ref, fused_ref, far_ref,
    grad_ref, low_ref, sums_ref, own_ref, send_ref,
):
    gain = vec_ref[4:5]
    sums_ref[...] = jnp.zeros_like(sums_ref)

    def through_norm(at):
        grad = part_ref[at, :].astype(F32) + got_ref[at, :].astype(F32)
        hat, factor = normed(stream_ref[at, :])
        dx = before_ref[at, :] + norm_grad(hat, factor, gain, grad)
        grad_ref[at, :] = dx
        low = dx.astype(BF16)
        low_ref[at, :] = low
        own_ref[at, :] = dot(low, fused_ref[...]).astype(BF16)
        send_ref[at, :] = dot(low, far_ref[...]).astype(BF16)
        sums_ref[0:4] += jnp.concatenate(
            [column_sum(low.astype(F32)), column_sum(dx), column_sum(grad * hat), column_sum(grad)], 0
        )

    chunk_loop(grad_ref.shape[0], through_norm)


def time_grads_kernel(place_ref, first_ref, grad_ref, row_sum_ref, send_ref, keep_ref, total_ref):
    half, rows, columns = keep_ref.shape
    width = columns - row_sum_ref.shape[1]
    z, y = place_ref[0], place_ref[1]
    total_ref[:, :width] = dot_tn(first_ref[...], grad_ref[...])
    total_ref[:, width:] = row_sum_ref[...]
    for k in range(half):
        mine = pl.ds(pl.multiple_of(((z ^ k) * 2 + y) * rows, 8), rows)
        theirs = pl.ds(pl.multiple_of(((z ^ k) * 2 + (1 - y)) * rows, 8), rows)
        send_ref[k] = total_ref[theirs, :].astype(BF16)
        keep_ref[k] = total_ref[mine, :]


def time_back_kernel(
    grad_ref, maps_ref, tokens_ref, back_ref, bias_ref, one_ref, two_ref, own_ref, far_ref, sums_ref, sorted_ref
):
    count, width = tokens_ref.shape[0], grad_ref.shape[1] // 3
    sums_ref[...] = jnp.zeros_like(sums_ref)
    sums_ref[2:3] = 0.5 * bias_ref[0:1]
    sums_ref[3:6] = 0.5 * one_ref[1:4]
    sums_ref[6:10] = 0.5 * two_ref[0:4]

    def project(at):
        grad = dot_nt(grad_ref[at, :], maps_ref[:, : 3 * width])
        hat, _ = normed(tokens_ref[at, :].astype(F32))
        sums_ref[0:2] += jnp.concatenate([column_sum(grad * hat), column_sum(grad)], 0)
        sorted_ref[at, :] = grad.astype(BF16)

    chunk_loop(count, project)
    rows = count // 2
    for i in range(0, rows, CHUNK):
        far_ref[i : i + CHUNK, :] = dot(back_ref[rows + i : rows + i + CHUNK, :], sorted_ref[...]).astype(BF16)
    for i in range(0, rows, CHUNK):
        own_ref[i : i + CHUNK, :] = dot(back_ref[i : i + CHUNK, :], sorted_ref[...]).astype(BF16)


def input_grad_kernel(part_ref, got_ref, tokens_ref, vec_ref, before_ref, out_ref):
    gain = vec_ref[0:1]

    def through_norm(at):
        grad = part_ref[at, :].astype(F32) + got_ref[at, :].astype(F32)
        hat, factor = normed(tokens_ref[at, :].astype(F32))
        out_ref[at, :] = before_ref[at, :] + norm_grad(hat, factor, gain, grad)

    chunk_loop(out_ref.shape[0], through_norm)


def layer_out_kernel(stream_ref, part_ref, got_ref, vec_ref, out_ref):
    out_ref[...] = stream_ref[...] + (part_ref[...].astype(F32) + got_ref[...].astype(F32)) + vec_ref[9:10]


def whole_rows_kernel(place_ref, own_ref, got_ref, out_ref):
    core = place_ref[3]
    rows = own_ref.shape[0]
    out_ref[pl.ds(pl.multiple_of(core * rows, rows), rows), :] = own_ref[...]
    out_ref[pl.ds(pl.multiple_of((1 - core) * rows, rows), rows), :] = got_ref[...]


def fused_grads_kernel(low_ref, heads_ref, got_heads_ref, own_ref, far_ref):
    ones = jnp.ones((low_ref.shape[0], own_ref.shape[1] - heads_ref.shape[1]), BF16)
    far_ref[...] = dot_tn(low_ref[...], jnp.concatenate([got_heads_ref[...], ones], 1)).astype(BF16)
    own_ref[...] = dot_tn(low_ref[...], jnp.concatenate([heads_ref[...], ones], 1))


def mix_grads_kernel(
    place_ref, fused_ref, got_ref, mix_ref, sums_ref, grad_out_ref, total_ref, row_sum_ref, bias_ref
):
    place = place_ref[2]
    width = total_ref.shape[1]
    both = fused_ref[...] + got_ref[...].astype(F32)
    row_sum_ref[...] = both[:, width:]
    fused = both[:, :width].astype(BF16)
    total_ref[...] = fused
    for j in range(4):
        block = mix_ref[place ^ j]
        grad_out_ref[j * width : (j + 1) * width, :] = dot_tn(block, fused).astype(BF16)
        bias_ref[:, j * width : (j + 1) * width] = dot(sums_ref[...].astype(BF16), block)


def mix_shard_kernel(place_ref, fused_ref, out_ref, keep_ref, send_ref):
    place = place_ref[2]
    width = out_ref.shape[1]
    fused = fused_ref[...].astype(BF16)
    for m in range(4):
        rows = out_ref[pl.ds(pl.multiple_of((place ^ m) * width, width), width), :]
        part = dot_nt(fused, rows)
        ref = send_ref if m % 2 else keep_ref
        ref[:, m // 2 * width : (m // 2 + 1) * width] = part.astype(ref.dtype)


def early_grad_kernel(groups, *refs):
    out_ref, square_ref = refs[-2:]
    count, column, square = (len(refs) - 2) // len(groups), 0, 0.0
    for i, (start, stop) in enumerate(groups):
        value = sum(ref[:, start:stop].astype(F32) for ref in refs[i * count : (i + 1) * count])
        out_ref[:, column : column + value.shape[1]] = value
        column += value.shape[1]
        square = square + jnp.sum(value * value)
    square_ref[...] = jnp.full(square_ref.shape, square, F32)


def whole_grad_kernel(early_ref, square_ref, vector_ref, bias_ref, out_ref, mix_ref, *refs):
    grad_ref, sums_ref = refs[-2:]
    width = mix_ref.shape[1]
    total = sum(ref[...].astype(F32) for ref in refs[:-2])
    row_sum = total[:, 3 * width : 3 * width + 1]
    mix = mix_ref[...] + row_sum * bias_ref[...]
    grad_ref[:, 5 * width :] = early_ref[...]
    square = square_ref[...]
    for i, value in ((0, total[:, : 3 * width]), (3, out_ref[:, :width]), (4, mix)):
        grad_ref[:, i * width : i * width + value.shape[1]] = value
        square = square + jnp.sum(value * value)
    sums_ref[...] = vector_ref[...]
    sums_ref[VECTORS : VECTORS + 1] = square


def adam_update(master, first_moment, second_moment, average, gradient, factor, rate, decay):
    clipped = gradient * factor
    first_new = BETA_FIRST * first_moment + (1.0 - BETA_FIRST) * clipped
    second_new = BETA_SECOND * second_moment + (1.0 - BETA_SECOND) * clipped * clipped
    first_hat = first_new / (1.0 - BETA_FIRST**STEP)
    second_hat = second_new / (1.0 - BETA_SECOND**STEP)
    master_new = master - rate * (first_hat / (jnp.sqrt(second_hat) + ADAM_EPS) + decay * master)
    average_new = AVERAGE_RATE * average + (1.0 - AVERAGE_RATE) * master_new
    return (master_new, first_new, second_new, average_new)


def local(
    tokens,
    cotangent,
    clip_ids,
    frame_ids,
    patch_ids,
    weights,
    weights_m,
    weights_v,
    weights_ema,
    vectors,
    vectors_m,
    vectors_v,
    vectors_ema,
):
    group_count = lax.axis_size("heads")
    core = lax.axis_index("heads") % 2
    place = places()
    count, features = tokens.shape
    width = features // group_count
    hidden = (weights.shape[1] - 9 * width) // 2
    rows = count // 2
    half = lax.axis_size("dp") // 2
    shard = weights.shape[0]

    wide = lambda n, dtype: shaped((rows, n), dtype)

    head_start = -(-(3 * width + 16) // 128) * 128
    head_piece, space_piece, up_piece, down_piece = local_call(
        "pack",
        pack_kernel,
        [shaped((shard, n), BF16) for n in (head_start + 2 * width, 4 * width, hidden, hidden)],
        weights, vectors,
    )
    head_z = z_blocks(head_piece)
    tokens_sorted, order, back, time_col, time_row, space_col, space_row, tokens_own, dy = local_call(
        "sort_rows",
        sort_kernel,
        [
            shaped((count, features), BF16),
            shaped((count, count), BF16),
            shaped((count, count), BF16),
            shaped((count, 8), F32),
            shaped((8, count), F32),
            shaped((count, 8), jnp.int32),
            shaped((8, count), jnp.int32),
            wide(features, BF16),
            wide(features, BF16),
        ],
        place, clip_ids, frame_ids, patch_ids, tokens, cotangent,
        smem=(0,),
        scratch=[pltpu.VMEM((count, features), BF16)],
    )
    head_z, _ = together(head_z, [tokens_sorted])
    head_z[0] = head_piece
    head_y = y_blocks(head_z, True)
    space_z = z_blocks(after(space_piece, *head_z))
    (head_y,) = together(head_y)
    time_maps, mix_map, out_map = assemble(
        "gather_head", head_z, head_y, (head_start, head_start + width)
    )
    mix_x = x_swap(mix_map)

    vec, first, time_inputs, time_own, time_send, time_logs = local_call(
        "time_forward",
        time_forward_kernel,
        [
            shaped((16, features), F32),
            shaped((count, features), BF16),
            shaped((count, 3 * width), BF16),
            wide(width, BF16),
            wide(width, BF16),
            shaped((8, count), F32),
        ],
        time_maps, tokens_sorted, back, time_col, time_row,
        scratch=[pltpu.VMEM((count, width), BF16)],
    )
    space_z, (mix_x, time_send) = together(space_z, [mix_x, time_send])
    mix_core = core_swap(jnp.concatenate([mix_map, mix_x], 1))
    time_got = core_swap(time_send)

    mix_blocks, fused, mix_bias = local_call(
        "mix_maps",
        mix_kernel,
        [
            shaped((group_count, features, width), BF16),
            shaped((features, width), BF16),
            shaped((1, features), F32),
        ],
        place, out_map, mix_map, mix_x, mix_core, vec,
        smem=(0,),
    )
    fused_far = core_swap(fused)
    space_y = y_blocks(space_z)
    up_z = z_blocks(after(up_piece, *space_z))
    (time_part,) = local_call("time_out", time_out_kernel, [wide(features, BF16)], time_own, time_got, fused, fused_far)
    stream_one, second = local_call(
        "space_norm",
        partial(norm_in_kernel, 4),
        [wide(features, F32), wide(features, BF16)],
        tokens_own, time_part, x_swap(time_part), mix_bias, vec,
        flops=LONG,
    )

    space_own = assemble("gather_space", space_z, space_y)
    space_far = core_swap(space_own)
    space_q, space_pairs = local_call(
        "space_in",
        space_in_kernel,
        [wide(2 * width, BF16), wide(4 * width, BF16)],
        second, space_own, space_far,
    )
    up_z, (space_q, space_pairs) = together(up_z, [space_q, space_pairs])
    up_y = y_blocks(up_z)
    down_z = z_blocks(after(down_piece, *up_z))
    space_got = core_swap(space_pairs)
    space_heads, space_logs, class_logs, space_part = local_call(
        "space_forward",
        space_forward_kernel,
        [wide(2 * width, BF16), shaped((8, rows), F32), shaped((CLASSES, 8), F32), wide(features, BF16)],
        place, space_q, space_pairs, space_got, space_col, space_row, space_own, space_far,
        smem=(0,),
        scratch=[pltpu.VMEM((count, 4 * width), BF16), pltpu.VMEM((CLASSES, 4 * width), BF16)],
    )
    up_y, down_z, (space_part,) = together(up_y, down_z, [space_part])
    stream_two, third = local_call(
        "feed_norm",
        partial(norm_in_kernel, 7),
        [wide(features, F32), wide(features, BF16)],
        stream_one, space_part, x_swap(space_part), vec[6:8], vec,
        flops=LONG,
    )

    up_own = assemble("gather_up", up_z, up_y)
    up_far = core_swap(up_own)
    down_own = assemble("gather_down", down_z, y_blocks(down_z))
    down_far = core_swap(down_own)
    activ, grad_pre, third_part = local_call(
        "feed",
        feed_kernel,
        [wide(2 * hidden, BF16), wide(2 * hidden, BF16), wide(features, BF16)],
        third, dy, up_own, up_far, down_own, down_far,
    )
    third_got = x_swap(third_part)
    feed_grad_far, feed_grad_own = [
        local_call(
            name,
            partial(feed_grads_kernel, group),
            [shaped((features, 2 * hidden), BF16)],
            third, grad_pre, dy, activ,
        )[0]
        for name, group in (("feed_grads_far", 1), ("feed_grads_own", 0))
    ]
    (feed_part,) = local_call("feed_out", feed_out_kernel, [wide(features, BF16)], activ, down_own, down_far)
    (up_send, up_keep), (down_send, down_keep) = split_rows(
        "split_feed", [(feed_grad_own, core_swap(feed_grad_far))], (hidden,)
    )
    up_y = [dp_swap(up_send, 1)]
    feed_part_got = x_swap(feed_part)

    grad_two, grad_two_low, sums_two, space_grad_heads = local_call(
        "space_back_in",
        space_back_in_kernel,
        [wide(features, F32), wide(features, BF16), shaped((8, features), F32), wide(2 * width, BF16)],
        third_part, third_got, stream_two, vec, dy, space_own, space_far,
    )
    space_dq, space_keep, space_send = local_call(
        "space_backward",
        space_backward_kernel,
        [wide(2 * width, BF16), wide(4 * width, F32), wide(4 * width, BF16)],
        place, space_grad_heads, space_q, space_pairs, space_got, space_logs, class_logs, space_col, space_row,
        smem=(0,),
        scratch=[
            pltpu.VMEM((count, 4 * width), BF16),
            pltpu.VMEM((CLASSES, 4 * width), BF16),
            pltpu.VMEM((count, 4 * width), F32),
            pltpu.VMEM((CLASSES, 4 * width), F32),
            pltpu.VMEM((CLASSES, 2 * width), BF16),
        ],
    )
    up_y, (space_send, feed_part_got) = together(up_y, [space_send, feed_part_got])
    up_shards = z_swaps(y_sums("sum_up", [(up_keep, up_y)]))
    space_got_grads = core_swap(space_send)
    down_y = [dp_swap(after(down_send, *up_y), 1)]
    grad_space, grad_space_far, second_part = local_call(
        "space_back",
        space_back_kernel,
        [wide(3 * width, BF16), wide(3 * width, BF16), wide(features, BF16)],
        space_dq, space_keep, space_got_grads, space_own, space_far,
    )
    second_got = x_swap(second_part)
    space_grad_far, space_grad_own = [
        local_call(
            name,
            partial(space_grads_kernel, group),
            [shaped((features, 4 * width), BF16)],
            second, grad, grad_two_low, space_heads,
        )[0]
        for name, group, grad in (("space_grads_far", 1, grad_space_far), ("space_grads_own", 0, grad_space))
    ]

    def whole(name, value):
        (out,) = local_call(
            name, whole_rows_kernel, [shaped((count, features), F32)], place, value, core_swap(value), smem=(0,)
        )
        return out

    (layer_half,) = local_call(
        "layer_out", layer_out_kernel, [wide(features, F32)], stream_two, feed_part, feed_part_got, vec
    )
    layer_rows = whole("layer_rows", after(layer_half, space_got_grads))
    up_shards, (second_got, layer_rows) = together(up_shards, [second_got, layer_rows])
    ((space_y_send, space_keep),) = split_rows("split_space", [(space_grad_own, core_swap(space_grad_far))])
    space_y = [dp_swap(space_y_send, 1)]
    grad_one, grad_one_low, sums_one, time_grad_own, time_grad_send = local_call(
        "time_back_in",
        time_back_in_kernel,
        [
            wide(features, F32),
            wide(features, BF16),
            shaped((8, features), F32),
            wide(width, BF16),
            wide(width, BF16),
        ],
        second_part, second_got, stream_one, vec, grad_two, fused, fused_far,
    )
    down_y, (time_grad_own, time_grad_send, grad_one_low) = together(
        down_y, [time_grad_own, time_grad_send, grad_one_low]
    )
    down_shards = z_swaps(y_sums("sum_down", [(down_keep, down_y)]))
    time_grad_got = core_swap(time_grad_send)
    fused_grad, fused_grad_far = local_call(
        "fused_grads",
        fused_grads_kernel,
        [shaped((features, width + SPARE), F32), shaped((features, width + SPARE), BF16)],
        grad_one_low, time_own, time_got,
    )
    fused_grad_got = core_swap(fused_grad_far)
    grad_time_out, fused_total, row_sum, bias_grad = local_call(
        "mix_grads",
        mix_grads_kernel,
        [
            shaped((features, width), BF16),
            shaped((features, width), BF16),
            shaped((features, SPARE), F32),
            shaped((8, features), F32),
        ],
        place, fused_grad, fused_grad_got, mix_blocks, sums_one,
        smem=(0,),
    )
    ((out_send, out_keep),) = split_rows("split_out", [(grad_time_out, None), (fused_total, None)])
    out_send, time_grad_own, time_grad_got = lax.optimization_barrier((out_send, time_grad_own, time_grad_got))
    out_y = [dp_swap(out_send, 1)]
    (grad_time,) = local_call(
        "time_backward",
        time_backward_kernel,
        [shaped((count, 3 * width), BF16)],
        time_grad_own, time_grad_got, order, time_inputs, time_logs, time_col, time_row,
        scratch=[pltpu.VMEM((count, width), BF16), pltpu.VMEM((count, 2 * width), F32)],
    )
    down_shards, space_y, out_y, (grad_time,) = together(down_shards, space_y, out_y, [grad_time])
    time_columns = 3 * width + SPARE
    time_send, time_keep = local_call(
        "time_grads",
        time_grads_kernel,
        [shaped((half, shard, time_columns), BF16), shaped((half, shard, time_columns), F32)],
        place, first, grad_time, row_sum,
        smem=(0,),
        scratch=[pltpu.VMEM((features, time_columns), F32)],
    )
    space_y, out_y, (time_send, grad_time) = together(space_y, out_y, [time_send, grad_time])
    time_y = [dp_swap(time_send, 1)]
    late_shards = z_swaps(y_sums("sum_late", [(out_keep, out_y), (space_keep, space_y)]))
    first_own, first_send, vector_sum = local_call(
        "time_back",
        time_back_kernel,
        [wide(features, BF16), wide(features, BF16), shaped((16, features), F32)],
        grad_time, time_maps, tokens_sorted, back, bias_grad, sums_one, sums_two,
        scratch=[pltpu.VMEM((count, features), BF16)],
    )
    time_y, late_shards, (first_send,) = together(time_y, late_shards, [first_send])
    first_part = (first_own.astype(F32) + core_swap(first_send).astype(F32)).astype(BF16)
    first_part_got = x_swap(first_part)
    time_shards = y_sums("sum_time", [(time_keep, time_y)])
    time_shards = z_swaps(time_shards)

    out_width = 2 * width
    out_total = sum([one[:, :out_width].astype(F32) for one in late_shards])
    mix_keep, mix_send = local_call(
        "mix_shard",
        mix_shard_kernel,
        [shaped((shard, out_width), F32), shaped((shard, out_width), BF16)],
        place, out_total[:, width:], out_map,
        smem=(0,),
    )
    mix_sum = mix_keep + core_swap(mix_send).astype(F32)
    mix_total = mix_sum[:, :width] + x_swap(mix_sum[:, width:].astype(BF16)).astype(F32)

    (grad_half,) = local_call(
        "input_grad", input_grad_kernel, [wide(features, F32)], first_part, first_part_got, tokens_own, vec, grad_one
    )
    bias_part = lax.dynamic_slice_in_dim(vec[2:3], lax.axis_index("heads") * width, width, 1)
    late = [out_width, out_width + 4 * width]
    early_grad, early_square = local_call(
        "early_grad",
        partial(early_grad_kernel, (late, [0, hidden], [0, hidden])),
        [shaped((shard, 4 * width + 2 * hidden), F32), shaped((1, features), F32)],
        *late_shards, *up_shards, *down_shards,
        staged=True,
    )
    time_shards, (mix_total, early_grad) = together(time_shards, [mix_total, early_grad])
    weight_grad, sums = local_call(
        "whole_grad",
        whole_grad_kernel,
        [shaped(weights.shape, F32), shaped((16, features), F32)],
        early_grad, early_square, vector_sum, bias_part, out_total, mix_total, *time_shards,
        staged=True,
    )
    sums, grad_half = lax.optimization_barrier((sums, grad_half))
    grad_rows = whole("grad_rows", grad_half)
    sums = all_sum(sums)
    vector_all = sums[:VECTORS]
    vector_grad = lax.dynamic_slice_in_dim(vector_all, lax.axis_index("dp") * shard, shard, 1)
    grad_norm = jnp.sqrt(sums[VECTORS, 0] + jnp.sum(vector_all * vector_all))
    limit = 0.5 * math.sqrt(NPARAM)
    factor = limit / jnp.maximum(grad_norm, limit)
    weights_out = adam_update(
        weights, weights_m, weights_v, weights_ema, weight_grad, factor, MATRIX_RATE, MATRIX_DECAY
    )
    vectors_out = adam_update(vectors, vectors_m, vectors_v, vectors_ema, vector_grad, factor, VECTOR_RATE, 0.0)

    return (
        layer_rows,
        grad_rows,
        weight_grad,
        vector_grad,
        grad_norm,
        *weights_out,
        *vectors_out,
    )


def solution(mesh):
    rows, square, line = P("dp", None), P("dp", "heads"), P(None, "dp")
    placed = (rows,) * 5 + (square,) * 4 + (line,) * 4
    return jax.shard_map(
        local,
        mesh=mesh,
        in_specs=placed,
        out_specs=(rows, rows, square, line, P()) + (square,) * 4 + (line,) * 4,
        check_vma=False,
    )
```

time: 361 us -> 306 us (0.85)
  starting transfers between devices: 95.8 us -> 72.1 us
  Pallas kernels: 107 us -> 88.6 us
  waiting for transfers between devices: 104 us -> 121 us
  local copies, waits for them, and re-layouts: 22.7 us -> 6.36 us
  other arithmetic: 20.2 us -> 8.7 us
    ppermute x56 -> x36, starting transfers between devices: 80.6 us -> 54.6 us  [dp_swap(): return lax.ppermute(value, 'dp', [(i, i ^ mask) for i in range(count)])]
    ppermute x56 -> x36, waiting for transfers between devices: 56.2 us -> 75.2 us  [dp_swap(): return lax.ppermute(value, 'dp', [(i, i ^ mask) for i in range(count)])]
    pallas_call x38 -> x42, Pallas kernels: 107 us -> 88.6 us  [local_call(): pl.pallas_call(kernel, name=name, out_shape=list(outs), in_specs=[SMEM if...]
    unnamed x206 -> x70, local copies, waits for them, and re-layouts: 15.2 us -> 5.61 us
    ppermute x10 -> x8, waiting for transfers between devices: 38 us -> 28.6 us  [x_swap(): return lax.ppermute(value, 'heads', [(i, i ^ 2) for i in range(4)])]
    ppermute x0 -> x6, starting transfers between devices: none -> 8 us  [all_sum(): lax.ppermute(value, ('dp', 'heads'), [(i, i ^ mask) for i in range(count)])]
    ppermute x0 -> x6, waiting for transfers between devices: none -> 6.81 us  [all_sum(): lax.ppermute(value, ('dp', 'heads'), [(i, i ^ mask) for i in range(count)])]
    ppermute x10 -> x8, starting transfers between devices: 12.4 us -> 7.54 us  [x_swap(): return lax.ppermute(value, 'heads', [(i, i ^ 2) for i in range(4)])]
  transfers between devices with their start and end apart: 85 -> 67, of which waited for: 33 -> 33; matrix products, arithmetic and copies ran while one was open for 7% -> 3% of each run, Pallas kernels for 25% -> 24%
where the time goes in v1:
time: 306 us; the launch traced here: 302 us
  waiting for transfers between devices  121 us (40%)
  Pallas kernels  88.6 us (29%)
  starting transfers between devices  72.1 us (24%)
  other arithmetic  8.7 us (3%)
  local copies, waits for them, and re-layouts  6.36 us (2%)
  between operations  4.57 us (1%)
    pallas_call x42, Pallas kernels, local_call(): pl.pallas_call(kernel, name=name, out_shape=list(outs), in_specs=[SMEM if...  88.6 us
    ppermute x36, waiting for transfers between devices, dp_swap(): return lax.ppermute(value, 'dp', [(i, i ^ mask) for i in range(count)])  75.2 us
    ppermute x36, starting transfers between devices, dp_swap(): return lax.ppermute(value, 'dp', [(i, i ^ mask) for i in range(count)])  54.6 us
    ppermute x8, waiting for transfers between devices, x_swap(): return lax.ppermute(value, 'heads', [(i, i ^ 2) for i in range(4)])  28.6 us
    ppermute x17, waiting for transfers between devices, core_swap(): return lax.ppermute(value, 'heads', [(i, i ^ 1) for i in range(4)])  10.6 us
    ppermute x6, starting transfers between devices, all_sum(): lax.ppermute(value, ('dp', 'heads'), [(i, i ^ mask) for i in range(count)])  8 us
    ppermute x8, starting transfers between devices, x_swap(): return lax.ppermute(value, 'heads', [(i, i ^ 2) for i in range(4)])  7.54 us
    ppermute x6, waiting for transfers between devices, all_sum(): lax.ppermute(value, ('dp', 'heads'), [(i, i ^ mask) for i in range(count)])  6.81 us
  transfers between devices with their start and end apart: 67, of which 33 were waited for; matrix products, arithmetic and copies ran while one was open for 3% of the time, Pallas kernels for 24%

profile of v1, /device:TPU:0, one launch (start us, length us, event | category | flops | bytes accessed | tf_op | source)
XLA Modules:
  0.0 301.6 jit_solution(5319872360448811230)
XLA Ops:
  2.9 5.1 %collective-permute-start.2 = (bf16[96,1024]{1,0:T(8,128)(2,1)S(1)}, bf16[96,1024]{1,0:T(8,128)(2,1)S(1)}, u32[]{:S(2)}, u32[]{:S(2)}) collective-permute-start(bf16[96,1024]{1,0:T(8,128)(2,1)S(1)} %get-tuple-element.179.refs_0_), channel_id=1, source_target_pairs={{0,24},{4,28},{8,16},{12,20},{16,8},{20,12},{24,0},{28,4},{1,25},{... | collective-permute-start | bytes 589832 | tf_op jit(solution)/shard_map/ppermute | solution.py:52
  13.2 5.2 %sort_rows.1 = (bf16[1024,768]{1,0:T(8,128)(2,1)S(1)}, bf16[1024,1024]{1,0:T(8,128)(2,1)S(1)}, bf16[1024,1024]{1,0:T(8,128)(2,1)S(1)}, f32[1024,8]{1,0:T(8,128)S...) custom-call(s32[4]{0:T(128)S(1)} %pad_add_fusion.place_ref, ...), custom_call_target="tpu_custom_call" | custom-call | tf_op jit(solution)/shard_map/sort_rows/pallas_call | solution.py:104
  18.4 6.3 %collective-permute-done.1.refs_2_ = bf16[96,1024]{1,0:T(8,128)(2,1)S(1)} collective-permute-done((bf16[96,1024]{1,0:T(8,128)(2,1)S(1)}, bf16[96,1024]{1,0:T(8,128)(2,1)S(1)}, u32[]{:S(2)}, u32[]{:S(2)}) %collective-permute-start.1) | collective-permute-done | bytes 196640 | tf_op jit(solution)/shard_map/ppermute | solution.py:52
  28.3 4.3 %collective-permute-done.4.refs_5_ = bf16[96,1024]{1,0:T(8,128)(2,1)S(1)} collective-permute-done((bf16[96,1024]{1,0:T(8,128)(2,1)S(1)}, bf16[96,1024]{1,0:T(8,128)(2,1)S(1)}, u32[]{:S(2)}, u32[]{:S(2)}) %collective-permute-start.4) | collective-permute-done | bytes 196640 | tf_op jit(solution)/shard_map/ppermute | solution.py:52
  32.6 4.2 %collective-permute-done.5.refs_6_ = bf16[96,1024]{1,0:T(8,128)(2,1)S(1)} collective-permute-done((bf16[96,1024]{1,0:T(8,128)(2,1)S(1)}, bf16[96,1024]{1,0:T(8,128)(2,1)S(1)}, u32[]{:S(2)}, u32[]{:S(2)}) %collective-permute-start.5) | collective-permute-done | bytes 196640 | tf_op jit(solution)/shard_map/ppermute | solution.py:52
  45.8 7.0 %time_forward.1 = (f32[16,768]{1,0:T(8,128)S(1)}, bf16[1024,768]{1,0:T(8,128)(2,1)S(1)}, bf16[1024,576]{1,0:T(8,128)(2,1)S(1)}, bf16[512,192]{1,0:T(8,128)(2,1)S...) custom-call(bf16[768,640]{1,0:T(8,128)(2,1)S(1)} %bitcast.41, ...), custom_call_target="tpu_custom_call" | custom-call | tf_op jit(solution)/shard_map/time_forward/pallas_call | solution.py:104
  65.7 2.7 collective-permute-start.15
  68.4 9.2 %collective-permute-done.18.refs_4_ = bf16[4,96,768]{2,1,0:T(8,128)(2,1)S(1)} collective-permute-done((bf16[4,96,768]{2,1,0:T(8,128)(2,1)S(1)}, bf16[4,96,768]{2,1,0:T(8,128)(2,1)S(1)}, u32[]{:S(2)}, u32[]{:S(2)}) %collective-permute-start.18) | collective-permute-done | bytes 589856 | tf_op jit(solution)/shard_map/ppermute | solution.py:52
  78.3 3.1 %collective-permute-done.14.got_ref = bf16[512,768]{1,0:T(8,128)(2,1)S(1)} collective-permute-done((bf16[512,768]{1,0:T(8,128)(2,1)S(1)}, bf16[512,768]{1,0:T(8,128)(2,1)S(1)}, u32[]{:S(2)}, u32[]{:S(2)}) %collective-permute-start.14) | collective-permute-done | bytes 786464 | tf_op jit(solution)/shard_map/ppermute | solution.py:47
  87.4 2.7 collective-permute-start.21
  90.1 7.3 %space_forward.1 = (bf16[512,384]{1,0:T(8,128)(2,1)S(1)}, f32[8,512]{1,0:T(8,128)S(1)}, f32[16,8]{1,0:T(8,128)S(1)}, bf16[512,768]{1,0:T(8,128)(2,1)S(1)}) custom-call(s32[4]{0:T(128)S(1)} %pad_add_fusion.place_ref, bf16[512,384]{1,0:T(8,128)(2,1)S(1)} %get-tuple-element.219.q_ref, bf16[512,768]{1,0:T(8,128)(2,1)S(1)} %get-tuple-element.220.pairs_ref, ...), custom_call_target="tpu_custom_call" | custom-call | tf_op jit(solution)/shard_map/space_forward/pallas_call | solution.py:104
  102.8 12.7 %collective-permute-done.27.refs_4_ = bf16[4,96,768]{2,1,0:T(8,128)(2,1)S(1)} collective-permute-done((bf16[4,96,768]{2,1,0:T(8,128)(2,1)S(1)}, bf16[4,96,768]{2,1,0:T(8,128)(2,1)S(1)}, u32[]{:S(2)}, u32[]{:S(2)}) %collective-permute-start.27) | collective-permute-done | bytes 589856 | tf_op jit(solution)/shard_map/ppermute | solution.py:52
  116.2 3.1 %collective-permute-done.25.got_ref = bf16[512,768]{1,0:T(8,128)(2,1)S(1)} collective-permute-done((bf16[512,768]{1,0:T(8,128)(2,1)S(1)}, bf16[512,768]{1,0:T(8,128)(2,1)S(1)}, u32[]{:S(2)}, u32[]{:S(2)}) %collective-permute-start.25) | collective-permute-done | bytes 786464 | tf_op jit(solution)/shard_map/ppermute | solution.py:47
  120.1 4.8 %feed.1 = (bf16[512,1536]{1,0:T(8,128)(2,1)S(1)}, bf16[512,1536]{1,0:T(8,128)(2,1)S(1)}, bf16[512,768]{1,0:T(8,128)(2,1)S(1)}) custom-call(bf16[512,768]{1,0:T(8,128)(2,1)S(1)} %get-tuple-element.225.third_ref, bf16[512,768]{1,0:T(8,128)(2,1)S(1)} %get-tuple-element.226.dy_ref, bf16[768,768]{1,0:T(8,128)(2,1)S(1)} %bitcast.39, ...), custom_call_target="tpu_custom_call" | custom-call | tf_op jit(solution)/shard_map/feed/pallas_call | solution.py:104
  134.0 12.8 %collective-permute-done.31.got_ref = bf16[512,768]{1,0:T(8,128)(2,1)S(1)} collective-permute-done((bf16[512,768]{1,0:T(8,128)(2,1)S(1)}, bf16[512,768]{1,0:T(8,128)(2,1)S(1)}, u32[]{:S(2)}, u32[]{:S(2)}) %collective-permute-start.31) | collective-permute-done | bytes 786464 | tf_op jit(solution)/shard_map/ppermute | solution.py:47
  146.8 2.9 space_back_in.1
  149.8 8.6 %space_backward.1 = (bf16[512,384]{1,0:T(8,128)(2,1)S(1)}, f32[512,768]{1,0:T(8,128)S(1)}, bf16[512,768]{1,0:T(8,128)(2,1)S(1)}) custom-call(s32[4]{0:T(128)S(1)} %pad_add_fusion.place_ref, bf16[512,384]{1,0:T(8,128)(2,1)S(1)} %get-tuple-element.238.heads_ref, bf16[512,384]{1,0:T(8,128)(2,1)S(1)} %get-tuple-element.219.q_ref, ...), custom_call_target="tpu_custom_call" | custom-call | tf_op jit(solution)/shard_map/space_backward/pallas_call | solution.py:104
  158.4 4.9 %collective-permute-done.32.got_ref = bf16[512,768]{1,0:T(8,128)(2,1)S(1)} collective-permute-done((bf16[512,768]{1,0:T(8,128)(2,1)S(1)}, bf16[512,768]{1,0:T(8,128)(2,1)S(1)}, u32[]{:S(2)}, u32[]{:S(2)}) %collective-permute-start.32) | collective-permute-done | bytes 786464 | tf_op jit(solution)/shard_map/ppermute | solution.py:47
  171.2 5.3 %collective-permute-done.33.refs_5_ = bf16[96,768]{1,0:T(8,128)(2,1)S(1)} collective-permute-done((bf16[96,768]{1,0:T(8,128)(2,1)S(1)}, bf16[96,768]{1,0:T(8,128)(2,1)S(1)}, u32[]{:S(2)}, u32[]{:S(2)}) %collective-permute-start.33) | collective-permute-done | bytes 147488 | tf_op jit(solution)/shard_map/ppermute | solution.py:52
  181.6 6.7 %collective-permute-done.34.refs_6_ = bf16[96,768]{1,0:T(8,128)(2,1)S(1)} collective-permute-done((bf16[96,768]{1,0:T(8,128)(2,1)S(1)}, bf16[96,768]{1,0:T(8,128)(2,1)S(1)}, u32[]{:S(2)}, u32[]{:S(2)}) %collective-permute-start.34) | collective-permute-done | bytes 147488 | tf_op jit(solution)/shard_map/ppermute | solution.py:52
  198.1 3.2 %collective-permute-start.40 = (bf16[96,768]{1,0:T(8,128)(2,1)S(1)}, bf16[96,768]{1,0:T(8,128)(2,1)S(1)}, u32[]{:S(2)}, u32[]{:S(2)}) collective-permute-start(bf16[96,768]{1,0:T(8,128)(2,1)S(1)} %get-tuple-element.265), channel_id=1, source_target_pairs={{0,8},{4,12},{8,0},{12,4},{16,24},{20,28},{24,16},{28,20},{1,9},{5... | collective-permute-start | bytes 442376 | tf_op jit(solution)/shard_map/ppermute | solution.py:52
  203.8 6.3 %time_backward.1.grad_ref = bf16[1024,576]{1,0:T(8,128)(2,1)S(1)} custom-call(bf16[512,192]{1,0:T(8,128)(2,1)S(1)} %get-tuple-element.284.own_ref, bf16[512,192]{1,0:T(8,128)(2,1)S(1)} %collective-permute-done.46.far_ref, bf16[1024,1024]{1,0:T(8,128)(2,1)S(1)} %get-tuple-element.286.order_ref, bf16[1024,576]{1,0:T(8,128)(2,1)S(1)} %get-tuple-element.287.inputs_ref, ...), custom_call_target="tpu_custom_call" | custom-call | tf_op jit(solution)/shard_map/time_backward/pallas_call | solution.py:104
  210.2 5.2 %collective-permute-done.41.refs_10_ = bf16[96,768]{1,0:T(8,128)(2,1)S(1)} collective-permute-done((bf16[96,768]{1,0:T(8,128)(2,1)S(1)}, bf16[96,768]{1,0:T(8,128)(2,1)S(1)}, u32[]{:S(2)}, u32[]{:S(2)}) %collective-permute-start.41) | collective-permute-done | bytes 147488 | tf_op jit(solution)/shard_map/ppermute | solution.py:52
  219.3 2.7 collective-permute-start.49
  224.5 4.2 %time_back.1 = (bf16[512,768]{1,0:T(8,128)(2,1)S(1)}, bf16[512,768]{1,0:T(8,128)(2,1)S(1)}, f32[16,768]{1,0:T(8,128)S(1)}) custom-call(bf16[1024,576]{1,0:T(8,128)(2,1)S(1)} %time_backward.1.grad_ref, bf16[768,640]{1,0:T(8,128)(2,1)S(1)} %bitcast.42, bf16[1024,768]{1,0:T(8,128)(2,1)S(1)} %get-tuple-element.180.tokens_ref, ...), custom_call_target="tpu_custom_call" | custom-call | tf_op jit(solution)/shard_map/time_back/pallas_call | solution.py:104
  230.5 10.3 %collective-permute-done.50.refs_2_ = bf16[96,1152]{1,0:T(8,128)(2,1)S(1)} collective-permute-done((bf16[96,1152]{1,0:T(8,128)(2,1)S(1)}, bf16[96,1152]{1,0:T(8,128)(2,1)S(1)}, u32[]{:S(2)}, u32[]{:S(2)}) %collective-permute-start.50) | collective-permute-done | bytes 221216 | tf_op jit(solution)/shard_map/ppermute | solution.py:52
  250.7 3.5 %collective-permute-start.52 = (bf16[96,640]{1,0:T(8,128)(2,1)S(1)}, bf16[96,640]{1,0:T(8,128)(2,1)S(1)}, u32[]{:S(2)}, u32[]{:S(2)}) collective-permute-start(bf16[96,640]{1,0:T(8,128)(2,1)S(1)} %get-tuple-element.310), channel_id=1, source_target_pairs={{0,8},{4,12},{8,0},{12,4},{16,24},{20,28},{24,16},{28,20},{1,9},{5... | collective-permute-start | bytes 368648 | tf_op jit(solution)/shard_map/ppermute | solution.py:52
  256.7 3.0 %early_grad.1 = (f32[96,2304]{1,0:T(8,128)S(1)}, f32[1,768]{1,0:T(1,128)S(1)}) custom-call(f32[96,1152]{1,0:T(8,128)S(1)} %get-tuple-element.313.refs_0_, bf16[96,1152]{1,0:T(8,128)(2,1)S(1)} %collective-permute-done.49.refs_1_, bf16[96,1152]{1,0:T(8,128)(2,1)S(1)} %collective-permute-done.50.refs_2_, bf16[96,1152]{1,0:T(8,128)(2,1)S(1)} %copy-done.11, ...), custom_call_target="tpu_custom_call" | custom-call | tf_op jit(solution)/shard_map/early_grad/pallas_call | solution.py:104
  259.7 4.3 %collective-permute-done.56 = bf16[96,192]{1,0:T(8,128)(2,1)S(1)} collective-permute-done((bf16[96,192]{1,0:T(8,128)(2,1)S(1)}, bf16[96,192]{1,0:T(8,128)(2,1)S(1)}, u32[]{:S(2)}, u32[]{:S(2)}) %collective-permute-start.56) | collective-permute-done | bytes 36896 | tf_op jit(solution)/shard_map/ppermute | solution.py:47
  266.3 2.9 whole_grad.1
  291.1 5.6 %add_multiply_fusion = (f32[96,3264]{1,0:T(8,128)}, f32[96,3264]{1,0:T(8,128)}, f32[96,3264]{1,0:T(8,128)}, f32[96,3264]{1,0:T(8,128)}) fusion(f32[96,3264]{1,0:T(8,128)} %param.21, f32[96,3264]{1,0:T(8,128)S(1)} %copy-done.1, f32[96,3264]{1,0:T(8,128)} %get-tuple-element.167, f32[]{:T(128)S(6)} %div.39, f32[96,3264]{1,0:T(8,128)} %param.19, f32[96,3264]{1,0:T(8,128)} %param.20), kind=kLoop, calls=%fused_computation.4 | loop fusion | flops 5326848 | bytes 11280388 | tf_op jit(solution)/shard_map/add | solution.py:939
  296.6 3.3 %grad_rows.1 = f32[1024,768]{1,0:T(8,128)} custom-call(s32[4]{0:T(128)S(1)} %pad_add_fusion.place_ref, f32[512,768]{1,0:T(8,128)S(1)} %input_grad.1.own_ref, f32[512,768]{1,0:T(8,128)} %collective-permute-done.59.got_ref), custom_call_target="tpu_custom_call" | custom-call | tf_op jit(solution)/shard_map/grad_rows/pallas_call | solution.py:104
  (235 shorter events, 123.5 us)
Async XLA Ops:
  2.9 15.5 %collective-permute-start.2 = (bf16[96,1024]{1,0:T(8,128)(2,1)S(1)}, bf16[96,1024]{1,0:T(8,128)(2,1)S(1)}, u32[]{:S(2)}, u32[]{:S(2)}) collective-permute-start(bf16[96,1024]{1,0:T(8,128)(2,1)S(1)} %get-tuple-element.179.refs_0_), channel_id=1, source_target_pairs={{0,24},{4,28},{8,16},{12,20},{16,8},{20,12},{24,0},{28,4},{1,25},{... | collective-permute-start | bytes 589832 | tf_op jit(solution)/shard_map/ppermute | solution.py:52
  8.0 16.7 %collective-permute-start.1 = (bf16[96,1024]{1,0:T(8,128)(2,1)S(1)}, bf16[96,1024]{1,0:T(8,128)(2,1)S(1)}, u32[]{:S(2)}, u32[]{:S(2)}) collective-permute-start(bf16[96,1024]{1,0:T(8,128)(2,1)S(1)} %get-tuple-element.179.refs_0_), channel_id=1, source_target_pairs={{0,16},{4,20},{8,24},{12,28},{16,0},{20,4},{24,8},{28,12},{1,17},{... | collective-permute-start | bytes 589832 | tf_op jit(solution)/shard_map/ppermute | solution.py:52
  8.0 16.7 %collective-permute-start = (bf16[96,1024]{1,0:T(8,128)(2,1)S(1)}, bf16[96,1024]{1,0:T(8,128)(2,1)S(1)}, u32[]{:S(2)}, u32[]{:S(2)}) collective-permute-start(bf16[96,1024]{1,0:T(8,128)(2,1)S(1)} %get-tuple-element.179.refs_0_), channel_id=1, source_target_pairs={{0,8},{4,12},{8,0},{12,4},{16,24},{20,28},{24,16},{28,20},{1,9},{5... | collective-permute-start | bytes 589832 | tf_op jit(solution)/shard_map/ppermute | solution.py:52
  8.7 19.6 %collective-permute-start.3 = (bf16[96,1024]{1,0:T(8,128)(2,1)S(1)}, bf16[96,1024]{1,0:T(8,128)(2,1)S(1)}, u32[]{:S(2)}, u32[]{:S(2)}) collective-permute-start(bf16[96,1024]{1,0:T(8,128)(2,1)S(1)} %get-tuple-element.179.refs_0_), channel_id=1, source_target_pairs={{0,4},{4,0},{8,12},{12,8},{16,20},{20,16},{24,28},{28,24},{1,5},{5... | collective-permute-start | bytes 589832 | tf_op jit(solution)/shard_map/ppermute | solution.py:52
  39.9 14.9 %collective-permute-start.10 = (bf16[768,192]{1,0:T(8,128)(2,1)S(1)}, bf16[768,192]{1,0:T(8,128)(2,1)S(1)}, u32[]{:S(2)}, u32[]{:S(2)}) collective-permute-start(bf16[768,192]{1,0:T(8,128)(2,1)S(1)} %bitcast.46), channel_id=1, source_target_pairs={{0,2},{1,3},{2,0},{3,1},{4,6},{5,7},{6,4},{7,5},{8,10},{9,11},{10,... | collective-permute-start | bytes 884744 | tf_op jit(solution)/shard_map/ppermute | solution.py:47
  61.8 19.6 %collective-permute-start.14 = (bf16[512,768]{1,0:T(8,128)(2,1)S(1)}, bf16[512,768]{1,0:T(8,128)(2,1)S(1)}, u32[]{:S(2)}, u32[]{:S(2)}) collective-permute-start(bf16[512,768]{1,0:T(8,128)(2,1)S(1)} %time_out.1.part_ref), channel_id=1, source_target_pairs={{0,2},{1,3},{2,0},{3,1},{4,6},{5,7},{6,4},{7,5},{8,10},{9,11},{10,... | collective-permute-start | bytes 2359304 | tf_op jit(solution)/shard_map/ppermute | solution.py:47
  62.4 15.2 %collective-permute-start.18 = (bf16[4,96,768]{2,1,0:T(8,128)(2,1)S(1)}, bf16[4,96,768]{2,1,0:T(8,128)(2,1)S(1)}, u32[]{:S(2)}, u32[]{:S(2)}) collective-permute-start(bf16[4,96,768]{2,1,0:T(8,128)(2,1)S(1)} %pad_maximum_fusion.1), channel_id=1, source_target_pairs={{0,4},{4,0},{8,12},{12,8},{16,20},{20,16},{24,28},{28,24},{1,5},{5... | collective-permute-start | bytes 1769480 | tf_op jit(solution)/shard_map/ppermute | solution.py:52
  64.1 19.9 %collective-permute-start.17 = (bf16[96,768]{1,0:T(8,128)(2,1)S(1)}, bf16[96,768]{1,0:T(8,128)(2,1)S(1)}, u32[]{:S(2)}, u32[]{:S(2)}) collective-permute-start(bf16[96,768]{1,0:T(8,128)(2,1)S(1)} %get-tuple-element.213.refs_0_), channel_id=1, source_target_pairs={{0,24},{4,28},{8,16},{12,20},{16,8},{20,12},{24,0},{28,4},{1,25},{... | collective-permute-start | bytes 442376 | tf_op jit(solution)/shard_map/ppermute | solution.py:52
  65.7 18.2 %collective-permute-start.16 = (bf16[96,768]{1,0:T(8,128)(2,1)S(1)}, bf16[96,768]{1,0:T(8,128)(2,1)S(1)}, u32[]{:S(2)}, u32[]{:S(2)}) collective-permute-start(bf16[96,768]{1,0:T(8,128)(2,1)S(1)} %get-tuple-element.213.refs_0_), channel_id=1, source_target_pairs={{0,16},{4,20},{8,24},{12,28},{16,0},{20,4},{24,8},{28,12},{1,17},{... | collective-permute-start | bytes 442376 | tf_op jit(solution)/shard_map/ppermute | solution.py:52
  65.7 18.2 %collective-permute-start.15 = (bf16[96,768]{1,0:T(8,128)(2,1)S(1)}, bf16[96,768]{1,0:T(8,128)(2,1)S(1)}, u32[]{:S(2)}, u32[]{:S(2)}) collective-permute-start(bf16[96,768]{1,0:T(8,128)(2,1)S(1)} %get-tuple-element.213.refs_0_), channel_id=1, source_target_pairs={{0,8},{4,12},{8,0},{12,4},{16,24},{20,28},{24,16},{28,20},{1,9},{5... | collective-permute-start | bytes 442376 | tf_op jit(solution)/shard_map/ppermute | solution.py:52
  84.1 15.8 %collective-permute-start.20 = (bf16[4,96,768]{2,1,0:T(8,128)(2,1)S(1)}, bf16[4,96,768]{2,1,0:T(8,128)(2,1)S(1)}, u32[]{:S(2)}, u32[]{:S(2)}) collective-permute-start(bf16[4,96,768]{2,1,0:T(8,128)(2,1)S(1)} %pad_maximum_fusion.2), channel_id=1, source_target_pairs={{0,4},{4,0},{8,12},{12,8},{16,20},{20,16},{24,28},{28,24},{1,5},{5... | collective-permute-start | bytes 1769480 | tf_op jit(solution)/shard_map/ppermute | solution.py:52
  87.4 12.5 %collective-permute-start.22 = (bf16[96,768]{1,0:T(8,128)(2,1)S(1)}, bf16[96,768]{1,0:T(8,128)(2,1)S(1)}, u32[]{:S(2)}, u32[]{:S(2)}) collective-permute-start(bf16[96,768]{1,0:T(8,128)(2,1)S(1)} %get-tuple-element.228.refs_0_), channel_id=1, source_target_pairs={{0,16},{4,20},{8,24},{12,28},{16,0},{20,4},{24,8},{28,12},{1,17},{... | collective-permute-start | bytes 442376 | tf_op jit(solution)/shard_map/ppermute | solution.py:52
  87.4 12.5 %collective-permute-start.21 = (bf16[96,768]{1,0:T(8,128)(2,1)S(1)}, bf16[96,768]{1,0:T(8,128)(2,1)S(1)}, u32[]{:S(2)}, u32[]{:S(2)}) collective-permute-start(bf16[96,768]{1,0:T(8,128)(2,1)S(1)} %get-tuple-element.228.refs_0_), channel_id=1, source_target_pairs={{0,8},{4,12},{8,0},{12,4},{16,24},{20,28},{24,16},{28,20},{1,9},{5... | collective-permute-start | bytes 442376 | tf_op jit(solution)/shard_map/ppermute | solution.py:52
  99.9 19.4 %collective-permute-start.25 = (bf16[512,768]{1,0:T(8,128)(2,1)S(1)}, bf16[512,768]{1,0:T(8,128)(2,1)S(1)}, u32[]{:S(2)}, u32[]{:S(2)}) collective-permute-start(bf16[512,768]{1,0:T(8,128)(2,1)S(1)} %get-tuple-element.224.part_ref), channel_id=1, source_target_pairs={{0,2},{1,3},{2,0},{3,1},{4,6},{5,7},{6,4},{7,5},{8,10},{9,11},{10,... | collective-permute-start | bytes 2359304 | tf_op jit(solution)/shard_map/ppermute | solution.py:47
  100.5 15.0 %collective-permute-start.27 = (bf16[4,96,768]{2,1,0:T(8,128)(2,1)S(1)}, bf16[4,96,768]{2,1,0:T(8,128)(2,1)S(1)}, u32[]{:S(2)}, u32[]{:S(2)}) collective-permute-start(bf16[4,96,768]{2,1,0:T(8,128)(2,1)S(1)} %pad_maximum_fusion.3), channel_id=1, source_target_pairs={{0,4},{4,0},{8,12},{12,8},{16,20},{20,16},{24,28},{28,24},{1,5},{5... | collective-permute-start | bytes 1769480 | tf_op jit(solution)/shard_map/ppermute | solution.py:52
  102.8 17.3 %collective-permute-start.26 = (bf16[768,768]{1,0:T(8,128)(2,1)S(1)}, bf16[768,768]{1,0:T(8,128)(2,1)S(1)}, u32[]{:S(2)}, u32[]{:S(2)}) collective-permute-start(bf16[768,768]{1,0:T(8,128)(2,1)S(1)} %bitcast.38), channel_id=1, source_target_pairs={{0,1},{1,0},{2,3},{3,2},{4,5},{5,4},{6,7},{7,6},{8,9},{9,8},{10,11... | collective-permute-start | bytes 3538952 | tf_op jit(solution)/shard_map/ppermute | solution.py:43
  126.4 20.4 %collective-permute-start.31 = (bf16[512,768]{1,0:T(8,128)(2,1)S(1)}, bf16[512,768]{1,0:T(8,128)(2,1)S(1)}, u32[]{:S(2)}, u32[]{:S(2)}) collective-permute-start(bf16[512,768]{1,0:T(8,128)(2,1)S(1)} %get-tuple-element.236.part_ref), channel_id=1, source_target_pairs={{0,2},{1,3},{2,0},{3,1},{4,6},{5,7},{6,4},{7,5},{8,10},{9,11},{10,... | collective-permute-start | bytes 2359304 | tf_op jit(solution)/shard_map/ppermute | solution.py:47
  128.7 34.6 %collective-permute-start.32 = (bf16[512,768]{1,0:T(8,128)(2,1)S(1)}, bf16[512,768]{1,0:T(8,128)(2,1)S(1)}, u32[]{:S(2)}, u32[]{:S(2)}) collective-permute-start(bf16[512,768]{1,0:T(8,128)(2,1)S(1)} %feed_out.1.part_ref), channel_id=1, source_target_pairs={{0,2},{1,3},{2,0},{3,1},{4,6},{5,7},{6,4},{7,5},{8,10},{9,11},{10,... | collective-permute-start | bytes 2359304 | tf_op jit(solution)/shard_map/ppermute | solution.py:47
  132.7 30.6 %collective-permute-start.30 = (bf16[4,96,768]{2,1,0:T(8,128)(2,1)S(1)}, bf16[4,96,768]{2,1,0:T(8,128)(2,1)S(1)}, u32[]{:S(2)}, u32[]{:S(2)}) collective-permute-start(bf16[4,96,768]{2,1,0:T(8,128)(2,1)S(1)} %get-tuple-element.235), channel_id=1, source_target_pairs={{0,4},{4,0},{8,12},{12,8},{16,20},{20,16},{24,28},{28,24},{1,5},{5... | collective-permute-start | bytes 1769480 | tf_op jit(solution)/shard_map/ppermute | solution.py:52
  168.7 24.0 %collective-permute-start.43 = (bf16[768,768]{1,0:T(8,128)(2,1)S(1)}, bf16[768,768]{1,0:T(8,128)(2,1)S(1)}, u32[]{:S(2)}, u32[]{:S(2)}) collective-permute-start(bf16[768,768]{1,0:T(8,128)(2,1)S(1)} %space_grads_far.1), channel_id=1, source_target_pairs={{0,1},{1,0},{2,3},{3,2},{4,5},{5,4},{6,7},{7,6},{8,9},{9,8},{10,11... | collective-permute-start | bytes 3538952 | tf_op jit(solution)/shard_map/ppermute | solution.py:43
  169.2 19.6 %collective-permute-start.37 = (bf16[512,768]{1,0:T(8,128)(2,1)S(1)}, bf16[512,768]{1,0:T(8,128)(2,1)S(1)}, u32[]{:S(2)}, u32[]{:S(2)}) collective-permute-start(bf16[512,768]{1,0:T(8,128)(2,1)S(1)} %get-tuple-element.250.part_ref), channel_id=1, source_target_pairs={{0,2},{1,3},{2,0},{3,1},{4,6},{5,7},{6,4},{7,5},{8,10},{9,11},{10,... | collective-permute-start | bytes 2359304 | tf_op jit(solution)/shard_map/ppermute | solution.py:47
  169.7 21.2 %collective-permute-start.39 = (bf16[4,96,768]{2,1,0:T(8,128)(2,1)S(1)}, bf16[4,96,768]{2,1,0:T(8,128)(2,1)S(1)}, u32[]{:S(2)}, u32[]{:S(2)}) collective-permute-start(bf16[4,96,768]{2,1,0:T(8,128)(2,1)S(1)} %get-tuple-element.257), channel_id=1, source_target_pairs={{0,4},{4,0},{8,12},{12,8},{16,20},{20,16},{24,28},{28,24},{1,5},{5... | collective-permute-start | bytes 1769480 | tf_op jit(solution)/shard_map/ppermute | solution.py:52
  193.6 21.8 %collective-permute-start.44 = (bf16[4,96,768]{2,1,0:T(8,128)(2,1)S(1)}, bf16[4,96,768]{2,1,0:T(8,128)(2,1)S(1)}, u32[]{:S(2)}, u32[]{:S(2)}) collective-permute-start(bf16[4,96,768]{2,1,0:T(8,128)(2,1)S(1)} %get-tuple-element.272), channel_id=1, source_target_pairs={{0,4},{4,0},{8,12},{12,8},{16,20},{20,16},{24,28},{28,24},{1,5},{5... | collective-permute-start | bytes 1769480 | tf_op jit(solution)/shard_map/ppermute | solution.py:52
  197.1 18.5 %collective-permute-start.47 = (bf16[4,96,384]{2,1,0:T(8,128)(2,1)S(1)}, bf16[4,96,384]{2,1,0:T(8,128)(2,1)S(1)}, u32[]{:S(2)}, u32[]{:S(2)}) collective-permute-start(bf16[4,96,384]{2,1,0:T(8,128)(2,1)S(1)} %get-tuple-element.283), channel_id=1, source_target_pairs={{0,4},{4,0},{8,12},{12,8},{16,20},{20,16},{24,28},{28,24},{1,5},{5... | collective-permute-start | bytes 884744 | tf_op jit(solution)/shard_map/ppermute | solution.py:52
  201.4 14.0 %collective-permute-start.41 = (bf16[96,768]{1,0:T(8,128)(2,1)S(1)}, bf16[96,768]{1,0:T(8,128)(2,1)S(1)}, u32[]{:S(2)}, u32[]{:S(2)}) collective-permute-start(bf16[96,768]{1,0:T(8,128)(2,1)S(1)} %get-tuple-element.266), channel_id=1, source_target_pairs={{0,16},{4,20},{8,24},{12,28},{16,0},{20,4},{24,8},{28,12},{1,17},{... | collective-permute-start | bytes 442376 | tf_op jit(solution)/shard_map/ppermute | solution.py:52
  201.6 13.7 %collective-permute-start.42 = (bf16[96,768]{1,0:T(8,128)(2,1)S(1)}, bf16[96,768]{1,0:T(8,128)(2,1)S(1)}, u32[]{:S(2)}, u32[]{:S(2)}) collective-permute-start(bf16[96,768]{1,0:T(8,128)(2,1)S(1)} %get-tuple-element.267), channel_id=1, source_target_pairs={{0,24},{4,28},{8,16},{12,20},{16,8},{20,12},{24,0},{28,4},{1,25},{... | collective-permute-start | bytes 442376 | tf_op jit(solution)/shard_map/ppermute | solution.py:52
  217.8 23.0 %collective-permute-start.48 = (bf16[4,96,640]{2,1,0:T(8,128)(2,1)S(1)}, bf16[4,96,640]{2,1,0:T(8,128)(2,1)S(1)}, u32[]{:S(2)}, u32[]{:S(2)}) collective-permute-start(bf16[4,96,640]{2,1,0:T(8,128)(2,1)S(1)} %get-tuple-element.295), channel_id=1, source_target_pairs={{0,4},{4,0},{8,12},{12,8},{16,20},{20,16},{24,28},{28,24},{1,5},{5... | collective-permute-start | bytes 1474568 | tf_op jit(solution)/shard_map/ppermute | solution.py:52
  222.0 18.7 %collective-permute-start.50 = (bf16[96,1152]{1,0:T(8,128)(2,1)S(1)}, bf16[96,1152]{1,0:T(8,128)(2,1)S(1)}, u32[]{:S(2)}, u32[]{:S(2)}) collective-permute-start(bf16[96,1152]{1,0:T(8,128)(2,1)S(1)} %get-tuple-element.302), channel_id=1, source_target_pairs={{0,16},{4,20},{8,24},{12,28},{16,0},{20,4},{24,8},{28,12},{1,17},{... | collective-permute-start | bytes 663560 | tf_op jit(solution)/shard_map/ppermute | solution.py:52
  222.5 18.3 %collective-permute-start.51 = (bf16[96,1152]{1,0:T(8,128)(2,1)S(1)}, bf16[96,1152]{1,0:T(8,128)(2,1)S(1)}, u32[]{:S(2)}, u32[]{:S(2)}) collective-permute-start(bf16[96,1152]{1,0:T(8,128)(2,1)S(1)} %get-tuple-element.303), channel_id=1, source_target_pairs={{0,24},{4,28},{8,16},{12,20},{16,8},{20,12},{24,0},{28,4},{1,25},{... | collective-permute-start | bytes 663560 | tf_op jit(solution)/shard_map/ppermute | solution.py:52
  243.4 25.8 %collective-permute-start.58 = (bf16[512,768]{1,0:T(8,128)(2,1)S(1)}, bf16[512,768]{1,0:T(8,128)(2,1)}, u32[]{:S(2)}, u32[]{:S(2)}) collective-permute-start(bf16[512,768]{1,0:T(8,128)(2,1)S(1)} %add_convert_fusion.part_ref), channel_id=1, source_target_pairs={{0,2},{1,3},{2,0},{3,1},{4,6},{5,7},{6,4},{7,5},{8,10},{9,11},{10,... | collective-permute-start | bytes 2359304 | tf_op jit(solution)/shard_map/ppermute | solution.py:47
  249.9 14.2 %collective-permute-start.56 = (bf16[96,192]{1,0:T(8,128)(2,1)S(1)}, bf16[96,192]{1,0:T(8,128)(2,1)S(1)}, u32[]{:S(2)}, u32[]{:S(2)}) collective-permute-start(bf16[96,192]{1,0:T(8,128)(2,1)S(1)} %slice.57), channel_id=1, source_target_pairs={{0,2},{1,3},{2,0},{3,1},{4,6},{5,7},{6,4},{7,5},{8,10},{9,11},{10,... | collective-permute-start | bytes 110600 | tf_op jit(solution)/shard_map/ppermute | solution.py:47
  250.7 13.4 %collective-permute-start.52 = (bf16[96,640]{1,0:T(8,128)(2,1)S(1)}, bf16[96,640]{1,0:T(8,128)(2,1)S(1)}, u32[]{:S(2)}, u32[]{:S(2)}) collective-permute-start(bf16[96,640]{1,0:T(8,128)(2,1)S(1)} %get-tuple-element.310), channel_id=1, source_target_pairs={{0,8},{4,12},{8,0},{12,4},{16,24},{20,28},{24,16},{28,20},{1,9},{5... | collective-permute-start | bytes 368648 | tf_op jit(solution)/shard_map/ppermute | solution.py:52
  (70 other events, 600.3 us)

commit v2 on v1

--- a/solution.py
+++ b/solution.py
@@ -52,18 +52,25 @@
     return lax.ppermute(value, "dp", [(i, i ^ mask) for i in range(count)])
 
 
-def all_sum(value):
+def all_sum(value, early, late):
     count = lax.axis_size("dp") * lax.axis_size("heads")
     value = value + core_swap(value)
-    step = 2
+    step, made = 2, None
     while step < count:
         masks = [step, 2 * step, 3 * step] if 2 * step < count else [step]
         got = [lax.ppermute(value, ("dp", "heads"), [(i, i ^ mask) for i in range(count)]) for mask in masks]
+        step *= 4
+        if made is None:
+            made = early(value)
+            got, made = together(got, made)
+        if step >= count:
+            break
         value = value + got[0]
         if len(got) > 1:
             value = value + (got[1] + got[2])
-        step *= 4
-    return value
+    made = late(value, *made)
+    got, made = together(got, made)
+    return [value, *got], made
 
 
 def after(value, *others):
@@ -186,7 +193,7 @@
 
 def places():
     dp, heads = lax.axis_index("dp"), lax.axis_index("heads")
-    return jnp.stack([dp // 2, dp % 2, heads, heads % 2]).astype(jnp.int32)
+    return jnp.stack([dp // 2, dp % 2, heads, heads % 2, dp]).astype(jnp.int32)
 
 
 def split_rows(name, totals, cuts=()):
@@ -864,11 +871,17 @@
     out_ref[...] = stream_ref[...] + (part_ref[...].astype(F32) + got_ref[...].astype(F32)) + vec_ref[9:10]
 
 
-def whole_rows_kernel(place_ref, own_ref, got_ref, out_ref):
+def whole_rows_kernel(place_ref, own_ref, got_ref, out_ref, sem):
     core = place_ref[3]
     rows = own_ref.shape[0]
-    out_ref[pl.ds(pl.multiple_of(core * rows, rows), rows), :] = own_ref[...]
-    out_ref[pl.ds(pl.multiple_of((1 - core) * rows, rows), rows), :] = got_ref[...]
+    copies = [
+        pltpu.make_async_copy(ref, out_ref.at[pl.ds(pl.multiple_of(at * rows, rows), rows)], sem.at[i])
+        for i, (ref, at) in enumerate(((own_ref, core), (got_ref, 1 - core)))
+    ]
+    for copy in copies:
+        copy.start()
+    for copy in copies:
+        copy.wait()
 
 
 def fused_grads_kernel(low_ref, heads_ref, got_heads_ref, own_ref, far_ref):
@@ -892,10 +905,13 @@
         bias_ref[:, j * width : (j + 1) * width] = dot(sums_ref[...].astype(BF16), block)
 
 
-def mix_shard_kernel(place_ref, fused_ref, out_ref, keep_ref, send_ref):
+def mix_shard_kernel(place_ref, out_ref, *refs):
+    ins, (grad_ref, keep_ref, send_ref) = refs[:-3], refs[-3:]
     place = place_ref[2]
     width = out_ref.shape[1]
-    fused = fused_ref[...].astype(BF16)
+    total = sum(ref[:, : 2 * width].astype(F32) for ref in ins)
+    grad_ref[...] = total[:, :width]
+    fused = total[:, width:].astype(BF16)
     for m in range(4):
         rows = out_ref[pl.ds(pl.multiple_of((place ^ m) * width, width), width), :]
         part = dot_nt(fused, rows)
@@ -903,30 +919,76 @@
         ref[:, m // 2 * width : (m // 2 + 1) * width] = part.astype(ref.dtype)
 
 
-def early_grad_kernel(groups, *refs):
-    out_ref, square_ref = refs[-2:]
-    count, column, square = (len(refs) - 2) // len(groups), 0, 0.0
-    for i, (start, stop) in enumerate(groups):
-        value = sum(ref[:, start:stop].astype(F32) for ref in refs[i * count : (i + 1) * count])
-        out_ref[:, column : column + value.shape[1]] = value
-        column += value.shape[1]
-        square = square + jnp.sum(value * value)
-    square_ref[...] = jnp.full(square_ref.shape, square, F32)
-
-
-def whole_grad_kernel(early_ref, square_ref, vector_ref, bias_ref, out_ref, mix_ref, *refs):
-    grad_ref, sums_ref = refs[-2:]
-    width = mix_ref.shape[1]
-    total = sum(ref[...].astype(F32) for ref in refs[:-2])
-    row_sum = total[:, 3 * width : 3 * width + 1]
-    mix = mix_ref[...] + row_sum * bias_ref[...]
-    grad_ref[:, 5 * width :] = early_ref[...]
-    square = square_ref[...]
-    for i, value in ((0, total[:, : 3 * width]), (3, out_ref[:, :width]), (4, mix)):
-        grad_ref[:, i * width : i * width + value.shape[1]] = value
-        square = square + jnp.sum(value * value)
-    sums_ref[...] = vector_ref[...]
-    sums_ref[VECTORS : VECTORS + 1] = square
+def mix_sum_kernel(keep_ref, got_ref, own_ref, send_ref):
+    width = own_ref.shape[1]
+    total = keep_ref[...] + got_ref[...].astype(F32)
+    own_ref[...] = total[:, :width]
+    send_ref[...] = total[:, width:].astype(BF16)
+
+
+def add_kernel(own_ref, got_ref, out_ref):
+    out_ref[...] = (own_ref[...].astype(F32) + got_ref[...].astype(F32)).astype(BF16)
+
+
+def whole_grad_kernel(head_ref, early_ref, grad_ref):
+    columns = head_ref.shape[1]
+    grad_ref[:, :columns] = head_ref[...]
+    grad_ref[:, columns:] = early_ref[...]
+
+
+def update_kernel(terms, shards, steps, place_ref, *refs):
+    sums, refs = refs[:terms], refs[terms:]
+    grad_ref, *matrix = refs[:5]
+    vectors, refs = refs[5:9], refs[9:]
+    new, (vector_grad_ref, norm_ref, *vectors_new) = refs[:4], refs[4:10]
+    held_in, held_out, sem_in, sem_out = refs[10:14], refs[14:18], refs[18], refs[19]
+    count = grad_ref.shape[0] // steps
+    cuts = [pl.ds(i * count, count) for i in range(steps)]
+    loads = [
+        [pltpu.make_async_copy(a.at[cut], b.at[cut], sem_in.at[i, j]) for j, (a, b) in enumerate(zip(matrix, held_in))]
+        for i, cut in enumerate(cuts)
+    ]
+    stores = [
+        [
+            pltpu.make_async_copy(a.at[cut], b.at[cut], sem_out.at[i, j])
+            for j, (a, b) in enumerate(zip(held_out, new))
+        ]
+        for i, cut in enumerate(cuts)
+    ]
+    for step in loads:
+        for copy in step:
+            copy.start()
+    total = sums[0][...]
+    if terms > 1:
+        total = total + sums[1][...]
+    if terms > 2:
+        total = total + (sums[2][...] + sums[3][...])
+    rows = total[:VECTORS]
+    norm = jnp.sqrt(total[VECTORS : VECTORS + 1, 0:1] + jnp.sum(rows * rows))
+    norm_ref[...] = norm
+    limit = 0.5 * math.sqrt(NPARAM)
+    factor = limit / jnp.maximum(norm, limit)
+    for i, cut in enumerate(cuts):
+        for copy in loads[i]:
+            copy.wait()
+        states = [ref[cut, :] for ref in held_in]
+        updated = adam_update(*states, grad_ref[cut, :], factor, MATRIX_RATE, MATRIX_DECAY)
+        for ref, value in zip(held_out, updated):
+            ref[cut, :] = value
+        for copy in stores[i]:
+            copy.start()
+    width = vector_grad_ref.shape[1]
+    vector_grad = 0.0
+    for j in range(shards):
+        part = rows[:, j * width : (j + 1) * width]
+        vector_grad = vector_grad + jnp.where(place_ref[4] == j, part, 0.0)
+    vector_grad_ref[...] = vector_grad
+    updated = adam_update(*[ref[...] for ref in vectors], vector_grad, factor, VECTOR_RATE, 0.0)
+    for ref, value in zip(vectors_new, updated):
+        ref[...] = value
+    for step in stores:
+        for copy in step:
+            copy.wait()
 
 
 def adam_update(master, first_moment, second_moment, average, gradient, factor, rate, decay):
@@ -993,9 +1055,12 @@
         smem=(0,),
         scratch=[pltpu.VMEM((count, features), BF16)],
     )
-    head_z, _ = together(head_z, [tokens_sorted])
-    head_z[0] = head_piece
-    head_y = y_blocks(head_z, True)
+    head_y = [dp_swap(head_piece, 1)]
+    before = tokens_sorted
+    for k in range(1, half):
+        head_z[k] = after(head_z[k], before)
+        before = head_z[k]
+        head_y.append(dp_swap(head_z[k], 1))
     space_z = z_blocks(after(space_piece, *head_z))
     (head_y,) = together(head_y)
     time_maps, mix_map, out_map = assemble(
@@ -1098,7 +1163,7 @@
         "split_feed", [(feed_grad_own, core_swap(feed_grad_far))], (hidden,)
     )
     up_y = [dp_swap(up_send, 1)]
-    feed_part_got = x_swap(feed_part)
+    third_got, feed_part = lax.optimization_barrier((third_got, feed_part))
 
     grad_two, grad_two_low, sums_two, space_grad_heads = local_call(
         "space_back_in",
@@ -1120,7 +1185,7 @@
             pltpu.VMEM((CLASSES, 2 * width), BF16),
         ],
     )
-    up_y, (space_send, feed_part_got) = together(up_y, [space_send, feed_part_got])
+    up_y, (space_send,) = together(up_y, [space_send])
     up_shards = z_swaps(y_sums("sum_up", [(up_keep, up_y)]))
     space_got_grads = core_swap(space_send)
     down_y = [dp_swap(after(down_send, *up_y), 1)]
@@ -1141,19 +1206,21 @@
         for name, group, grad in (("space_grads_far", 1, grad_space_far), ("space_grads_own", 0, grad_space))
     ]
 
-    def whole(name, value):
-        (out,) = local_call(
-            name, whole_rows_kernel, [shaped((count, features), F32)], place, value, core_swap(value), smem=(0,)
-        )
-        return out
-
-    (layer_half,) = local_call(
-        "layer_out", layer_out_kernel, [wide(features, F32)], stream_two, feed_part, feed_part_got, vec
-    )
-    layer_rows = whole("layer_rows", after(layer_half, space_got_grads))
-    up_shards, (second_got, layer_rows) = together(up_shards, [second_got, layer_rows])
+    def whole(name, value, got):
+        return pl.pallas_call(
+            whole_rows_kernel,
+            name=name,
+            out_shape=shaped((count, features), F32),
+            in_specs=[SMEM, VMEM, VMEM],
+            out_specs=ANY,
+            scratch_shapes=[pltpu.SemaphoreType.DMA((2,))],
+            compiler_params=pltpu.CompilerParams(vmem_limit_bytes=2**21),
+            cost_estimate=pl.CostEstimate(flops=0, bytes_accessed=0, transcendentals=0),
+        )(place, value, got)
+
     ((space_y_send, space_keep),) = split_rows("split_space", [(space_grad_own, core_swap(space_grad_far))])
     space_y = [dp_swap(space_y_send, 1)]
+    up_shards, (second_got, space_y_send) = together(up_shards, [second_got, space_y_send])
     grad_one, grad_one_low, sums_one, time_grad_own, time_grad_send = local_call(
         "time_back_in",
         time_back_in_kernel,
@@ -1220,63 +1287,89 @@
         grad_time, time_maps, tokens_sorted, back, bias_grad, sums_one, sums_two,
         scratch=[pltpu.VMEM((count, features), BF16)],
     )
-    time_y, late_shards, (first_send,) = together(time_y, late_shards, [first_send])
-    first_part = (first_own.astype(F32) + core_swap(first_send).astype(F32)).astype(BF16)
-    first_part_got = x_swap(first_part)
-    time_shards = y_sums("sum_time", [(time_keep, time_y)])
-    time_shards = z_swaps(time_shards)
+    feed_part_got = x_swap(after(feed_part, time_send))
+    time_y, late_shards, (first_send, feed_part_got) = together(time_y, late_shards, [first_send, feed_part_got])
+    first_got = core_swap(first_send)
 
     out_width = 2 * width
-    out_total = sum([one[:, :out_width].astype(F32) for one in late_shards])
-    mix_keep, mix_send = local_call(
+    out_grad, mix_keep, mix_send = local_call(
         "mix_shard",
         mix_shard_kernel,
-        [shaped((shard, out_width), F32), shaped((shard, out_width), BF16)],
-        place, out_total[:, width:], out_map,
+        [shaped((shard, width), F32), shaped((shard, out_width), F32), shaped((shard, out_width), BF16)],
+        place, out_map, *late_shards,
         smem=(0,),
     )
-    mix_sum = mix_keep + core_swap(mix_send).astype(F32)
-    mix_total = mix_sum[:, :width] + x_swap(mix_sum[:, width:].astype(BF16)).astype(F32)
-
-    (grad_half,) = local_call(
-        "input_grad", input_grad_kernel, [wide(features, F32)], first_part, first_part_got, tokens_own, vec, grad_one
-    )
+    (first_part,) = local_call("first_part", add_kernel, [wide(features, BF16)], first_own, first_got)
+    mix_own, mix_send = local_call(
+        "mix_sum",
+        mix_sum_kernel,
+        [shaped((shard, width), F32), shaped((shard, width), BF16)],
+        mix_keep, core_swap(mix_send),
+    )
+    mix_got = x_swap(mix_send)
+    first_part = after(first_part, mix_send)
+    first_part_got = x_swap(first_part)
+    (layer_half,) = local_call(
+        "layer_out", layer_out_kernel, [wide(features, F32)], stream_two, feed_part, feed_part_got, vec
+    )
+    layer_got = core_swap(after(layer_half, first_got))
+    time_shards = y_sums("sum_time", [(time_keep, time_y)])
+    time_shards, (mix_got, layer_got) = together(time_shards, [mix_got, layer_got])
+    time_shards = z_swaps(time_shards)
+    layer_rows = whole("layer_rows", layer_half, layer_got)
+
     bias_part = lax.dynamic_slice_in_dim(vec[2:3], lax.axis_index("heads") * width, width, 1)
     late = [out_width, out_width + 4 * width]
-    early_grad, early_square = local_call(
-        "early_grad",
-        partial(early_grad_kernel, (late, [0, hidden], [0, hidden])),
-        [shaped((shard, 4 * width + 2 * hidden), F32), shaped((1, features), F32)],
-        *late_shards, *up_shards, *down_shards,
-        staged=True,
-    )
-    time_shards, (mix_total, early_grad) = together(time_shards, [mix_total, early_grad])
-    weight_grad, sums = local_call(
-        "whole_grad",
-        whole_grad_kernel,
-        [shaped(weights.shape, F32), shaped((16, features), F32)],
-        early_grad, early_square, vector_sum, bias_part, out_total, mix_total, *time_shards,
-        staged=True,
-    )
-    sums, grad_half = lax.optimization_barrier((sums, grad_half))
-    grad_rows = whole("grad_rows", grad_half)
-    sums = all_sum(sums)
-    vector_all = sums[:VECTORS]
-    vector_grad = lax.dynamic_slice_in_dim(vector_all, lax.axis_index("dp") * shard, shard, 1)
-    grad_norm = jnp.sqrt(sums[VECTORS, 0] + jnp.sum(vector_all * vector_all))
-    limit = 0.5 * math.sqrt(NPARAM)
-    factor = limit / jnp.maximum(grad_norm, limit)
-    weights_out = adam_update(
-        weights, weights_m, weights_v, weights_ema, weight_grad, factor, MATRIX_RATE, MATRIX_DECAY
-    )
-    vectors_out = adam_update(vectors, vectors_m, vectors_v, vectors_ema, vector_grad, factor, VECTOR_RATE, 0.0)
-
+    total = lambda shards: sum([one.astype(F32) for one in shards])
+    up_shards, down_shards, _ = together(up_shards, down_shards, [first_part])
+    early_grad = jnp.concatenate([total(late_shards)[:, out_width:], total(up_shards), total(down_shards)], 1)
+    early_square = jnp.sum(early_grad * early_grad)
+    time_shards, (early_grad, early_square, layer_rows) = together(time_shards, [early_grad, early_square, layer_rows])
+    time_total = total(time_shards)
+    mix_grad = mix_own + mix_got.astype(F32) + time_total[:, 3 * width : 3 * width + 1] * bias_part
+    head_grad = jnp.concatenate([time_total[:, : 3 * width], out_grad, mix_grad], 1)
+    square = early_square + jnp.sum(head_grad * head_grad)
+    row = lax.broadcasted_iota(jnp.int32, vector_sum.shape, 0)
+    sums = jnp.where(row == VECTORS, square, vector_sum)
+
+    def input_half(ready):
+        return local_call(
+            "input_grad",
+            input_grad_kernel,
+            [wide(features, F32)],
+            first_part, after(first_part_got, ready), tokens_own, vec, grad_one,
+        )
+
+    def last_results(ready, grad_half):
+        grad_rows = whole("grad_rows", grad_half, core_swap(grad_half))
+        (weight_grad,) = local_call(
+            "whole_grad", whole_grad_kernel, [shaped(weights.shape, F32)], after(head_grad, ready), early_grad
+        )
+        return [grad_rows, weight_grad]
+
+    terms, (grad_rows, weight_grad) = all_sum(sums, input_half, last_results)
+    steps = max(one for one in (1, 2, 3, 4) if shard % (8 * one) == 0)
+    states = [weights, weights_m, weights_v, weights_ema]
+    vector_states = [vectors, vectors_m, vectors_v, vectors_ema]
+    outs = pl.pallas_call(
+        partial(update_kernel, len(terms), lax.axis_size("dp"), steps),
+        name="update",
+        out_shape=[shaped(weights.shape, F32)] * 4
+        + [shaped(vectors.shape, F32), shaped((1, 1), F32)]
+        + [shaped(vectors.shape, F32)] * 4,
+        in_specs=[SMEM] + [VMEM] * (len(terms) + 1) + [ANY] * 4 + [VMEM] * 4,
+        out_specs=[ANY] * 4 + [VMEM] * 6,
+        scratch_shapes=[pltpu.VMEM(weights.shape, F32)] * 8
+        + [pltpu.SemaphoreType.DMA((steps, 4)), pltpu.SemaphoreType.DMA((steps, 4))],
+        compiler_params=pltpu.CompilerParams(vmem_limit_bytes=14 * 2**20),
+    )(place, *terms, weight_grad, *states, *vector_states)
+    weights_out, (vector_grad, grad_norm, *vectors_out) = outs[:4], outs[4:]
     return (
         layer_rows,
         grad_rows,
         weight_grad,
         vector_grad,
-        grad_norm,
+        grad_norm[0, 0],
         *weights_out,
         *vectors_out,
     )

time: 306 us -> 289 us (0.944)
  waiting for transfers between devices: 121 us -> 104 us
  local copies, waits for them, and re-layouts: 6.36 us -> 14.1 us
  other arithmetic: 8.7 us -> 2.55 us
    pallas_call x0 -> x3, Pallas kernels: none -> 11.3 us  [the longest x1 6.01 us: local(): pl.pallas_call(partial(update_kernel, len(terms), lax.axis_size('dp'), st...]
    pallas_call x42 -> x41, Pallas kernels: 88.6 us -> 77.6 us  [local_call(): pl.pallas_call(kernel, name=name, out_shape=list(outs), in_specs=[SMEM if...]
    unnamed x70 -> x104, local copies, waits for them, and re-layouts: 5.61 us -> 13.8 us
    add x5 -> x4, other arithmetic: 7.31 us -> 0.39 us  [the longest x3 0.29 us: local(): total = lambda shards: sum([one.astype(F32) for one in shards])]
    ppermute x8, waiting for transfers between devices: 28.6 us -> 22.2 us  [x_swap(): return lax.ppermute(value, 'heads', [(i, i ^ 2) for i in range(4)])]
    ppermute x6, waiting for transfers between devices: 6.81 us -> 0.58 us  [all_sum(): lax.ppermute(value, ('dp', 'heads'), [(i, i ^ mask) for i in range(count)])]
    ppermute x36, waiting for transfers between devices: 75.2 us -> 70 us  [dp_swap(): return lax.ppermute(value, 'dp', [(i, i ^ mask) for i in range(count)])]
  transfers between devices with their start and end apart: 67 -> 67, of which waited for: 33 -> 28; matrix products, arithmetic and copies ran while one was open for 3% -> 1% of each run, Pallas kernels for 24% -> 24%
where the time goes in v2:
time: 289 us; the launch traced here: 284 us
  waiting for transfers between devices  104 us (36%)
  Pallas kernels  88.9 us (31%)
  starting transfers between devices  70.9 us (25%)
  local copies, waits for them, and re-layouts  14.1 us (5%)
  between operations  3.14 us (1%)
    pallas_call x41, Pallas kernels, local_call(): pl.pallas_call(kernel, name=name, out_shape=list(outs), in_specs=[SMEM if...  77.6 us
    ppermute x36, waiting for transfers between devices, dp_swap(): return lax.ppermute(value, 'dp', [(i, i ^ mask) for i in range(count)])  70 us
    ppermute x36, starting transfers between devices, dp_swap(): return lax.ppermute(value, 'dp', [(i, i ^ mask) for i in range(count)])  54.1 us
    ppermute x8, waiting for transfers between devices, x_swap(): return lax.ppermute(value, 'heads', [(i, i ^ 2) for i in range(4)])  22.2 us
    unnamed x104, local copies, waits for them, and re-layouts  13.8 us
    ppermute x17, waiting for transfers between devices, core_swap(): return lax.ppermute(value, 'heads', [(i, i ^ 1) for i in range(4)])  11.6 us
    ppermute x6, starting transfers between devices, all_sum(): lax.ppermute(value, ('dp', 'heads'), [(i, i ^ mask) for i in range(count)])  7.95 us
    ppermute x8, starting transfers between devices, x_swap(): return lax.ppermute(value, 'heads', [(i, i ^ 2) for i in range(4)])  6.61 us
  transfers between devices with their start and end apart: 67, of which 28 were waited for; matrix products, arithmetic and copies ran while one was open for 1% of the time, Pallas kernels for 24%

profile of v2, /device:TPU:0, one launch (start us, length us, event | category | flops | bytes accessed | tf_op | source)
XLA Modules:
  0.0 284.0 jit_solution(10182247892131645813)
XLA Ops:
  2.9 3.1 %collective-permute-start = (bf16[96,1024]{1,0:T(8,128)(2,1)S(1)}, bf16[96,1024]{1,0:T(8,128)(2,1)S(1)}, u32[]{:S(2)}, u32[]{:S(2)}) collective-permute-start(bf16[96,1024]{1,0:T(8,128)(2,1)S(1)} %get-tuple-element.214.refs_0_), channel_id=1, source_target_pairs={{0,8},{4,12},{8,0},{12,4},{16,24},{20,28},{24,16},{28,20},{1,9},{5... | collective-permute-start | bytes 589832 | tf_op jit(solution)/shard_map/ppermute | solution.py:52
  6.0 2.6 collective-permute-start.1
  13.2 5.2 %sort_rows.1 = (bf16[1024,768]{1,0:T(8,128)(2,1)S(1)}, bf16[1024,1024]{1,0:T(8,128)(2,1)S(1)}, bf16[1024,1024]{1,0:T(8,128)(2,1)S(1)}, f32[1024,8]{1,0:T(8,128)S...) custom-call(s32[5]{0:T(128)S(1)} %stack.47.place_ref, ...), custom_call_target="tpu_custom_call" | custom-call | tf_op jit(solution)/shard_map/sort_rows/pallas_call | solution.py:111
  18.4 4.7 %collective-permute-done.1.refs_2_ = bf16[96,1024]{1,0:T(8,128)(2,1)S(1)} collective-permute-done((bf16[96,1024]{1,0:T(8,128)(2,1)S(1)}, bf16[96,1024]{1,0:T(8,128)(2,1)S(1)}, u32[]{:S(2)}, u32[]{:S(2)}) %collective-permute-start.1) | collective-permute-done | bytes 196640 | tf_op jit(solution)/shard_map/ppermute | solution.py:52
  26.7 4.3 %collective-permute-done.6.refs_7_ = bf16[96,1024]{1,0:T(8,128)(2,1)S(1)} collective-permute-done((bf16[96,1024]{1,0:T(8,128)(2,1)S(1)}, bf16[96,1024]{1,0:T(8,128)(2,1)S(1)}, u32[]{:S(2)}, u32[]{:S(2)}) %collective-permute-start.6) | collective-permute-done | bytes 196640 | tf_op jit(solution)/shard_map/ppermute | solution.py:52
  31.0 2.7 collective-permute-done.5.refs_6_
  39.5 4.8 %collective-permute-start.8 = (bf16[96,768]{1,0:T(8,128)(2,1)S(1)}, bf16[96,768]{1,0:T(8,128)(2,1)S(1)}, u32[]{:S(2)}, u32[]{:S(2)}) collective-permute-start(bf16[96,768]{1,0:T(8,128)(2,1)S(1)} %get-tuple-element.242.refs_0_), channel_id=1, source_target_pairs={{0,16},{4,20},{8,24},{12,28},{16,0},{20,4},{24,8},{28,12},{1,17},{... | collective-permute-start | bytes 442376 | tf_op jit(solution)/shard_map/ppermute | solution.py:52
  44.4 7.0 %time_forward.1 = (f32[16,768]{1,0:T(8,128)S(1)}, bf16[1024,768]{1,0:T(8,128)(2,1)S(1)}, bf16[1024,576]{1,0:T(8,128)(2,1)S(1)}, bf16[512,192]{1,0:T(8,128)(2,1)S...) custom-call(bf16[768,640]{1,0:T(8,128)(2,1)S(1)} %bitcast.44, ...), custom_call_target="tpu_custom_call" | custom-call | tf_op jit(solution)/shard_map/time_forward/pallas_call | solution.py:111
  66.9 9.2 %collective-permute-done.18.refs_4_ = bf16[4,96,768]{2,1,0:T(8,128)(2,1)S(1)} collective-permute-done((bf16[4,96,768]{2,1,0:T(8,128)(2,1)S(1)}, bf16[4,96,768]{2,1,0:T(8,128)(2,1)S(1)}, u32[]{:S(2)}, u32[]{:S(2)}) %collective-permute-start.18) | collective-permute-done | bytes 589856 | tf_op jit(solution)/shard_map/ppermute | solution.py:52
  76.8 3.1 %collective-permute-done.14.got_ref = bf16[512,768]{1,0:T(8,128)(2,1)S(1)} collective-permute-done((bf16[512,768]{1,0:T(8,128)(2,1)S(1)}, bf16[512,768]{1,0:T(8,128)(2,1)S(1)}, u32[]{:S(2)}, u32[]{:S(2)}) %collective-permute-start.14) | collective-permute-done | bytes 786464 | tf_op jit(solution)/shard_map/ppermute | solution.py:47
  88.6 7.3 %space_forward.1 = (bf16[512,384]{1,0:T(8,128)(2,1)S(1)}, f32[8,512]{1,0:T(8,128)S(1)}, f32[16,8]{1,0:T(8,128)S(1)}, bf16[512,768]{1,0:T(8,128)(2,1)S(1)}) custom-call(s32[5]{0:T(128)S(1)} %stack.47.place_ref, bf16[512,384]{1,0:T(8,128)(2,1)S(1)} %get-tuple-element.256.q_ref, bf16[512,768]{1,0:T(8,128)(2,1)S(1)} %get-tuple-element.257.pairs_ref, ...), custom_call_target="tpu_custom_call" | custom-call | tf_op jit(solution)/shard_map/space_forward/pallas_call | solution.py:111
  95.9 3.1 %collective-permute-done.22.refs_2_ = bf16[96,768]{1,0:T(8,128)(2,1)S(1)} collective-permute-done((bf16[96,768]{1,0:T(8,128)(2,1)S(1)}, bf16[96,768]{1,0:T(8,128)(2,1)S(1)}, u32[]{:S(2)}, u32[]{:S(2)}) %collective-permute-start.22) | collective-permute-done | bytes 147488 | tf_op jit(solution)/shard_map/ppermute | solution.py:52
  101.3 12.9 %collective-permute-done.27.refs_4_ = bf16[4,96,768]{2,1,0:T(8,128)(2,1)S(1)} collective-permute-done((bf16[4,96,768]{2,1,0:T(8,128)(2,1)S(1)}, bf16[4,96,768]{2,1,0:T(8,128)(2,1)S(1)}, u32[]{:S(2)}, u32[]{:S(2)}) %collective-permute-start.27) | collective-permute-done | bytes 589856 | tf_op jit(solution)/shard_map/ppermute | solution.py:52
  114.9 3.1 %collective-permute-done.25.got_ref = bf16[512,768]{1,0:T(8,128)(2,1)S(1)} collective-permute-done((bf16[512,768]{1,0:T(8,128)(2,1)S(1)}, bf16[512,768]{1,0:T(8,128)(2,1)S(1)}, u32[]{:S(2)}, u32[]{:S(2)}) %collective-permute-start.25) | collective-permute-done | bytes 786464 | tf_op jit(solution)/shard_map/ppermute | solution.py:47
  118.8 4.7 %feed.1 = (bf16[512,1536]{1,0:T(8,128)(2,1)S(1)}, bf16[512,1536]{1,0:T(8,128)(2,1)S(1)}, bf16[512,768]{1,0:T(8,128)(2,1)S(1)}) custom-call(bf16[512,768]{1,0:T(8,128)(2,1)S(1)} %get-tuple-element.262.third_ref, bf16[512,768]{1,0:T(8,128)(2,1)S(1)} %get-tuple-element.263.dy_ref, bf16[768,768]{1,0:T(8,128)(2,1)S(1)} %bitcast.42, ...), custom_call_target="tpu_custom_call" | custom-call | tf_op jit(solution)/shard_map/feed/pallas_call | solution.py:111
  133.4 11.6 %collective-permute-done.31.got_ref = bf16[512,768]{1,0:T(8,128)(2,1)S(1)} collective-permute-done((bf16[512,768]{1,0:T(8,128)(2,1)S(1)}, bf16[512,768]{1,0:T(8,128)(2,1)S(1)}, u32[]{:S(2)}, u32[]{:S(2)}) %collective-permute-start.31) | collective-permute-done | bytes 786464 | tf_op jit(solution)/shard_map/ppermute | solution.py:47
  145.0 2.9 %space_back_in.1 = (f32[512,768]{1,0:T(8,128)S(1)}, bf16[512,768]{1,0:T(8,128)(2,1)S(1)}, f32[8,768]{1,0:T(8,128)S(1)}, bf16[512,384]{1,0:T(8,128)(2,1)S(1)}) custom-call(bf16[512,768]{1,0:T(8,128)(2,1)S(1)} %get-tuple-element.274.part_ref, bf16[512,768]{1,0:T(8,128)(2,1)S(1)} %collective-permute-done.31.got_ref, ...), custom_call_target="tpu_custom_call" | custom-call | tf_op jit(solution)/shard_map/space_back_in/pallas_call | solution.py:111
  147.9 8.6 %space_backward.1 = (bf16[512,384]{1,0:T(8,128)(2,1)S(1)}, f32[512,768]{1,0:T(8,128)S(1)}, bf16[512,768]{1,0:T(8,128)(2,1)S(1)}) custom-call(s32[5]{0:T(128)S(1)} %stack.47.place_ref, bf16[512,384]{1,0:T(8,128)(2,1)S(1)} %get-tuple-element.277.heads_ref, bf16[512,384]{1,0:T(8,128)(2,1)S(1)} %get-tuple-element.256.q_ref, ...), custom_call_target="tpu_custom_call" | custom-call | tf_op jit(solution)/shard_map/space_backward/pallas_call | solution.py:111
  163.9 3.0 %collective-permute-start.35 = (bf16[96,768]{1,0:T(8,128)(2,1)S(1)}, bf16[96,768]{1,0:T(8,128)(2,1)S(1)}, u32[]{:S(2)}, u32[]{:S(2)}) collective-permute-start(bf16[96,768]{1,0:T(8,128)(2,1)S(1)} %get-tuple-element.290), channel_id=1, source_target_pairs={{0,16},{4,20},{8,24},{12,28},{16,0},{20,4},{24,8},{28,12},{1,17},{... | collective-permute-start | bytes 442376 | tf_op jit(solution)/shard_map/ppermute | solution.py:52
  171.9 6.0 %collective-permute-done.35 = bf16[96,768]{1,0:T(8,128)(2,1)S(1)} collective-permute-done((bf16[96,768]{1,0:T(8,128)(2,1)S(1)}, bf16[96,768]{1,0:T(8,128)(2,1)S(1)}, u32[]{:S(2)}, u32[]{:S(2)}) %collective-permute-start.35) | collective-permute-done | bytes 147488 | tf_op jit(solution)/shard_map/ppermute | solution.py:52
  178.0 3.9 %collective-permute-done.37.got_ref = bf16[512,768]{1,0:T(8,128)(2,1)S(1)} collective-permute-done((bf16[512,768]{1,0:T(8,128)(2,1)S(1)}, bf16[512,768]{1,0:T(8,128)(2,1)S(1)}, u32[]{:S(2)}, u32[]{:S(2)}) %collective-permute-start.37) | collective-permute-done | bytes 786464 | tf_op jit(solution)/shard_map/ppermute | solution.py:47
  189.9 3.0 %collective-permute-start.40 = (bf16[96,768]{1,0:T(8,128)(2,1)S(1)}, bf16[96,768]{1,0:T(8,128)(2,1)S(1)}, u32[]{:S(2)}, u32[]{:S(2)}) collective-permute-start(bf16[96,768]{1,0:T(8,128)(2,1)S(1)} %get-tuple-element.305), channel_id=1, source_target_pairs={{0,16},{4,20},{8,24},{12,28},{16,0},{20,4},{24,8},{28,12},{1,17},{... | collective-permute-start | bytes 442376 | tf_op jit(solution)/shard_map/ppermute | solution.py:52
  194.3 6.3 %time_backward.1.grad_ref = bf16[1024,576]{1,0:T(8,128)(2,1)S(1)} custom-call(bf16[512,192]{1,0:T(8,128)(2,1)S(1)} %get-tuple-element.318.own_ref, bf16[512,192]{1,0:T(8,128)(2,1)S(1)} %collective-permute-done.44.far_ref, bf16[1024,1024]{1,0:T(8,128)(2,1)S(1)} %get-tuple-element.320.order_ref, bf16[1024,576]{1,0:T(8,128)(2,1)S(1)} %get-tuple-element.321.inputs_ref, ...), custom_call_target="tpu_custom_call" | custom-call | tf_op jit(solution)/shard_map/time_backward/pallas_call | solution.py:111
  200.7 3.3 %collective-permute-done.40 = bf16[96,768]{1,0:T(8,128)(2,1)S(1)} collective-permute-done((bf16[96,768]{1,0:T(8,128)(2,1)S(1)}, bf16[96,768]{1,0:T(8,128)(2,1)S(1)}, u32[]{:S(2)}, u32[]{:S(2)}) %collective-permute-start.40) | collective-permute-done | bytes 147488 | tf_op jit(solution)/shard_map/ppermute | solution.py:52
  204.0 2.9 %collective-permute-done.45.refs_1_ = bf16[4,96,384]{2,1,0:T(8,128)(2,1)S(1)} collective-permute-done((bf16[4,96,384]{2,1,0:T(8,128)(2,1)S(1)}, bf16[4,96,384]{2,1,0:T(8,128)(2,1)S(1)}, u32[]{:S(2)}, u32[]{:S(2)}) %collective-permute-start.45) | collective-permute-done | bytes 294944 | tf_op jit(solution)/shard_map/ppermute | solution.py:52
  211.0 3.0 %collective-permute-start.48 = (bf16[96,1152]{1,0:T(8,128)(2,1)S(1)}, bf16[96,1152]{1,0:T(8,128)(2,1)S(1)}, u32[]{:S(2)}, u32[]{:S(2)}) collective-permute-start(bf16[96,1152]{1,0:T(8,128)(2,1)S(1)} %get-tuple-element.336), channel_id=1, source_target_pairs={{0,16},{4,20},{8,24},{12,28},{16,0},{20,4},{24,8},{28,12},{1,17},{... | collective-permute-start | bytes 663560 | tf_op jit(solution)/shard_map/ppermute | solution.py:52
  215.4 4.2 %time_back.1 = (bf16[512,768]{1,0:T(8,128)(2,1)S(1)}, bf16[512,768]{1,0:T(8,128)(2,1)S(1)}, f32[16,768]{1,0:T(8,128)S(1)}) custom-call(bf16[1024,576]{1,0:T(8,128)(2,1)S(1)} %time_backward.1.grad_ref, bf16[768,640]{1,0:T(8,128)(2,1)S(1)} %bitcast.45, bf16[1024,768]{1,0:T(8,128)(2,1)S(1)} %get-tuple-element.215.tokens_ref, ...), custom_call_target="tpu_custom_call" | custom-call | tf_op jit(solution)/shard_map/time_back/pallas_call | solution.py:111
  221.1 8.7 %collective-permute-done.48.refs_2_ = bf16[96,1152]{1,0:T(8,128)(2,1)S(1)} collective-permute-done((bf16[96,1152]{1,0:T(8,128)(2,1)S(1)}, bf16[96,1152]{1,0:T(8,128)(2,1)S(1)}, u32[]{:S(2)}, u32[]{:S(2)}) %collective-permute-start.48) | collective-permute-done | bytes 221216 | tf_op jit(solution)/shard_map/ppermute | solution.py:52
  242.8 2.7 collective-permute-start.55
  248.8 3.1 %layer_rows.1 = f32[1024,768]{1,0:T(8,128)} custom-call(s32[5]{0:T(128)S(1)} %stack.47.place_ref, f32[512,768]{1,0:T(8,128)S(1)} %layer_out.1.own_ref, f32[512,768]{1,0:T(8,128)} %collective-permute-done.54.got_ref), custom_call_target="tpu_custom_call" | custom-call | tf_op jit(solution)/shard_map/layer_rows/pallas_call | solution.py:1210
  251.9 5.3 %collective-permute-done.56 = bf16[96,640]{1,0:T(8,128)(2,1)S(1)} collective-permute-done((bf16[96,640]{1,0:T(8,128)(2,1)S(1)}, bf16[96,640]{1,0:T(8,128)(2,1)S(1)}, u32[]{:S(2)}, u32[]{:S(2)}) %collective-permute-start.56) | collective-permute-done | bytes 122912 | tf_op jit(solution)/shard_map/ppermute | solution.py:52
  277.7 6.0 %update.1 = (f32[96,3264]{1,0:T(8,128)}, f32[96,3264]{1,0:T(8,128)}, f32[96,3264]{1,0:T(8,128)}, f32[96,3264]{1,0:T(8,128)}, f32[10,96]{1,0:T(8,128)}, /*index=5...) custom-call(s32[5]{0:T(128)S(1)} %stack.47.place_ref, ...), custom_call_target="tpu_custom_call" | custom-call | tf_op jit(solution)/shard_map/update/pallas_call | solution.py:1354
  (269 shorter events, 118.3 us)
Async XLA Ops:
  2.9 15.5 %collective-permute-start = (bf16[96,1024]{1,0:T(8,128)(2,1)S(1)}, bf16[96,1024]{1,0:T(8,128)(2,1)S(1)}, u32[]{:S(2)}, u32[]{:S(2)}) collective-permute-start(bf16[96,1024]{1,0:T(8,128)(2,1)S(1)} %get-tuple-element.214.refs_0_), channel_id=1, source_target_pairs={{0,8},{4,12},{8,0},{12,4},{16,24},{20,28},{24,16},{28,20},{1,9},{5... | collective-permute-start | bytes 589832 | tf_op jit(solution)/shard_map/ppermute | solution.py:52
  6.0 17.2 %collective-permute-start.1 = (bf16[96,1024]{1,0:T(8,128)(2,1)S(1)}, bf16[96,1024]{1,0:T(8,128)(2,1)S(1)}, u32[]{:S(2)}, u32[]{:S(2)}) collective-permute-start(bf16[96,1024]{1,0:T(8,128)(2,1)S(1)} %get-tuple-element.214.refs_0_), channel_id=1, source_target_pairs={{0,16},{4,20},{8,24},{12,28},{16,0},{20,4},{24,8},{28,12},{1,17},{... | collective-permute-start | bytes 589832 | tf_op jit(solution)/shard_map/ppermute | solution.py:52
  8.6 14.6 %collective-permute-start.2 = (bf16[96,1024]{1,0:T(8,128)(2,1)S(1)}, bf16[96,1024]{1,0:T(8,128)(2,1)S(1)}, u32[]{:S(2)}, u32[]{:S(2)}) collective-permute-start(bf16[96,1024]{1,0:T(8,128)(2,1)S(1)} %get-tuple-element.214.refs_0_), channel_id=1, source_target_pairs={{0,24},{4,28},{8,16},{12,20},{16,8},{20,12},{24,0},{28,4},{1,25},{... | collective-permute-start | bytes 589832 | tf_op jit(solution)/shard_map/ppermute | solution.py:52
  8.6 18.1 %collective-permute-start.3 = (bf16[96,1024]{1,0:T(8,128)(2,1)S(1)}, bf16[96,1024]{1,0:T(8,128)(2,1)S(1)}, u32[]{:S(2)}, u32[]{:S(2)}) collective-permute-start(bf16[96,1024]{1,0:T(8,128)(2,1)S(1)} %get-tuple-element.214.refs_0_), channel_id=1, source_target_pairs={{0,4},{4,0},{8,12},{12,8},{16,20},{20,16},{24,28},{28,24},{1,5},{5... | collective-permute-start | bytes 589832 | tf_op jit(solution)/shard_map/ppermute | solution.py:52
  36.5 16.8 %collective-permute-start.10 = (bf16[768,192]{1,0:T(8,128)(2,1)S(1)}, bf16[768,192]{1,0:T(8,128)(2,1)S(1)}, u32[]{:S(2)}, u32[]{:S(2)}) collective-permute-start(bf16[768,192]{1,0:T(8,128)(2,1)S(1)} %bitcast.49), channel_id=1, source_target_pairs={{0,2},{1,3},{2,0},{3,1},{4,6},{5,7},{6,4},{7,5},{8,10},{9,11},{10,... | collective-permute-start | bytes 884744 | tf_op jit(solution)/shard_map/ppermute | solution.py:47
  38.1 13.2 %collective-permute-start.9 = (bf16[96,768]{1,0:T(8,128)(2,1)S(1)}, bf16[96,768]{1,0:T(8,128)(2,1)S(1)}, u32[]{:S(2)}, u32[]{:S(2)}) collective-permute-start(bf16[96,768]{1,0:T(8,128)(2,1)S(1)} %get-tuple-element.242.refs_0_), channel_id=1, source_target_pairs={{0,24},{4,28},{8,16},{12,20},{16,8},{20,12},{24,0},{28,4},{1,25},{... | collective-permute-start | bytes 442376 | tf_op jit(solution)/shard_map/ppermute | solution.py:52
  39.5 13.9 %collective-permute-start.8 = (bf16[96,768]{1,0:T(8,128)(2,1)S(1)}, bf16[96,768]{1,0:T(8,128)(2,1)S(1)}, u32[]{:S(2)}, u32[]{:S(2)}) collective-permute-start(bf16[96,768]{1,0:T(8,128)(2,1)S(1)} %get-tuple-element.242.refs_0_), channel_id=1, source_target_pairs={{0,16},{4,20},{8,24},{12,28},{16,0},{20,4},{24,8},{28,12},{1,17},{... | collective-permute-start | bytes 442376 | tf_op jit(solution)/shard_map/ppermute | solution.py:52
  60.3 19.6 %collective-permute-start.14 = (bf16[512,768]{1,0:T(8,128)(2,1)S(1)}, bf16[512,768]{1,0:T(8,128)(2,1)S(1)}, u32[]{:S(2)}, u32[]{:S(2)}) collective-permute-start(bf16[512,768]{1,0:T(8,128)(2,1)S(1)} %time_out.1.part_ref), channel_id=1, source_target_pairs={{0,2},{1,3},{2,0},{3,1},{4,6},{5,7},{6,4},{7,5},{8,10},{9,11},{10,... | collective-permute-start | bytes 2359304 | tf_op jit(solution)/shard_map/ppermute | solution.py:47
  61.0 15.2 %collective-permute-start.18 = (bf16[4,96,768]{2,1,0:T(8,128)(2,1)S(1)}, bf16[4,96,768]{2,1,0:T(8,128)(2,1)S(1)}, u32[]{:S(2)}, u32[]{:S(2)}) collective-permute-start(bf16[4,96,768]{2,1,0:T(8,128)(2,1)S(1)} %pad_maximum_fusion.2), channel_id=1, source_target_pairs={{0,4},{4,0},{8,12},{12,8},{16,20},{20,16},{24,28},{28,24},{1,5},{5... | collective-permute-start | bytes 1769480 | tf_op jit(solution)/shard_map/ppermute | solution.py:52
  62.6 19.9 %collective-permute-start.17 = (bf16[96,768]{1,0:T(8,128)(2,1)S(1)}, bf16[96,768]{1,0:T(8,128)(2,1)S(1)}, u32[]{:S(2)}, u32[]{:S(2)}) collective-permute-start(bf16[96,768]{1,0:T(8,128)(2,1)S(1)} %get-tuple-element.250.refs_0_), channel_id=1, source_target_pairs={{0,24},{4,28},{8,16},{12,20},{16,8},{20,12},{24,0},{28,4},{1,25},{... | collective-permute-start | bytes 442376 | tf_op jit(solution)/shard_map/ppermute | solution.py:52
  65.0 17.4 %collective-permute-start.16 = (bf16[96,768]{1,0:T(8,128)(2,1)S(1)}, bf16[96,768]{1,0:T(8,128)(2,1)S(1)}, u32[]{:S(2)}, u32[]{:S(2)}) collective-permute-start(bf16[96,768]{1,0:T(8,128)(2,1)S(1)} %get-tuple-element.250.refs_0_), channel_id=1, source_target_pairs={{0,16},{4,20},{8,24},{12,28},{16,0},{20,4},{24,8},{28,12},{1,17},{... | collective-permute-start | bytes 442376 | tf_op jit(solution)/shard_map/ppermute | solution.py:52
  65.0 17.4 %collective-permute-start.15 = (bf16[96,768]{1,0:T(8,128)(2,1)S(1)}, bf16[96,768]{1,0:T(8,128)(2,1)S(1)}, u32[]{:S(2)}, u32[]{:S(2)}) collective-permute-start(bf16[96,768]{1,0:T(8,128)(2,1)S(1)} %get-tuple-element.250.refs_0_), channel_id=1, source_target_pairs={{0,8},{4,12},{8,0},{12,4},{16,24},{20,28},{24,16},{28,20},{1,9},{5... | collective-permute-start | bytes 442376 | tf_op jit(solution)/shard_map/ppermute | solution.py:52
  82.6 16.4 %collective-permute-start.20 = (bf16[4,96,768]{2,1,0:T(8,128)(2,1)S(1)}, bf16[4,96,768]{2,1,0:T(8,128)(2,1)S(1)}, u32[]{:S(2)}, u32[]{:S(2)}) collective-permute-start(bf16[4,96,768]{2,1,0:T(8,128)(2,1)S(1)} %pad_maximum_fusion.3), channel_id=1, source_target_pairs={{0,4},{4,0},{8,12},{12,8},{16,20},{20,16},{24,28},{28,24},{1,5},{5... | collective-permute-start | bytes 1769480 | tf_op jit(solution)/shard_map/ppermute | solution.py:52
  86.7 12.4 %collective-permute-start.22 = (bf16[96,768]{1,0:T(8,128)(2,1)S(1)}, bf16[96,768]{1,0:T(8,128)(2,1)S(1)}, u32[]{:S(2)}, u32[]{:S(2)}) collective-permute-start(bf16[96,768]{1,0:T(8,128)(2,1)S(1)} %get-tuple-element.265.refs_0_), channel_id=1, source_target_pairs={{0,16},{4,20},{8,24},{12,28},{16,0},{20,4},{24,8},{28,12},{1,17},{... | collective-permute-start | bytes 442376 | tf_op jit(solution)/shard_map/ppermute | solution.py:52
  86.7 12.4 %collective-permute-start.21 = (bf16[96,768]{1,0:T(8,128)(2,1)S(1)}, bf16[96,768]{1,0:T(8,128)(2,1)S(1)}, u32[]{:S(2)}, u32[]{:S(2)}) collective-permute-start(bf16[96,768]{1,0:T(8,128)(2,1)S(1)} %get-tuple-element.265.refs_0_), channel_id=1, source_target_pairs={{0,8},{4,12},{8,0},{12,4},{16,24},{20,28},{24,16},{28,20},{1,9},{5... | collective-permute-start | bytes 442376 | tf_op jit(solution)/shard_map/ppermute | solution.py:52
  99.1 19.0 %collective-permute-start.25 = (bf16[512,768]{1,0:T(8,128)(2,1)S(1)}, bf16[512,768]{1,0:T(8,128)(2,1)S(1)}, u32[]{:S(2)}, u32[]{:S(2)}) collective-permute-start(bf16[512,768]{1,0:T(8,128)(2,1)S(1)} %get-tuple-element.261.part_ref), channel_id=1, source_target_pairs={{0,2},{1,3},{2,0},{3,1},{4,6},{5,7},{6,4},{7,5},{8,10},{9,11},{10,... | collective-permute-start | bytes 2359304 | tf_op jit(solution)/shard_map/ppermute | solution.py:47
  99.7 14.6 %collective-permute-start.27 = (bf16[4,96,768]{2,1,0:T(8,128)(2,1)S(1)}, bf16[4,96,768]{2,1,0:T(8,128)(2,1)S(1)}, u32[]{:S(2)}, u32[]{:S(2)}) collective-permute-start(bf16[4,96,768]{2,1,0:T(8,128)(2,1)S(1)} %pad_maximum_fusion.4), channel_id=1, source_target_pairs={{0,4},{4,0},{8,12},{12,8},{16,20},{20,16},{24,28},{28,24},{1,5},{5... | collective-permute-start | bytes 1769480 | tf_op jit(solution)/shard_map/ppermute | solution.py:52
  101.3 17.5 %collective-permute-start.26 = (bf16[768,768]{1,0:T(8,128)(2,1)S(1)}, bf16[768,768]{1,0:T(8,128)(2,1)S(1)}, u32[]{:S(2)}, u32[]{:S(2)}) collective-permute-start(bf16[768,768]{1,0:T(8,128)(2,1)S(1)} %bitcast.41), channel_id=1, source_target_pairs={{0,1},{1,0},{2,3},{3,2},{4,5},{5,4},{6,7},{7,6},{8,9},{9,8},{10,11... | collective-permute-start | bytes 3538952 | tf_op jit(solution)/shard_map/ppermute | solution.py:43
  125.0 20.0 %collective-permute-start.31 = (bf16[512,768]{1,0:T(8,128)(2,1)S(1)}, bf16[512,768]{1,0:T(8,128)(2,1)S(1)}, u32[]{:S(2)}, u32[]{:S(2)}) collective-permute-start(bf16[512,768]{1,0:T(8,128)(2,1)S(1)} %get-tuple-element.274.part_ref), channel_id=1, source_target_pairs={{0,2},{1,3},{2,0},{3,1},{4,6},{5,7},{6,4},{7,5},{8,10},{9,11},{10,... | collective-permute-start | bytes 2359304 | tf_op jit(solution)/shard_map/ppermute | solution.py:47
  130.6 25.9 %collective-permute-start.30 = (bf16[4,96,768]{2,1,0:T(8,128)(2,1)S(1)}, bf16[4,96,768]{2,1,0:T(8,128)(2,1)S(1)}, u32[]{:S(2)}, u32[]{:S(2)}) collective-permute-start(bf16[4,96,768]{2,1,0:T(8,128)(2,1)S(1)} %get-tuple-element.273), channel_id=1, source_target_pairs={{0,4},{4,0},{8,12},{12,8},{16,20},{20,16},{24,28},{28,24},{1,5},{5... | collective-permute-start | bytes 1769480 | tf_op jit(solution)/shard_map/ppermute | solution.py:52
  162.1 19.8 %collective-permute-start.37 = (bf16[512,768]{1,0:T(8,128)(2,1)S(1)}, bf16[512,768]{1,0:T(8,128)(2,1)S(1)}, u32[]{:S(2)}, u32[]{:S(2)}) collective-permute-start(bf16[512,768]{1,0:T(8,128)(2,1)S(1)} %get-tuple-element.286.part_ref), channel_id=1, source_target_pairs={{0,2},{1,3},{2,0},{3,1},{4,6},{5,7},{6,4},{7,5},{8,10},{9,11},{10,... | collective-permute-start | bytes 2359304 | tf_op jit(solution)/shard_map/ppermute | solution.py:47
  162.6 21.5 %collective-permute-start.32 = (bf16[4,96,768]{2,1,0:T(8,128)(2,1)S(1)}, bf16[4,96,768]{2,1,0:T(8,128)(2,1)S(1)}, u32[]{:S(2)}, u32[]{:S(2)}) collective-permute-start(bf16[4,96,768]{2,1,0:T(8,128)(2,1)S(1)} %get-tuple-element.282), channel_id=1, source_target_pairs={{0,4},{4,0},{8,12},{12,8},{16,20},{20,16},{24,28},{28,24},{1,5},{5... | collective-permute-start | bytes 1769480 | tf_op jit(solution)/shard_map/ppermute | solution.py:52
  163.9 14.1 %collective-permute-start.35 = (bf16[96,768]{1,0:T(8,128)(2,1)S(1)}, bf16[96,768]{1,0:T(8,128)(2,1)S(1)}, u32[]{:S(2)}, u32[]{:S(2)}) collective-permute-start(bf16[96,768]{1,0:T(8,128)(2,1)S(1)} %get-tuple-element.290), channel_id=1, source_target_pairs={{0,16},{4,20},{8,24},{12,28},{16,0},{20,4},{24,8},{28,12},{1,17},{... | collective-permute-start | bytes 442376 | tf_op jit(solution)/shard_map/ppermute | solution.py:52
  184.9 19.1 %collective-permute-start.42 = (bf16[4,96,768]{2,1,0:T(8,128)(2,1)S(1)}, bf16[4,96,768]{2,1,0:T(8,128)(2,1)S(1)}, u32[]{:S(2)}, u32[]{:S(2)}) collective-permute-start(bf16[4,96,768]{2,1,0:T(8,128)(2,1)S(1)} %get-tuple-element.296), channel_id=1, source_target_pairs={{0,4},{4,0},{8,12},{12,8},{16,20},{20,16},{24,28},{28,24},{1,5},{5... | collective-permute-start | bytes 1769480 | tf_op jit(solution)/shard_map/ppermute | solution.py:52
  188.6 18.3 %collective-permute-start.45 = (bf16[4,96,384]{2,1,0:T(8,128)(2,1)S(1)}, bf16[4,96,384]{2,1,0:T(8,128)(2,1)S(1)}, u32[]{:S(2)}, u32[]{:S(2)}) collective-permute-start(bf16[4,96,384]{2,1,0:T(8,128)(2,1)S(1)} %get-tuple-element.317), channel_id=1, source_target_pairs={{0,4},{4,0},{8,12},{12,8},{16,20},{20,16},{24,28},{28,24},{1,5},{5... | collective-permute-start | bytes 884744 | tf_op jit(solution)/shard_map/ppermute | solution.py:52
  189.9 14.1 %collective-permute-start.40 = (bf16[96,768]{1,0:T(8,128)(2,1)S(1)}, bf16[96,768]{1,0:T(8,128)(2,1)S(1)}, u32[]{:S(2)}, u32[]{:S(2)}) collective-permute-start(bf16[96,768]{1,0:T(8,128)(2,1)S(1)} %get-tuple-element.305), channel_id=1, source_target_pairs={{0,16},{4,20},{8,24},{12,28},{16,0},{20,4},{24,8},{28,12},{1,17},{... | collective-permute-start | bytes 442376 | tf_op jit(solution)/shard_map/ppermute | solution.py:52
  209.1 22.2 %collective-permute-start.50 = (bf16[512,768]{1,0:T(8,128)(2,1)S(1)}, bf16[512,768]{1,0:T(8,128)(2,1)S(1)}, u32[]{:S(2)}, u32[]{:S(2)}) collective-permute-start(bf16[512,768]{1,0:T(8,128)(2,1)S(1)} %feed_out.1.part_ref), channel_id=1, source_target_pairs={{0,2},{1,3},{2,0},{3,1},{4,6},{5,7},{6,4},{7,5},{8,10},{9,11},{10,... | collective-permute-start | bytes 2359304 | tf_op jit(solution)/shard_map/ppermute | solution.py:47
  209.7 21.5 %collective-permute-start.46 = (bf16[4,96,640]{2,1,0:T(8,128)(2,1)S(1)}, bf16[4,96,640]{2,1,0:T(8,128)(2,1)S(1)}, u32[]{:S(2)}, u32[]{:S(2)}) collective-permute-start(bf16[4,96,640]{2,1,0:T(8,128)(2,1)S(1)} %get-tuple-element.329), channel_id=1, source_target_pairs={{0,4},{4,0},{8,12},{12,8},{16,20},{20,16},{24,28},{28,24},{1,5},{5... | collective-permute-start | bytes 1474568 | tf_op jit(solution)/shard_map/ppermute | solution.py:52
  211.0 18.8 %collective-permute-start.48 = (bf16[96,1152]{1,0:T(8,128)(2,1)S(1)}, bf16[96,1152]{1,0:T(8,128)(2,1)S(1)}, u32[]{:S(2)}, u32[]{:S(2)}) collective-permute-start(bf16[96,1152]{1,0:T(8,128)(2,1)S(1)} %get-tuple-element.336), channel_id=1, source_target_pairs={{0,16},{4,20},{8,24},{12,28},{16,0},{20,4},{24,8},{28,12},{1,17},{... | collective-permute-start | bytes 663560 | tf_op jit(solution)/shard_map/ppermute | solution.py:52
  214.0 16.5 %collective-permute-start.49 = (bf16[96,1152]{1,0:T(8,128)(2,1)S(1)}, bf16[96,1152]{1,0:T(8,128)(2,1)S(1)}, u32[]{:S(2)}, u32[]{:S(2)}) collective-permute-start(bf16[96,1152]{1,0:T(8,128)(2,1)S(1)} %get-tuple-element.337), channel_id=1, source_target_pairs={{0,24},{4,28},{8,16},{12,20},{16,8},{20,12},{24,0},{28,4},{1,25},{... | collective-permute-start | bytes 663560 | tf_op jit(solution)/shard_map/ppermute | solution.py:52
  241.5 23.0 %collective-permute-start.62 = (bf16[512,768]{1,0:T(8,128)(2,1)S(1)}, bf16[512,768]{1,0:T(8,128)(2,1)}, u32[]{:S(2)}, u32[]{:S(2)}) collective-permute-start(bf16[512,768]{1,0:T(8,128)(2,1)S(1)} %first_part.1.part_ref), channel_id=1, source_target_pairs={{0,2},{1,3},{2,0},{3,1},{4,6},{5,7},{6,4},{7,5},{8,10},{9,11},{10,... | collective-permute-start | bytes 2359304 | tf_op jit(solution)/shard_map/ppermute | solution.py:47
  245.5 11.7 %collective-permute-start.56 = (bf16[96,640]{1,0:T(8,128)(2,1)S(1)}, bf16[96,640]{1,0:T(8,128)(2,1)S(1)}, u32[]{:S(2)}, u32[]{:S(2)}) collective-permute-start(bf16[96,640]{1,0:T(8,128)(2,1)S(1)} %get-tuple-element.361), channel_id=1, source_target_pairs={{0,16},{4,20},{8,24},{12,28},{16,0},{20,4},{24,8},{28,12},{1,17},{... | collective-permute-start | bytes 368648 | tf_op jit(solution)/shard_map/ppermute | solution.py:52
  (87 other events, 483.8 us)

commit v3 on v2

--- a/solution.py
+++ b/solution.py
@@ -834,9 +834,10 @@
 
 
 def time_back_kernel(
-    grad_ref, maps_ref, tokens_ref, back_ref, bias_ref, one_ref, two_ref, own_ref, far_ref, sums_ref, sorted_ref
+    grad_ref, maps_ref, tokens_ref, back_ref, bias_ref, one_ref, two_ref, own_ref, sums_ref, *refs
 ):
     count, width = tokens_ref.shape[0], grad_ref.shape[1] // 3
+    far_refs, sorted_ref = refs[:-1], refs[-1]
     sums_ref[...] = jnp.zeros_like(sums_ref)
     sums_ref[2:3] = 0.5 * bias_ref[0:1]
     sums_ref[3:6] = 0.5 * one_ref[1:4]
@@ -850,8 +851,10 @@
 
     chunk_loop(count, project)
     rows = count // 2
-    for i in range(0, rows, CHUNK):
-        far_ref[i : i + CHUNK, :] = dot(back_ref[rows + i : rows + i + CHUNK, :], sorted_ref[...]).astype(BF16)
+    cut = rows // len(far_refs)
+    for i, far_ref in enumerate(far_refs):
+        at = slice(rows + i * cut, rows + (i + 1) * cut)
+        far_ref[...] = dot(back_ref[at, :], sorted_ref[...]).astype(BF16)
     for i in range(0, rows, CHUNK):
         own_ref[i : i + CHUNK, :] = dot(back_ref[i : i + CHUNK, :], sorted_ref[...]).astype(BF16)
 
@@ -926,8 +929,12 @@
     send_ref[...] = total[:, width:].astype(BF16)
 
 
-def add_kernel(own_ref, got_ref, out_ref):
-    out_ref[...] = (own_ref[...].astype(F32) + got_ref[...].astype(F32)).astype(BF16)
+def add_kernel(own_ref, *refs):
+    got_refs, out_ref = refs[:-1], refs[-1]
+    rows = got_refs[0].shape[0]
+    for i, ref in enumerate(got_refs):
+        at = slice(i * rows, (i + 1) * rows)
+        out_ref[at, :] = (own_ref[at, :].astype(F32) + ref[...].astype(F32)).astype(BF16)
 
 
 def whole_grad_kernel(head_ref, early_ref, grad_ref):
@@ -1162,7 +1169,7 @@
     (up_send, up_keep), (down_send, down_keep) = split_rows(
         "split_feed", [(feed_grad_own, core_swap(feed_grad_far))], (hidden,)
     )
-    up_y = [dp_swap(up_send, 1)]
+    up_y, down_y = [dp_swap(up_send, 1)], [dp_swap(down_send, 1)]
     third_got, feed_part = lax.optimization_barrier((third_got, feed_part))
 
     grad_two, grad_two_low, sums_two, space_grad_heads = local_call(
@@ -1185,10 +1192,9 @@
             pltpu.VMEM((CLASSES, 2 * width), BF16),
         ],
     )
-    up_y, (space_send,) = together(up_y, [space_send])
+    up_y, down_y, (space_send,) = together(up_y, down_y, [space_send])
     up_shards = z_swaps(y_sums("sum_up", [(up_keep, up_y)]))
     space_got_grads = core_swap(space_send)
-    down_y = [dp_swap(after(down_send, *up_y), 1)]
     grad_space, grad_space_far, second_part = local_call(
         "space_back",
         space_back_kernel,
@@ -1214,13 +1220,14 @@
             in_specs=[SMEM, VMEM, VMEM],
             out_specs=ANY,
             scratch_shapes=[pltpu.SemaphoreType.DMA((2,))],
-            compiler_params=pltpu.CompilerParams(vmem_limit_bytes=2**21),
+            compiler_params=pltpu.CompilerParams(vmem_limit_bytes=2**23),
             cost_estimate=pl.CostEstimate(flops=0, bytes_accessed=0, transcendentals=0),
         )(place, value, got)
 
     ((space_y_send, space_keep),) = split_rows("split_space", [(space_grad_own, core_swap(space_grad_far))])
     space_y = [dp_swap(space_y_send, 1)]
-    up_shards, (second_got, space_y_send) = together(up_shards, [second_got, space_y_send])
+    up_shards, space_y, (second_got,) = together(up_shards, space_y, [second_got])
+    feed_part_got = x_swap(after(feed_part, space_y_send))
     grad_one, grad_one_low, sums_one, time_grad_own, time_grad_send = local_call(
         "time_back_in",
         time_back_in_kernel,
@@ -1232,9 +1239,6 @@
             wide(width, BF16),
         ],
         second_part, second_got, stream_one, vec, grad_two, fused, fused_far,
-    )
-    down_y, (time_grad_own, time_grad_send, grad_one_low) = together(
-        down_y, [time_grad_own, time_grad_send, grad_one_low]
     )
     down_shards = z_swaps(y_sums("sum_down", [(down_keep, down_y)]))
     time_grad_got = core_swap(time_grad_send)
@@ -1267,7 +1271,11 @@
         time_grad_own, time_grad_got, order, time_inputs, time_logs, time_col, time_row,
         scratch=[pltpu.VMEM((count, width), BF16), pltpu.VMEM((count, 2 * width), F32)],
     )
-    down_shards, space_y, out_y, (grad_time,) = together(down_shards, space_y, out_y, [grad_time])
+    down_shards, out_y, (grad_time, feed_part_got) = together(down_shards, out_y, [grad_time, feed_part_got])
+    (layer_half,) = local_call(
+        "layer_out", layer_out_kernel, [wide(features, F32)], stream_two, feed_part, feed_part_got, vec
+    )
+    layer_got = core_swap(layer_half)
     time_columns = 3 * width + SPARE
     time_send, time_keep = local_call(
         "time_grads",
@@ -1277,19 +1285,27 @@
         smem=(0,),
         scratch=[pltpu.VMEM((features, time_columns), F32)],
     )
-    space_y, out_y, (time_send, grad_time) = together(space_y, out_y, [time_send, grad_time])
+    out_y, (time_send, grad_time, layer_got) = together(out_y, [time_send, grad_time, layer_got])
     time_y = [dp_swap(time_send, 1)]
-    late_shards = z_swaps(y_sums("sum_late", [(out_keep, out_y), (space_keep, space_y)]))
-    first_own, first_send, vector_sum = local_call(
+    late_sums = jnp.concatenate(
+        [keep + arrived[0].astype(F32) for keep, arrived in ((out_keep, out_y), (space_keep, space_y))], 2
+    )
+    late_shards = z_swaps([late_sums[0], *[late_sums[k].astype(BF16) for k in range(1, half)]])
+    first_own, vector_sum, *first_sends = local_call(
         "time_back",
         time_back_kernel,
-        [wide(features, BF16), wide(features, BF16), shaped((16, features), F32)],
+        [wide(features, BF16), shaped((16, features), F32), wide(features, BF16)],
         grad_time, time_maps, tokens_sorted, back, bias_grad, sums_one, sums_two,
         scratch=[pltpu.VMEM((count, features), BF16)],
     )
-    feed_part_got = x_swap(after(feed_part, time_send))
-    time_y, late_shards, (first_send, feed_part_got) = together(time_y, late_shards, [first_send, feed_part_got])
-    first_got = core_swap(first_send)
+    first_got = [core_swap(one) for one in first_sends]
+    (first_part,) = local_call("first_part", add_kernel, [wide(features, BF16)], first_own, *first_got)
+    time_y, (first_part,) = together(time_y, [first_part])
+    first_part_got = x_swap(first_part)
+    time_shards = y_sums("sum_time", [(time_keep, time_y)])
+    layer_rows = whole("layer_rows", after(layer_half, time_shards[0]), layer_got)
+    late_shards = lax.optimization_barrier((*late_shards, time_shards[0], layer_rows))[: len(late_shards)]
+    time_shards = z_swaps(time_shards)
 
     out_width = 2 * width
     out_grad, mix_keep, mix_send = local_call(
@@ -1298,8 +1314,8 @@
         [shaped((shard, width), F32), shaped((shard, out_width), F32), shaped((shard, out_width), BF16)],
         place, out_map, *late_shards,
         smem=(0,),
-    )
-    (first_part,) = local_call("first_part", add_kernel, [wide(features, BF16)], first_own, first_got)
+        flops=LONG,
+    )
     mix_own, mix_send = local_call(
         "mix_sum",
         mix_sum_kernel,
@@ -1307,16 +1323,6 @@
         mix_keep, core_swap(mix_send),
     )
     mix_got = x_swap(mix_send)
-    first_part = after(first_part, mix_send)
-    first_part_got = x_swap(first_part)
-    (layer_half,) = local_call(
-        "layer_out", layer_out_kernel, [wide(features, F32)], stream_two, feed_part, feed_part_got, vec
-    )
-    layer_got = core_swap(after(layer_half, first_got))
-    time_shards = y_sums("sum_time", [(time_keep, time_y)])
-    time_shards, (mix_got, layer_got) = together(time_shards, [mix_got, layer_got])
-    time_shards = z_swaps(time_shards)
-    layer_rows = whole("layer_rows", layer_half, layer_got)
 
     bias_part = lax.dynamic_slice_in_dim(vec[2:3], lax.axis_index("heads") * width, width, 1)
     late = [out_width, out_width + 4 * width]
@@ -1324,7 +1330,7 @@
     up_shards, down_shards, _ = together(up_shards, down_shards, [first_part])
     early_grad = jnp.concatenate([total(late_shards)[:, out_width:], total(up_shards), total(down_shards)], 1)
     early_square = jnp.sum(early_grad * early_grad)
-    time_shards, (early_grad, early_square, layer_rows) = together(time_shards, [early_grad, early_square, layer_rows])
+    time_shards, (early_grad, early_square, mix_got) = together(time_shards, [early_grad, early_square, mix_got])
     time_total = total(time_shards)
     mix_grad = mix_own + mix_got.astype(F32) + time_total[:, 3 * width : 3 * width + 1] * bias_part
     head_grad = jnp.concatenate([time_total[:, : 3 * width], out_grad, mix_grad], 1)
@@ -1361,7 +1367,7 @@
         out_specs=[ANY] * 4 + [VMEM] * 6,
         scratch_shapes=[pltpu.VMEM(weights.shape, F32)] * 8
         + [pltpu.SemaphoreType.DMA((steps, 4)), pltpu.SemaphoreType.DMA((steps, 4))],
-        compiler_params=pltpu.CompilerParams(vmem_limit_bytes=14 * 2**20),
+        compiler_params=pltpu.CompilerParams(vmem_limit_bytes=20 * 2**20),
     )(place, *terms, weight_grad, *states, *vector_states)
     weights_out, (vector_grad, grad_norm, *vectors_out) = outs[:4], outs[4:]
     return (

time: 289 us -> 289 us (level)
  waiting for transfers between devices: 104 us -> 101 us
  Pallas kernels: 88.9 us -> 91.8 us
    unnamed x104 -> x108, local copies, waits for them, and re-layouts: 13.8 us -> 11.2 us
    pallas_call x41 -> x40, Pallas kernels: 77.6 us -> 80 us  [local_call(): pl.pallas_call(kernel, name=name, out_shape=list(outs), in_specs=[SMEM if...]
  transfers between devices with their start and end apart: 67 -> 67, of which waited for: 28 -> 28; matrix products, arithmetic and copies ran while one was open for 1% -> 2% of each run, Pallas kernels for 24% -> 25%
where the time goes in v3:
time: 289 us; the launch traced here: 284 us
  waiting for transfers between devices  101 us (35%)
  Pallas kernels  91.8 us (32%)
  starting transfers between devices  71.6 us (25%)
  local copies, waits for them, and re-layouts  11.6 us (4%)
  other arithmetic  5.28 us (2%)
  between operations  3.17 us (1%)
    pallas_call x40, Pallas kernels, local_call(): pl.pallas_call(kernel, name=name, out_shape=list(outs), in_specs=[SMEM if...  80 us
    ppermute x36, waiting for transfers between devices, dp_swap(): return lax.ppermute(value, 'dp', [(i, i ^ mask) for i in range(count)])  68.2 us
    ppermute x36, starting transfers between devices, dp_swap(): return lax.ppermute(value, 'dp', [(i, i ^ mask) for i in range(count)])  53.2 us
    ppermute x8, waiting for transfers between devices, x_swap(): return lax.ppermute(value, 'heads', [(i, i ^ 2) for i in range(4)])  19.6 us
    ppermute x17, waiting for transfers between devices, core_swap(): return lax.ppermute(value, 'heads', [(i, i ^ 1) for i in range(4)])  11.8 us
    unnamed x108, local copies, waits for them, and re-layouts  11.2 us
    ppermute x6, starting transfers between devices, all_sum(): lax.ppermute(value, ('dp', 'heads'), [(i, i ^ mask) for i in range(count)])  10.5 us
    pallas_call x1, Pallas kernels, local(): pl.pallas_call(partial(update_kernel, len(terms), lax.axis_size('dp'), st...  6 us
  transfers between devices with their start and end apart: 67, of which 28 were waited for; matrix products, arithmetic and copies ran while one was open for 2% of the time, Pallas kernels for 25%

profile of v3, /device:TPU:0, one launch (start us, length us, event | category | flops | bytes accessed | tf_op | source)
XLA Modules:
  0.0 284.0 jit_solution(15579155231256635383)
XLA Ops:
  2.9 3.1 %collective-permute-start = (bf16[96,1024]{1,0:T(8,128)(2,1)S(1)}, bf16[96,1024]{1,0:T(8,128)(2,1)S(1)}, u32[]{:S(2)}, u32[]{:S(2)}) collective-permute-start(bf16[96,1024]{1,0:T(8,128)(2,1)S(1)} %get-tuple-element.200.refs_0_), channel_id=1, source_target_pairs={{0,8},{4,12},{8,0},{12,4},{16,24},{20,28},{24,16},{28,20},{1,9},{5... | collective-permute-start | bytes 589832 | tf_op jit(solution)/shard_map/ppermute | solution.py:52
  6.0 2.6 collective-permute-start.1
  13.2 5.2 %sort_rows.1 = (bf16[1024,768]{1,0:T(8,128)(2,1)S(1)}, bf16[1024,1024]{1,0:T(8,128)(2,1)S(1)}, bf16[1024,1024]{1,0:T(8,128)(2,1)S(1)}, f32[1024,8]{1,0:T(8,128)S...) custom-call(s32[5]{0:T(128)S(1)} %stack.47.place_ref, ...), custom_call_target="tpu_custom_call" | custom-call | tf_op jit(solution)/shard_map/sort_rows/pallas_call | solution.py:111
  18.8 4.3 %collective-permute-done.1.refs_2_ = bf16[96,1024]{1,0:T(8,128)(2,1)S(1)} collective-permute-done((bf16[96,1024]{1,0:T(8,128)(2,1)S(1)}, bf16[96,1024]{1,0:T(8,128)(2,1)S(1)}, u32[]{:S(2)}, u32[]{:S(2)}) %collective-permute-start.1) | collective-permute-done | bytes 196640 | tf_op jit(solution)/shard_map/ppermute | solution.py:52
  26.4 4.1 %collective-permute-done.5.refs_6_ = bf16[96,1024]{1,0:T(8,128)(2,1)S(1)} collective-permute-done((bf16[96,1024]{1,0:T(8,128)(2,1)S(1)}, bf16[96,1024]{1,0:T(8,128)(2,1)S(1)}, u32[]{:S(2)}, u32[]{:S(2)}) %collective-permute-start.5) | collective-permute-done | bytes 196640 | tf_op jit(solution)/shard_map/ppermute | solution.py:52
  35.9 3.5 %collective-permute-start.8 = (bf16[96,768]{1,0:T(8,128)(2,1)S(1)}, bf16[96,768]{1,0:T(8,128)(2,1)S(1)}, u32[]{:S(2)}, u32[]{:S(2)}) collective-permute-start(bf16[96,768]{1,0:T(8,128)(2,1)S(1)} %get-tuple-element.226.refs_0_), channel_id=1, source_target_pairs={{0,16},{4,20},{8,24},{12,28},{16,0},{20,4},{24,8},{28,12},{1,17},{... | collective-permute-start | bytes 442376 | tf_op jit(solution)/shard_map/ppermute | solution.py:52
  39.7 7.1 %time_forward.1 = (f32[16,768]{1,0:T(8,128)S(1)}, bf16[1024,768]{1,0:T(8,128)(2,1)S(1)}, bf16[1024,576]{1,0:T(8,128)(2,1)S(1)}, bf16[512,192]{1,0:T(8,128)(2,1)S...) custom-call(bf16[768,640]{1,0:T(8,128)(2,1)S(1)} %bitcast.52, ...), custom_call_target="tpu_custom_call" | custom-call | tf_op jit(solution)/shard_map/time_forward/pallas_call | solution.py:111
  61.7 10.1 %collective-permute-done.18.refs_4_ = bf16[4,96,768]{2,1,0:T(8,128)(2,1)S(1)} collective-permute-done((bf16[4,96,768]{2,1,0:T(8,128)(2,1)S(1)}, bf16[4,96,768]{2,1,0:T(8,128)(2,1)S(1)}, u32[]{:S(2)}, u32[]{:S(2)}) %collective-permute-start.18) | collective-permute-done | bytes 589856 | tf_op jit(solution)/shard_map/ppermute | solution.py:52
  72.4 3.0 %collective-permute-done.14.got_ref = bf16[512,768]{1,0:T(8,128)(2,1)S(1)} collective-permute-done((bf16[512,768]{1,0:T(8,128)(2,1)S(1)}, bf16[512,768]{1,0:T(8,128)(2,1)S(1)}, u32[]{:S(2)}, u32[]{:S(2)}) %collective-permute-start.14) | collective-permute-done | bytes 786464 | tf_op jit(solution)/shard_map/ppermute | solution.py:47
  83.4 7.3 %space_forward.1 = (bf16[512,384]{1,0:T(8,128)(2,1)S(1)}, f32[8,512]{1,0:T(8,128)S(1)}, f32[16,8]{1,0:T(8,128)S(1)}, bf16[512,768]{1,0:T(8,128)(2,1)S(1)}) custom-call(s32[5]{0:T(128)S(1)} %stack.47.place_ref, bf16[512,384]{1,0:T(8,128)(2,1)S(1)} %get-tuple-element.240.q_ref, bf16[512,768]{1,0:T(8,128)(2,1)S(1)} %get-tuple-element.241.pairs_ref, ...), custom_call_target="tpu_custom_call" | custom-call | tf_op jit(solution)/shard_map/space_forward/pallas_call | solution.py:111
  90.7 4.3 %collective-permute-done.22.refs_2_ = bf16[96,768]{1,0:T(8,128)(2,1)S(1)} collective-permute-done((bf16[96,768]{1,0:T(8,128)(2,1)S(1)}, bf16[96,768]{1,0:T(8,128)(2,1)S(1)}, u32[]{:S(2)}, u32[]{:S(2)}) %collective-permute-start.22) | collective-permute-done | bytes 147488 | tf_op jit(solution)/shard_map/ppermute | solution.py:52
  97.8 11.6 %collective-permute-done.27.refs_4_ = bf16[4,96,768]{2,1,0:T(8,128)(2,1)S(1)} collective-permute-done((bf16[4,96,768]{2,1,0:T(8,128)(2,1)S(1)}, bf16[4,96,768]{2,1,0:T(8,128)(2,1)S(1)}, u32[]{:S(2)}, u32[]{:S(2)}) %collective-permute-start.27) | collective-permute-done | bytes 589856 | tf_op jit(solution)/shard_map/ppermute | solution.py:52
  110.1 3.0 %collective-permute-done.25.got_ref = bf16[512,768]{1,0:T(8,128)(2,1)S(1)} collective-permute-done((bf16[512,768]{1,0:T(8,128)(2,1)S(1)}, bf16[512,768]{1,0:T(8,128)(2,1)S(1)}, u32[]{:S(2)}, u32[]{:S(2)}) %collective-permute-start.25) | collective-permute-done | bytes 786464 | tf_op jit(solution)/shard_map/ppermute | solution.py:47
  113.9 5.0 %feed.1 = (bf16[512,1536]{1,0:T(8,128)(2,1)S(1)}, bf16[512,1536]{1,0:T(8,128)(2,1)S(1)}, bf16[512,768]{1,0:T(8,128)(2,1)S(1)}) custom-call(bf16[512,768]{1,0:T(8,128)(2,1)S(1)} %get-tuple-element.247.third_ref, bf16[512,768]{1,0:T(8,128)(2,1)S(1)} %get-tuple-element.248.dy_ref, bf16[768,768]{1,0:T(8,128)(2,1)S(1)} %bitcast.50, ...), custom_call_target="tpu_custom_call" | custom-call | tf_op jit(solution)/shard_map/feed/pallas_call | solution.py:111
  122.5 2.4 collective-permute-done.30
  129.7 10.7 %collective-permute-done.29.got_ref = bf16[512,768]{1,0:T(8,128)(2,1)S(1)} collective-permute-done((bf16[512,768]{1,0:T(8,128)(2,1)S(1)}, bf16[512,768]{1,0:T(8,128)(2,1)S(1)}, u32[]{:S(2)}, u32[]{:S(2)}) %collective-permute-start.29) | collective-permute-done | bytes 786464 | tf_op jit(solution)/shard_map/ppermute | solution.py:47
  140.4 3.0 %space_back_in.1 = (f32[512,768]{1,0:T(8,128)S(1)}, bf16[512,768]{1,0:T(8,128)(2,1)S(1)}, f32[8,768]{1,0:T(8,128)S(1)}, bf16[512,384]{1,0:T(8,128)(2,1)S(1)}) custom-call(bf16[512,768]{1,0:T(8,128)(2,1)S(1)} %get-tuple-element.254.part_ref, bf16[512,768]{1,0:T(8,128)(2,1)S(1)} %collective-permute-done.29.got_ref, ...), custom_call_target="tpu_custom_call" | custom-call | tf_op jit(solution)/shard_map/space_back_in/pallas_call | solution.py:111
  143.4 8.7 %space_backward.1 = (bf16[512,384]{1,0:T(8,128)(2,1)S(1)}, f32[512,768]{1,0:T(8,128)S(1)}, bf16[512,768]{1,0:T(8,128)(2,1)S(1)}) custom-call(s32[5]{0:T(128)S(1)} %stack.47.place_ref, bf16[512,384]{1,0:T(8,128)(2,1)S(1)} %get-tuple-element.262.heads_ref, bf16[512,384]{1,0:T(8,128)(2,1)S(1)} %get-tuple-element.240.q_ref, ...), custom_call_target="tpu_custom_call" | custom-call | tf_op jit(solution)/shard_map/space_backward/pallas_call | solution.py:111
  165.0 3.5 %collective-permute-start.37 = (bf16[96,768]{1,0:T(8,128)(2,1)S(1)}, bf16[96,768]{1,0:T(8,128)(2,1)}, u32[]{:S(2)}, u32[]{:S(2)}) collective-permute-start(bf16[96,768]{1,0:T(8,128)(2,1)S(1)} %get-tuple-element.278), channel_id=1, source_target_pairs={{0,8},{4,12},{8,0},{12,4},{16,24},{20,28},{24,16},{28,20},{1,9},{5... | collective-permute-start | bytes 442376 | tf_op jit(solution)/shard_map/ppermute | solution.py:52
  171.1 3.5 %collective-permute-done.37 = bf16[96,768]{1,0:T(8,128)(2,1)} collective-permute-done((bf16[96,768]{1,0:T(8,128)(2,1)S(1)}, bf16[96,768]{1,0:T(8,128)(2,1)}, u32[]{:S(2)}, u32[]{:S(2)}) %collective-permute-start.37) | collective-permute-done | bytes 147488 | tf_op jit(solution)/shard_map/ppermute | solution.py:52
  175.2 7.4 %collective-permute-done.38 = bf16[96,768]{1,0:T(8,128)(2,1)S(1)} collective-permute-done((bf16[96,768]{1,0:T(8,128)(2,1)S(1)}, bf16[96,768]{1,0:T(8,128)(2,1)S(1)}, u32[]{:S(2)}, u32[]{:S(2)}) %collective-permute-start.38) | collective-permute-done | bytes 147488 | tf_op jit(solution)/shard_map/ppermute | solution.py:52
  197.4 6.3 %time_backward.1.grad_ref = bf16[1024,576]{1,0:T(8,128)(2,1)S(1)} custom-call(bf16[512,192]{1,0:T(8,128)(2,1)S(1)} %get-tuple-element.299.own_ref, bf16[512,192]{1,0:T(8,128)(2,1)S(1)} %collective-permute-done.44.far_ref, bf16[1024,1024]{1,0:T(8,128)(2,1)S(1)} %get-tuple-element.301.order_ref, bf16[1024,576]{1,0:T(8,128)(2,1)S(1)} %get-tuple-element.302.inputs_ref, ...), custom_call_target="tpu_custom_call" | custom-call | tf_op jit(solution)/shard_map/time_backward/pallas_call | solution.py:111
  203.8 5.1 %collective-permute-done.34 = bf16[96,768]{1,0:T(8,128)(2,1)S(1)} collective-permute-done((bf16[96,768]{1,0:T(8,128)(2,1)S(1)}, bf16[96,768]{1,0:T(8,128)(2,1)S(1)}, u32[]{:S(2)}, u32[]{:S(2)}) %collective-permute-start.34) | collective-permute-done | bytes 147488 | tf_op jit(solution)/shard_map/ppermute | solution.py:52
  216.2 4.3 %time_back.1 = (bf16[512,768]{1,0:T(8,128)(2,1)S(1)}, f32[16,768]{1,0:T(8,128)S(1)}, bf16[512,768]{1,0:T(8,128)(2,1)S(1)}) custom-call(bf16[1024,576]{1,0:T(8,128)(2,1)S(1)} %time_backward.1.grad_ref, bf16[768,640]{1,0:T(8,128)(2,1)S(1)} %bitcast.53, bf16[1024,768]{1,0:T(8,128)(2,1)S(1)} %copy-done.1, bf16[1024,1024]{1,0:T(8,128)(2,1)S(1)} %get-tuple-element.210.back_ref, ...), custom_call_target="tpu_custom_call" | custom-call | tf_op jit(solution)/shard_map/time_back/pallas_call | solution.py:111
  221.0 2.4 collective-permute-start.53
  231.4 3.6 %layer_rows.1 = f32[1024,768]{1,0:T(8,128)} custom-call(s32[5]{0:T(128)S(1)} %stack.47.place_ref, f32[512,768]{1,0:T(8,128)} %layer_out.1.own_ref, f32[512,768]{1,0:T(8,128)} %collective-permute-done.47.got_ref), custom_call_target="tpu_custom_call" | custom-call | tf_op jit(solution)/shard_map/layer_rows/pallas_call | solution.py:1216
  236.0 6.1 %collective-permute-done.54.refs_2_ = bf16[96,1152]{1,0:T(8,128)(2,1)S(1)} collective-permute-done((bf16[96,1152]{1,0:T(8,128)(2,1)S(1)}, bf16[96,1152]{1,0:T(8,128)(2,1)S(1)}, u32[]{:S(2)}, u32[]{:S(2)}) %collective-permute-start.54) | collective-permute-done | bytes 221216 | tf_op jit(solution)/shard_map/ppermute | solution.py:52
  242.1 2.7 collective-permute-start.52
  248.6 2.8 collective-permute-done.57
  251.4 3.4 %collective-permute-done.51 = bf16[96,640]{1,0:T(8,128)(2,1)S(1)} collective-permute-done((bf16[96,640]{1,0:T(8,128)(2,1)S(1)}, bf16[96,640]{1,0:T(8,128)(2,1)S(1)}, u32[]{:S(2)}, u32[]{:S(2)}) %collective-permute-start.51) | collective-permute-done | bytes 122912 | tf_op jit(solution)/shard_map/ppermute | solution.py:52
  265.9 4.5 %collective-permute-start.63 = (f32[16,768]{1,0:T(8,128)S(1)}, f32[16,768]{1,0:T(8,128)S(1)}, u32[]{:S(2)}, u32[]{:S(2)}) collective-permute-start(f32[16,768]{1,0:T(8,128)S(1)} %add_add_fusion.refs_0_), channel_id=1, source_target_pairs={{0,8},{1,9},{2,10},{3,11},{4,12},{5,13},{6,14},{7,15},{8,0},{9,1},... | collective-permute-start | bytes 147464 | tf_op jit(solution)/shard_map/ppermute | solution.py:61
  277.8 6.0 %update.1 = (f32[96,3264]{1,0:T(8,128)}, f32[96,3264]{1,0:T(8,128)}, f32[96,3264]{1,0:T(8,128)}, f32[96,3264]{1,0:T(8,128)}, f32[10,96]{1,0:T(8,128)}, /*index=5...) custom-call(s32[5]{0:T(128)S(1)} %stack.47.place_ref, ...), custom_call_target="tpu_custom_call" | custom-call | tf_op jit(solution)/shard_map/update/pallas_call | solution.py:1360
  (277 shorter events, 120.5 us)
Async XLA Ops:
  2.9 15.6 %collective-permute-start = (bf16[96,1024]{1,0:T(8,128)(2,1)S(1)}, bf16[96,1024]{1,0:T(8,128)(2,1)S(1)}, u32[]{:S(2)}, u32[]{:S(2)}) collective-permute-start(bf16[96,1024]{1,0:T(8,128)(2,1)S(1)} %get-tuple-element.200.refs_0_), channel_id=1, source_target_pairs={{0,8},{4,12},{8,0},{12,4},{16,24},{20,28},{24,16},{28,20},{1,9},{5... | collective-permute-start | bytes 589832 | tf_op jit(solution)/shard_map/ppermute | solution.py:52
  6.0 17.2 %collective-permute-start.1 = (bf16[96,1024]{1,0:T(8,128)(2,1)S(1)}, bf16[96,1024]{1,0:T(8,128)(2,1)S(1)}, u32[]{:S(2)}, u32[]{:S(2)}) collective-permute-start(bf16[96,1024]{1,0:T(8,128)(2,1)S(1)} %get-tuple-element.200.refs_0_), channel_id=1, source_target_pairs={{0,16},{4,20},{8,24},{12,28},{16,0},{20,4},{24,8},{28,12},{1,17},{... | collective-permute-start | bytes 589832 | tf_op jit(solution)/shard_map/ppermute | solution.py:52
  8.6 16.1 %collective-permute-start.2 = (bf16[96,1024]{1,0:T(8,128)(2,1)S(1)}, bf16[96,1024]{1,0:T(8,128)(2,1)S(1)}, u32[]{:S(2)}, u32[]{:S(2)}) collective-permute-start(bf16[96,1024]{1,0:T(8,128)(2,1)S(1)} %get-tuple-element.200.refs_0_), channel_id=1, source_target_pairs={{0,24},{4,28},{8,16},{12,20},{16,8},{20,12},{24,0},{28,4},{1,25},{... | collective-permute-start | bytes 589832 | tf_op jit(solution)/shard_map/ppermute | solution.py:52
  8.6 16.6 %collective-permute-start.3 = (bf16[96,1024]{1,0:T(8,128)(2,1)S(1)}, bf16[96,1024]{1,0:T(8,128)(2,1)}, u32[]{:S(2)}, u32[]{:S(2)}) collective-permute-start(bf16[96,1024]{1,0:T(8,128)(2,1)S(1)} %get-tuple-element.200.refs_0_), channel_id=1, source_target_pairs={{0,4},{4,0},{8,12},{12,8},{16,20},{20,16},{24,28},{28,24},{1,5},{5... | collective-permute-start | bytes 589832 | tf_op jit(solution)/shard_map/ppermute | solution.py:52
  33.8 15.1 %collective-permute-start.10 = (bf16[768,192]{1,0:T(8,128)(2,1)S(1)}, bf16[768,192]{1,0:T(8,128)(2,1)S(1)}, u32[]{:S(2)}, u32[]{:S(2)}) collective-permute-start(bf16[768,192]{1,0:T(8,128)(2,1)S(1)} %bitcast.55), channel_id=1, source_target_pairs={{0,2},{1,3},{2,0},{3,1},{4,6},{5,7},{6,4},{7,5},{8,10},{9,11},{10,... | collective-permute-start | bytes 884744 | tf_op jit(solution)/shard_map/ppermute | solution.py:47
  35.9 12.9 %collective-permute-start.8 = (bf16[96,768]{1,0:T(8,128)(2,1)S(1)}, bf16[96,768]{1,0:T(8,128)(2,1)S(1)}, u32[]{:S(2)}, u32[]{:S(2)}) collective-permute-start(bf16[96,768]{1,0:T(8,128)(2,1)S(1)} %get-tuple-element.226.refs_0_), channel_id=1, source_target_pairs={{0,16},{4,20},{8,24},{12,28},{16,0},{20,4},{24,8},{28,12},{1,17},{... | collective-permute-start | bytes 442376 | tf_op jit(solution)/shard_map/ppermute | solution.py:52
  55.8 19.6 %collective-permute-start.14 = (bf16[512,768]{1,0:T(8,128)(2,1)S(1)}, bf16[512,768]{1,0:T(8,128)(2,1)S(1)}, u32[]{:S(2)}, u32[]{:S(2)}) collective-permute-start(bf16[512,768]{1,0:T(8,128)(2,1)S(1)} %time_out.1.part_ref), channel_id=1, source_target_pairs={{0,2},{1,3},{2,0},{3,1},{4,6},{5,7},{6,4},{7,5},{8,10},{9,11},{10,... | collective-permute-start | bytes 2359304 | tf_op jit(solution)/shard_map/ppermute | solution.py:47
  56.6 15.2 %collective-permute-start.18 = (bf16[4,96,768]{2,1,0:T(8,128)(2,1)S(1)}, bf16[4,96,768]{2,1,0:T(8,128)(2,1)S(1)}, u32[]{:S(2)}, u32[]{:S(2)}) collective-permute-start(bf16[4,96,768]{2,1,0:T(8,128)(2,1)S(1)} %pad_maximum_fusion.3), channel_id=1, source_target_pairs={{0,4},{4,0},{8,12},{12,8},{16,20},{20,16},{24,28},{28,24},{1,5},{5... | collective-permute-start | bytes 1769480 | tf_op jit(solution)/shard_map/ppermute | solution.py:52
  56.9 21.1 %collective-permute-start.15 = (bf16[96,768]{1,0:T(8,128)(2,1)S(1)}, bf16[96,768]{1,0:T(8,128)(2,1)S(1)}, u32[]{:S(2)}, u32[]{:S(2)}) collective-permute-start(bf16[96,768]{1,0:T(8,128)(2,1)S(1)} %get-tuple-element.234.refs_0_), channel_id=1, source_target_pairs={{0,8},{4,12},{8,0},{12,4},{16,24},{20,28},{24,16},{28,20},{1,9},{5... | collective-permute-start | bytes 442376 | tf_op jit(solution)/shard_map/ppermute | solution.py:52
  59.3 18.7 %collective-permute-start.16 = (bf16[96,768]{1,0:T(8,128)(2,1)S(1)}, bf16[96,768]{1,0:T(8,128)(2,1)S(1)}, u32[]{:S(2)}, u32[]{:S(2)}) collective-permute-start(bf16[96,768]{1,0:T(8,128)(2,1)S(1)} %get-tuple-element.234.refs_0_), channel_id=1, source_target_pairs={{0,16},{4,20},{8,24},{12,28},{16,0},{20,4},{24,8},{28,12},{1,17},{... | collective-permute-start | bytes 442376 | tf_op jit(solution)/shard_map/ppermute | solution.py:52
  60.3 17.7 %collective-permute-start.17 = (bf16[96,768]{1,0:T(8,128)(2,1)S(1)}, bf16[96,768]{1,0:T(8,128)(2,1)S(1)}, u32[]{:S(2)}, u32[]{:S(2)}) collective-permute-start(bf16[96,768]{1,0:T(8,128)(2,1)S(1)} %get-tuple-element.234.refs_0_), channel_id=1, source_target_pairs={{0,24},{4,28},{8,16},{12,20},{16,8},{20,12},{24,0},{28,4},{1,25},{... | collective-permute-start | bytes 442376 | tf_op jit(solution)/shard_map/ppermute | solution.py:52
  78.2 16.7 %collective-permute-start.20 = (bf16[4,96,768]{2,1,0:T(8,128)(2,1)S(1)}, bf16[4,96,768]{2,1,0:T(8,128)(2,1)S(1)}, u32[]{:S(2)}, u32[]{:S(2)}) collective-permute-start(bf16[4,96,768]{2,1,0:T(8,128)(2,1)S(1)} %pad_maximum_fusion.4), channel_id=1, source_target_pairs={{0,4},{4,0},{8,12},{12,8},{16,20},{20,16},{24,28},{28,24},{1,5},{5... | collective-permute-start | bytes 1769480 | tf_op jit(solution)/shard_map/ppermute | solution.py:52
  81.0 13.9 %collective-permute-start.22 = (bf16[96,768]{1,0:T(8,128)(2,1)S(1)}, bf16[96,768]{1,0:T(8,128)(2,1)S(1)}, u32[]{:S(2)}, u32[]{:S(2)}) collective-permute-start(bf16[96,768]{1,0:T(8,128)(2,1)S(1)} %get-tuple-element.250.refs_0_), channel_id=1, source_target_pairs={{0,16},{4,20},{8,24},{12,28},{16,0},{20,4},{24,8},{28,12},{1,17},{... | collective-permute-start | bytes 442376 | tf_op jit(solution)/shard_map/ppermute | solution.py:52
  94.9 18.2 %collective-permute-start.25 = (bf16[512,768]{1,0:T(8,128)(2,1)S(1)}, bf16[512,768]{1,0:T(8,128)(2,1)S(1)}, u32[]{:S(2)}, u32[]{:S(2)}) collective-permute-start(bf16[512,768]{1,0:T(8,128)(2,1)S(1)} %get-tuple-element.245.part_ref), channel_id=1, source_target_pairs={{0,2},{1,3},{2,0},{3,1},{4,6},{5,7},{6,4},{7,5},{8,10},{9,11},{10,... | collective-permute-start | bytes 2359304 | tf_op jit(solution)/shard_map/ppermute | solution.py:47
  95.6 13.8 %collective-permute-start.27 = (bf16[4,96,768]{2,1,0:T(8,128)(2,1)S(1)}, bf16[4,96,768]{2,1,0:T(8,128)(2,1)S(1)}, u32[]{:S(2)}, u32[]{:S(2)}) collective-permute-start(bf16[4,96,768]{2,1,0:T(8,128)(2,1)S(1)} %pad_maximum_fusion.5), channel_id=1, source_target_pairs={{0,4},{4,0},{8,12},{12,8},{16,20},{20,16},{24,28},{28,24},{1,5},{5... | collective-permute-start | bytes 1769480 | tf_op jit(solution)/shard_map/ppermute | solution.py:52
  97.8 16.2 %collective-permute-start.26 = (bf16[768,768]{1,0:T(8,128)(2,1)S(1)}, bf16[768,768]{1,0:T(8,128)(2,1)S(1)}, u32[]{:S(2)}, u32[]{:S(2)}) collective-permute-start(bf16[768,768]{1,0:T(8,128)(2,1)S(1)} %bitcast.49), channel_id=1, source_target_pairs={{0,1},{1,0},{2,3},{3,2},{4,5},{5,4},{6,7},{7,6},{8,9},{9,8},{10,11... | collective-permute-start | bytes 3538952 | tf_op jit(solution)/shard_map/ppermute | solution.py:43
  120.4 20.0 %collective-permute-start.29 = (bf16[512,768]{1,0:T(8,128)(2,1)S(1)}, bf16[512,768]{1,0:T(8,128)(2,1)S(1)}, u32[]{:S(2)}, u32[]{:S(2)}) collective-permute-start(bf16[512,768]{1,0:T(8,128)(2,1)S(1)} %get-tuple-element.254.part_ref), channel_id=1, source_target_pairs={{0,2},{1,3},{2,0},{3,1},{4,6},{5,7},{6,4},{7,5},{8,10},{9,11},{10,... | collective-permute-start | bytes 2359304 | tf_op jit(solution)/shard_map/ppermute | solution.py:47
  126.0 26.1 %collective-permute-start.31 = (bf16[4,96,768]{2,1,0:T(8,128)(2,1)S(1)}, bf16[4,96,768]{2,1,0:T(8,128)(2,1)S(1)}, u32[]{:S(2)}, u32[]{:S(2)}) collective-permute-start(bf16[4,96,768]{2,1,0:T(8,128)(2,1)S(1)} %get-tuple-element.259), channel_id=1, source_target_pairs={{0,4},{4,0},{8,12},{12,8},{16,20},{20,16},{24,28},{28,24},{1,5},{5... | collective-permute-start | bytes 1769480 | tf_op jit(solution)/shard_map/ppermute | solution.py:52
  127.0 27.0 %collective-permute-start.32 = (bf16[4,96,768]{2,1,0:T(8,128)(2,1)S(1)}, bf16[4,96,768]{2,1,0:T(8,128)(2,1)S(1)}, u32[]{:S(2)}, u32[]{:S(2)}) collective-permute-start(bf16[4,96,768]{2,1,0:T(8,128)(2,1)S(1)} %get-tuple-element.260), channel_id=1, source_target_pairs={{0,4},{4,0},{8,12},{12,8},{16,20},{20,16},{24,28},{28,24},{1,5},{5... | collective-permute-start | bytes 1769480 | tf_op jit(solution)/shard_map/ppermute | solution.py:52
  159.6 22.9 %collective-permute-start.42 = (bf16[512,768]{1,0:T(8,128)(2,1)S(1)}, bf16[512,768]{1,0:T(8,128)(2,1)S(1)}, u32[]{:S(2)}, u32[]{:S(2)}) collective-permute-start(bf16[512,768]{1,0:T(8,128)(2,1)S(1)} %get-tuple-element.274.part_ref), channel_id=1, source_target_pairs={{0,2},{1,3},{2,0},{3,1},{4,6},{5,7},{6,4},{7,5},{8,10},{9,11},{10,... | collective-permute-start | bytes 2359304 | tf_op jit(solution)/shard_map/ppermute | solution.py:47
  163.1 19.4 %collective-permute-start.41 = (bf16[4,96,768]{2,1,0:T(8,128)(2,1)S(1)}, bf16[4,96,768]{2,1,0:T(8,128)(2,1)S(1)}, u32[]{:S(2)}, u32[]{:S(2)}) collective-permute-start(bf16[4,96,768]{2,1,0:T(8,128)(2,1)S(1)} %get-tuple-element.285), channel_id=1, source_target_pairs={{0,4},{4,0},{8,12},{12,8},{16,20},{20,16},{24,28},{28,24},{1,5},{5... | collective-permute-start | bytes 1769480 | tf_op jit(solution)/shard_map/ppermute | solution.py:52
  168.6 14.0 %collective-permute-start.38 = (bf16[96,768]{1,0:T(8,128)(2,1)S(1)}, bf16[96,768]{1,0:T(8,128)(2,1)S(1)}, u32[]{:S(2)}, u32[]{:S(2)}) collective-permute-start(bf16[96,768]{1,0:T(8,128)(2,1)S(1)} %get-tuple-element.279), channel_id=1, source_target_pairs={{0,16},{4,20},{8,24},{12,28},{16,0},{20,4},{24,8},{28,12},{1,17},{... | collective-permute-start | bytes 442376 | tf_op jit(solution)/shard_map/ppermute | solution.py:52
  174.6 34.3 %collective-permute-start.46 = (bf16[512,768]{1,0:T(8,128)(2,1)S(1)}, bf16[512,768]{1,0:T(8,128)(2,1)S(1)}, u32[]{:S(2)}, u32[]{:S(2)}) collective-permute-start(bf16[512,768]{1,0:T(8,128)(2,1)S(1)} %feed_out.1.part_ref), channel_id=1, source_target_pairs={{0,2},{1,3},{2,0},{3,1},{4,6},{5,7},{6,4},{7,5},{8,10},{9,11},{10,... | collective-permute-start | bytes 2359304 | tf_op jit(solution)/shard_map/ppermute | solution.py:47
  191.0 17.9 %collective-permute-start.45 = (bf16[4,96,384]{2,1,0:T(8,128)(2,1)S(1)}, bf16[4,96,384]{2,1,0:T(8,128)(2,1)S(1)}, u32[]{:S(2)}, u32[]{:S(2)}) collective-permute-start(bf16[4,96,384]{2,1,0:T(8,128)(2,1)S(1)} %get-tuple-element.298), channel_id=1, source_target_pairs={{0,4},{4,0},{8,12},{12,8},{16,20},{20,16},{24,28},{28,24},{1,5},{5... | collective-permute-start | bytes 884744 | tf_op jit(solution)/shard_map/ppermute | solution.py:52
  194.9 14.0 %collective-permute-start.34 = (bf16[96,768]{1,0:T(8,128)(2,1)S(1)}, bf16[96,768]{1,0:T(8,128)(2,1)S(1)}, u32[]{:S(2)}, u32[]{:S(2)}) collective-permute-start(bf16[96,768]{1,0:T(8,128)(2,1)S(1)} %get-tuple-element.269), channel_id=1, source_target_pairs={{0,16},{4,20},{8,24},{12,28},{16,0},{20,4},{24,8},{28,12},{1,17},{... | collective-permute-start | bytes 442376 | tf_op jit(solution)/shard_map/ppermute | solution.py:52
  214.7 13.7 %collective-permute-start.48 = (bf16[4,96,640]{2,1,0:T(8,128)(2,1)S(1)}, bf16[4,96,640]{2,1,0:T(8,128)(2,1)S(1)}, u32[]{:S(2)}, u32[]{:S(2)}) collective-permute-start(bf16[4,96,640]{2,1,0:T(8,128)(2,1)S(1)} %get-tuple-element.312), channel_id=1, source_target_pairs={{0,4},{4,0},{8,12},{12,8},{16,20},{20,16},{24,28},{28,24},{1,5},{5... | collective-permute-start | bytes 1474568 | tf_op jit(solution)/shard_map/ppermute | solution.py:52
  221.0 13.9 %collective-permute-start.53 = (bf16[96,1152]{1,0:T(8,128)(2,1)S(1)}, bf16[96,1152]{1,0:T(8,128)(2,1)S(1)}, u32[]{:S(2)}, u32[]{:S(2)}) collective-permute-start(bf16[96,1152]{1,0:T(8,128)(2,1)S(1)} %get-tuple-element.391), channel_id=1, source_target_pairs={{0,8},{4,12},{8,0},{12,4},{16,24},{20,28},{24,16},{28,20},{1,9},{5... | collective-permute-start | bytes 663560 | tf_op jit(solution)/shard_map/ppermute | solution.py:52
  223.4 18.7 %collective-permute-start.54 = (bf16[96,1152]{1,0:T(8,128)(2,1)S(1)}, bf16[96,1152]{1,0:T(8,128)(2,1)S(1)}, u32[]{:S(2)}, u32[]{:S(2)}) collective-permute-start(bf16[96,1152]{1,0:T(8,128)(2,1)S(1)} %get-tuple-element.390), channel_id=1, source_target_pairs={{0,16},{4,20},{8,24},{12,28},{16,0},{20,4},{24,8},{28,12},{1,17},{... | collective-permute-start | bytes 663560 | tf_op jit(solution)/shard_map/ppermute | solution.py:52
  224.4 20.4 %collective-permute-start.55 = (bf16[96,1152]{1,0:T(8,128)(2,1)S(1)}, bf16[96,1152]{1,0:T(8,128)(2,1)S(1)}, u32[]{:S(2)}, u32[]{:S(2)}) collective-permute-start(bf16[96,1152]{1,0:T(8,128)(2,1)S(1)} %get-tuple-element.389), channel_id=1, source_target_pairs={{0,24},{4,28},{8,16},{12,20},{16,8},{20,12},{24,0},{28,4},{1,25},{... | collective-permute-start | bytes 663560 | tf_op jit(solution)/shard_map/ppermute | solution.py:52
  228.5 22.9 %collective-permute-start.50 = (bf16[96,640]{1,0:T(8,128)(2,1)S(1)}, bf16[96,640]{1,0:T(8,128)(2,1)S(1)}, u32[]{:S(2)}, u32[]{:S(2)}) collective-permute-start(bf16[96,640]{1,0:T(8,128)(2,1)S(1)} %get-tuple-element.322), channel_id=1, source_target_pairs={{0,8},{4,12},{8,0},{12,4},{16,24},{20,28},{24,16},{28,20},{1,9},{5... | collective-permute-start | bytes 368648 | tf_op jit(solution)/shard_map/ppermute | solution.py:52
  230.8 31.2 %collective-permute-start.62 = (bf16[512,768]{1,0:T(8,128)(2,1)S(1)}, bf16[512,768]{1,0:T(8,128)(2,1)}, u32[]{:S(2)}, u32[]{:S(2)}) collective-permute-start(bf16[512,768]{1,0:T(8,128)(2,1)S(1)} %first_part.1.part_ref), channel_id=1, source_target_pairs={{0,2},{1,3},{2,0},{3,1},{4,6},{5,7},{6,4},{7,5},{8,10},{9,11},{10,... | collective-permute-start | bytes 2359304 | tf_op jit(solution)/shard_map/ppermute | solution.py:47
  235.0 19.8 %collective-permute-start.51 = (bf16[96,640]{1,0:T(8,128)(2,1)S(1)}, bf16[96,640]{1,0:T(8,128)(2,1)S(1)}, u32[]{:S(2)}, u32[]{:S(2)}) collective-permute-start(bf16[96,640]{1,0:T(8,128)(2,1)S(1)} %get-tuple-element.323), channel_id=1, source_target_pairs={{0,16},{4,20},{8,24},{12,28},{16,0},{20,4},{24,8},{28,12},{1,17},{... | collective-permute-start | bytes 368648 | tf_op jit(solution)/shard_map/ppermute | solution.py:52
  (89 other events, 564.5 us)

commit v4 on v2

--- a/solution.py
+++ b/solution.py
@@ -160,7 +160,9 @@
 
 
 def z_blocks(piece):
-    return [piece] + [dp_swap(piece, 2 * k) for k in range(1, lax.axis_size("dp") // 2)]
+    order = range(lax.axis_size("dp") // 2 - 1, 0, -1)
+    got = {k: dp_swap(piece, 2 * k) for k in order}
+    return [piece] + [got[k] for k in sorted(got)]
 
 
 def y_blocks(mine, fine=False):
@@ -1214,7 +1216,7 @@
             in_specs=[SMEM, VMEM, VMEM],
             out_specs=ANY,
             scratch_shapes=[pltpu.SemaphoreType.DMA((2,))],
-            compiler_params=pltpu.CompilerParams(vmem_limit_bytes=2**21),
+            compiler_params=pltpu.CompilerParams(vmem_limit_bytes=2**23),
             cost_estimate=pl.CostEstimate(flops=0, bytes_accessed=0, transcendentals=0),
         )(place, value, got)
 
@@ -1361,7 +1363,7 @@
         out_specs=[ANY] * 4 + [VMEM] * 6,
         scratch_shapes=[pltpu.VMEM(weights.shape, F32)] * 8
         + [pltpu.SemaphoreType.DMA((steps, 4)), pltpu.SemaphoreType.DMA((steps, 4))],
-        compiler_params=pltpu.CompilerParams(vmem_limit_bytes=14 * 2**20),
+        compiler_params=pltpu.CompilerParams(vmem_limit_bytes=20 * 2**20),
     )(place, *terms, weight_grad, *states, *vector_states)
     weights_out, (vector_grad, grad_norm, *vectors_out) = outs[:4], outs[4:]
     return (

time: 289 us -> 289 us (level)
  no operation moved by 1% of the time
where the time goes in v4:
time: 289 us; the launch traced here: 284 us
  waiting for transfers between devices  104 us (36%)
  Pallas kernels  88.9 us (31%)
  starting transfers between devices  70.9 us (25%)
  local copies, waits for them, and re-layouts  14.1 us (5%)
  between operations  3.14 us (1%)
    pallas_call x41, Pallas kernels, local_call(): pl.pallas_call(kernel, name=name, out_shape=list(outs), in_specs=[SMEM if...  77.6 us
    ppermute x36, waiting for transfers between devices, dp_swap(): return lax.ppermute(value, 'dp', [(i, i ^ mask) for i in range(count)])  70 us
    ppermute x36, starting transfers between devices, dp_swap(): return lax.ppermute(value, 'dp', [(i, i ^ mask) for i in range(count)])  54.1 us
    ppermute x8, waiting for transfers between devices, x_swap(): return lax.ppermute(value, 'heads', [(i, i ^ 2) for i in range(4)])  22.2 us
    unnamed x104, local copies, waits for them, and re-layouts  13.8 us
    ppermute x17, waiting for transfers between devices, core_swap(): return lax.ppermute(value, 'heads', [(i, i ^ 1) for i in range(4)])  11.6 us
    ppermute x6, starting transfers between devices, all_sum(): lax.ppermute(value, ('dp', 'heads'), [(i, i ^ mask) for i in range(count)])  7.95 us
    ppermute x8, starting transfers between devices, x_swap(): return lax.ppermute(value, 'heads', [(i, i ^ 2) for i in range(4)])  6.61 us
  transfers between devices with their start and end apart: 67, of which 28 were waited for; matrix products, arithmetic and copies ran while one was open for 1% of the time, Pallas kernels for 24%

profile of v4, /device:TPU:0, one launch (start us, length us, event | category | flops | bytes accessed | tf_op | source)
XLA Modules:
  0.0 284.0 jit_solution(2700870554707426076)
XLA Ops:
  2.9 3.1 %collective-permute-start = (bf16[96,1024]{1,0:T(8,128)(2,1)S(1)}, bf16[96,1024]{1,0:T(8,128)(2,1)S(1)}, u32[]{:S(2)}, u32[]{:S(2)}) collective-permute-start(bf16[96,1024]{1,0:T(8,128)(2,1)S(1)} %get-tuple-element.214.refs_0_), channel_id=1, source_target_pairs={{0,8},{4,12},{8,0},{12,4},{16,24},{20,28},{24,16},{28,20},{1,9},{5... | collective-permute-start | bytes 589832 | tf_op jit(solution)/shard_map/ppermute | solution.py:52
  6.0 2.6 collective-permute-start.1
  13.2 5.2 %sort_rows.1 = (bf16[1024,768]{1,0:T(8,128)(2,1)S(1)}, bf16[1024,1024]{1,0:T(8,128)(2,1)S(1)}, bf16[1024,1024]{1,0:T(8,128)(2,1)S(1)}, f32[1024,8]{1,0:T(8,128)S...) custom-call(s32[5]{0:T(128)S(1)} %stack.47.place_ref, ...), custom_call_target="tpu_custom_call" | custom-call | tf_op jit(solution)/shard_map/sort_rows/pallas_call | solution.py:111
  18.4 4.7 %collective-permute-done.1.refs_2_ = bf16[96,1024]{1,0:T(8,128)(2,1)S(1)} collective-permute-done((bf16[96,1024]{1,0:T(8,128)(2,1)S(1)}, bf16[96,1024]{1,0:T(8,128)(2,1)S(1)}, u32[]{:S(2)}, u32[]{:S(2)}) %collective-permute-start.1) | collective-permute-done | bytes 196640 | tf_op jit(solution)/shard_map/ppermute | solution.py:52
  26.7 4.3 %collective-permute-done.6.refs_7_ = bf16[96,1024]{1,0:T(8,128)(2,1)S(1)} collective-permute-done((bf16[96,1024]{1,0:T(8,128)(2,1)S(1)}, bf16[96,1024]{1,0:T(8,128)(2,1)S(1)}, u32[]{:S(2)}, u32[]{:S(2)}) %collective-permute-start.6) | collective-permute-done | bytes 196640 | tf_op jit(solution)/shard_map/ppermute | solution.py:52
  31.0 2.7 collective-permute-done.5.refs_6_
  39.5 4.8 %collective-permute-start.8 = (bf16[96,768]{1,0:T(8,128)(2,1)S(1)}, bf16[96,768]{1,0:T(8,128)(2,1)S(1)}, u32[]{:S(2)}, u32[]{:S(2)}) collective-permute-start(bf16[96,768]{1,0:T(8,128)(2,1)S(1)} %get-tuple-element.242.refs_0_), channel_id=1, source_target_pairs={{0,16},{4,20},{8,24},{12,28},{16,0},{20,4},{24,8},{28,12},{1,17},{... | collective-permute-start | bytes 442376 | tf_op jit(solution)/shard_map/ppermute | solution.py:52
  44.4 7.0 %time_forward.1 = (f32[16,768]{1,0:T(8,128)S(1)}, bf16[1024,768]{1,0:T(8,128)(2,1)S(1)}, bf16[1024,576]{1,0:T(8,128)(2,1)S(1)}, bf16[512,192]{1,0:T(8,128)(2,1)S...) custom-call(bf16[768,640]{1,0:T(8,128)(2,1)S(1)} %bitcast.44, ...), custom_call_target="tpu_custom_call" | custom-call | tf_op jit(solution)/shard_map/time_forward/pallas_call | solution.py:111
  66.9 9.2 %collective-permute-done.18.refs_4_ = bf16[4,96,768]{2,1,0:T(8,128)(2,1)S(1)} collective-permute-done((bf16[4,96,768]{2,1,0:T(8,128)(2,1)S(1)}, bf16[4,96,768]{2,1,0:T(8,128)(2,1)S(1)}, u32[]{:S(2)}, u32[]{:S(2)}) %collective-permute-start.18) | collective-permute-done | bytes 589856 | tf_op jit(solution)/shard_map/ppermute | solution.py:52
  76.8 3.1 %collective-permute-done.14.got_ref = bf16[512,768]{1,0:T(8,128)(2,1)S(1)} collective-permute-done((bf16[512,768]{1,0:T(8,128)(2,1)S(1)}, bf16[512,768]{1,0:T(8,128)(2,1)S(1)}, u32[]{:S(2)}, u32[]{:S(2)}) %collective-permute-start.14) | collective-permute-done | bytes 786464 | tf_op jit(solution)/shard_map/ppermute | solution.py:47
  88.6 7.3 %space_forward.1 = (bf16[512,384]{1,0:T(8,128)(2,1)S(1)}, f32[8,512]{1,0:T(8,128)S(1)}, f32[16,8]{1,0:T(8,128)S(1)}, bf16[512,768]{1,0:T(8,128)(2,1)S(1)}) custom-call(s32[5]{0:T(128)S(1)} %stack.47.place_ref, bf16[512,384]{1,0:T(8,128)(2,1)S(1)} %get-tuple-element.256.q_ref, bf16[512,768]{1,0:T(8,128)(2,1)S(1)} %get-tuple-element.257.pairs_ref, ...), custom_call_target="tpu_custom_call" | custom-call | tf_op jit(solution)/shard_map/space_forward/pallas_call | solution.py:111
  95.9 3.1 %collective-permute-done.22.refs_2_ = bf16[96,768]{1,0:T(8,128)(2,1)S(1)} collective-permute-done((bf16[96,768]{1,0:T(8,128)(2,1)S(1)}, bf16[96,768]{1,0:T(8,128)(2,1)S(1)}, u32[]{:S(2)}, u32[]{:S(2)}) %collective-permute-start.22) | collective-permute-done | bytes 147488 | tf_op jit(solution)/shard_map/ppermute | solution.py:52
  101.3 12.9 %collective-permute-done.27.refs_4_ = bf16[4,96,768]{2,1,0:T(8,128)(2,1)S(1)} collective-permute-done((bf16[4,96,768]{2,1,0:T(8,128)(2,1)S(1)}, bf16[4,96,768]{2,1,0:T(8,128)(2,1)S(1)}, u32[]{:S(2)}, u32[]{:S(2)}) %collective-permute-start.27) | collective-permute-done | bytes 589856 | tf_op jit(solution)/shard_map/ppermute | solution.py:52
  114.9 3.1 %collective-permute-done.25.got_ref = bf16[512,768]{1,0:T(8,128)(2,1)S(1)} collective-permute-done((bf16[512,768]{1,0:T(8,128)(2,1)S(1)}, bf16[512,768]{1,0:T(8,128)(2,1)S(1)}, u32[]{:S(2)}, u32[]{:S(2)}) %collective-permute-start.25) | collective-permute-done | bytes 786464 | tf_op jit(solution)/shard_map/ppermute | solution.py:47
  118.8 4.7 %feed.1 = (bf16[512,1536]{1,0:T(8,128)(2,1)S(1)}, bf16[512,1536]{1,0:T(8,128)(2,1)S(1)}, bf16[512,768]{1,0:T(8,128)(2,1)S(1)}) custom-call(bf16[512,768]{1,0:T(8,128)(2,1)S(1)} %get-tuple-element.262.third_ref, bf16[512,768]{1,0:T(8,128)(2,1)S(1)} %get-tuple-element.263.dy_ref, bf16[768,768]{1,0:T(8,128)(2,1)S(1)} %bitcast.42, ...), custom_call_target="tpu_custom_call" | custom-call | tf_op jit(solution)/shard_map/feed/pallas_call | solution.py:111
  133.4 11.6 %collective-permute-done.31.got_ref = bf16[512,768]{1,0:T(8,128)(2,1)S(1)} collective-permute-done((bf16[512,768]{1,0:T(8,128)(2,1)S(1)}, bf16[512,768]{1,0:T(8,128)(2,1)S(1)}, u32[]{:S(2)}, u32[]{:S(2)}) %collective-permute-start.31) | collective-permute-done | bytes 786464 | tf_op jit(solution)/shard_map/ppermute | solution.py:47
  145.0 2.9 %space_back_in.1 = (f32[512,768]{1,0:T(8,128)S(1)}, bf16[512,768]{1,0:T(8,128)(2,1)S(1)}, f32[8,768]{1,0:T(8,128)S(1)}, bf16[512,384]{1,0:T(8,128)(2,1)S(1)}) custom-call(bf16[512,768]{1,0:T(8,128)(2,1)S(1)} %get-tuple-element.274.part_ref, bf16[512,768]{1,0:T(8,128)(2,1)S(1)} %collective-permute-done.31.got_ref, ...), custom_call_target="tpu_custom_call" | custom-call | tf_op jit(solution)/shard_map/space_back_in/pallas_call | solution.py:111
  147.9 8.6 %space_backward.1 = (bf16[512,384]{1,0:T(8,128)(2,1)S(1)}, f32[512,768]{1,0:T(8,128)S(1)}, bf16[512,768]{1,0:T(8,128)(2,1)S(1)}) custom-call(s32[5]{0:T(128)S(1)} %stack.47.place_ref, bf16[512,384]{1,0:T(8,128)(2,1)S(1)} %get-tuple-element.277.heads_ref, bf16[512,384]{1,0:T(8,128)(2,1)S(1)} %get-tuple-element.256.q_ref, ...), custom_call_target="tpu_custom_call" | custom-call | tf_op jit(solution)/shard_map/space_backward/pallas_call | solution.py:111
  163.9 3.0 %collective-permute-start.35 = (bf16[96,768]{1,0:T(8,128)(2,1)S(1)}, bf16[96,768]{1,0:T(8,128)(2,1)S(1)}, u32[]{:S(2)}, u32[]{:S(2)}) collective-permute-start(bf16[96,768]{1,0:T(8,128)(2,1)S(1)} %get-tuple-element.290), channel_id=1, source_target_pairs={{0,16},{4,20},{8,24},{12,28},{16,0},{20,4},{24,8},{28,12},{1,17},{... | collective-permute-start | bytes 442376 | tf_op jit(solution)/shard_map/ppermute | solution.py:52
  171.9 6.0 %collective-permute-done.35 = bf16[96,768]{1,0:T(8,128)(2,1)S(1)} collective-permute-done((bf16[96,768]{1,0:T(8,128)(2,1)S(1)}, bf16[96,768]{1,0:T(8,128)(2,1)S(1)}, u32[]{:S(2)}, u32[]{:S(2)}) %collective-permute-start.35) | collective-permute-done | bytes 147488 | tf_op jit(solution)/shard_map/ppermute | solution.py:52
  178.0 3.9 %collective-permute-done.37.got_ref = bf16[512,768]{1,0:T(8,128)(2,1)S(1)} collective-permute-done((bf16[512,768]{1,0:T(8,128)(2,1)S(1)}, bf16[512,768]{1,0:T(8,128)(2,1)S(1)}, u32[]{:S(2)}, u32[]{:S(2)}) %collective-permute-start.37) | collective-permute-done | bytes 786464 | tf_op jit(solution)/shard_map/ppermute | solution.py:47
  189.9 3.0 %collective-permute-start.40 = (bf16[96,768]{1,0:T(8,128)(2,1)S(1)}, bf16[96,768]{1,0:T(8,128)(2,1)S(1)}, u32[]{:S(2)}, u32[]{:S(2)}) collective-permute-start(bf16[96,768]{1,0:T(8,128)(2,1)S(1)} %get-tuple-element.305), channel_id=1, source_target_pairs={{0,16},{4,20},{8,24},{12,28},{16,0},{20,4},{24,8},{28,12},{1,17},{... | collective-permute-start | bytes 442376 | tf_op jit(solution)/shard_map/ppermute | solution.py:52
  194.3 6.3 %time_backward.1.grad_ref = bf16[1024,576]{1,0:T(8,128)(2,1)S(1)} custom-call(bf16[512,192]{1,0:T(8,128)(2,1)S(1)} %get-tuple-element.318.own_ref, bf16[512,192]{1,0:T(8,128)(2,1)S(1)} %collective-permute-done.44.far_ref, bf16[1024,1024]{1,0:T(8,128)(2,1)S(1)} %get-tuple-element.320.order_ref, bf16[1024,576]{1,0:T(8,128)(2,1)S(1)} %get-tuple-element.321.inputs_ref, ...), custom_call_target="tpu_custom_call" | custom-call | tf_op jit(solution)/shard_map/time_backward/pallas_call | solution.py:111
  200.7 3.3 %collective-permute-done.40 = bf16[96,768]{1,0:T(8,128)(2,1)S(1)} collective-permute-done((bf16[96,768]{1,0:T(8,128)(2,1)S(1)}, bf16[96,768]{1,0:T(8,128)(2,1)S(1)}, u32[]{:S(2)}, u32[]{:S(2)}) %collective-permute-start.40) | collective-permute-done | bytes 147488 | tf_op jit(solution)/shard_map/ppermute | solution.py:52
  204.0 2.9 %collective-permute-done.45.refs_1_ = bf16[4,96,384]{2,1,0:T(8,128)(2,1)S(1)} collective-permute-done((bf16[4,96,384]{2,1,0:T(8,128)(2,1)S(1)}, bf16[4,96,384]{2,1,0:T(8,128)(2,1)S(1)}, u32[]{:S(2)}, u32[]{:S(2)}) %collective-permute-start.45) | collective-permute-done | bytes 294944 | tf_op jit(solution)/shard_map/ppermute | solution.py:52
  211.0 3.0 %collective-permute-start.48 = (bf16[96,1152]{1,0:T(8,128)(2,1)S(1)}, bf16[96,1152]{1,0:T(8,128)(2,1)S(1)}, u32[]{:S(2)}, u32[]{:S(2)}) collective-permute-start(bf16[96,1152]{1,0:T(8,128)(2,1)S(1)} %get-tuple-element.336), channel_id=1, source_target_pairs={{0,16},{4,20},{8,24},{12,28},{16,0},{20,4},{24,8},{28,12},{1,17},{... | collective-permute-start | bytes 663560 | tf_op jit(solution)/shard_map/ppermute | solution.py:52
  215.4 4.2 %time_back.1 = (bf16[512,768]{1,0:T(8,128)(2,1)S(1)}, bf16[512,768]{1,0:T(8,128)(2,1)S(1)}, f32[16,768]{1,0:T(8,128)S(1)}) custom-call(bf16[1024,576]{1,0:T(8,128)(2,1)S(1)} %time_backward.1.grad_ref, bf16[768,640]{1,0:T(8,128)(2,1)S(1)} %bitcast.45, bf16[1024,768]{1,0:T(8,128)(2,1)S(1)} %get-tuple-element.215.tokens_ref, ...), custom_call_target="tpu_custom_call" | custom-call | tf_op jit(solution)/shard_map/time_back/pallas_call | solution.py:111
  221.1 8.7 %collective-permute-done.48.refs_2_ = bf16[96,1152]{1,0:T(8,128)(2,1)S(1)} collective-permute-done((bf16[96,1152]{1,0:T(8,128)(2,1)S(1)}, bf16[96,1152]{1,0:T(8,128)(2,1)S(1)}, u32[]{:S(2)}, u32[]{:S(2)}) %collective-permute-start.48) | collective-permute-done | bytes 221216 | tf_op jit(solution)/shard_map/ppermute | solution.py:52
  242.8 2.7 collective-permute-start.55
  248.8 3.1 %layer_rows.1 = f32[1024,768]{1,0:T(8,128)} custom-call(s32[5]{0:T(128)S(1)} %stack.47.place_ref, f32[512,768]{1,0:T(8,128)S(1)} %layer_out.1.own_ref, f32[512,768]{1,0:T(8,128)} %collective-permute-done.54.got_ref), custom_call_target="tpu_custom_call" | custom-call | tf_op jit(solution)/shard_map/layer_rows/pallas_call | solution.py:1212
  251.9 5.3 %collective-permute-done.56 = bf16[96,640]{1,0:T(8,128)(2,1)S(1)} collective-permute-done((bf16[96,640]{1,0:T(8,128)(2,1)S(1)}, bf16[96,640]{1,0:T(8,128)(2,1)S(1)}, u32[]{:S(2)}, u32[]{:S(2)}) %collective-permute-start.56) | collective-permute-done | bytes 122912 | tf_op jit(solution)/shard_map/ppermute | solution.py:52
  277.7 6.0 %update.1 = (f32[96,3264]{1,0:T(8,128)}, f32[96,3264]{1,0:T(8,128)}, f32[96,3264]{1,0:T(8,128)}, f32[96,3264]{1,0:T(8,128)}, f32[10,96]{1,0:T(8,128)}, /*index=5...) custom-call(s32[5]{0:T(128)S(1)} %stack.47.place_ref, ...), custom_call_target="tpu_custom_call" | custom-call | tf_op jit(solution)/shard_map/update/pallas_call | solution.py:1356
  (269 shorter events, 118.3 us)
Async XLA Ops:
  2.9 15.5 %collective-permute-start = (bf16[96,1024]{1,0:T(8,128)(2,1)S(1)}, bf16[96,1024]{1,0:T(8,128)(2,1)S(1)}, u32[]{:S(2)}, u32[]{:S(2)}) collective-permute-start(bf16[96,1024]{1,0:T(8,128)(2,1)S(1)} %get-tuple-element.214.refs_0_), channel_id=1, source_target_pairs={{0,8},{4,12},{8,0},{12,4},{16,24},{20,28},{24,16},{28,20},{1,9},{5... | collective-permute-start | bytes 589832 | tf_op jit(solution)/shard_map/ppermute | solution.py:52
  6.0 17.2 %collective-permute-start.1 = (bf16[96,1024]{1,0:T(8,128)(2,1)S(1)}, bf16[96,1024]{1,0:T(8,128)(2,1)S(1)}, u32[]{:S(2)}, u32[]{:S(2)}) collective-permute-start(bf16[96,1024]{1,0:T(8,128)(2,1)S(1)} %get-tuple-element.214.refs_0_), channel_id=1, source_target_pairs={{0,16},{4,20},{8,24},{12,28},{16,0},{20,4},{24,8},{28,12},{1,17},{... | collective-permute-start | bytes 589832 | tf_op jit(solution)/shard_map/ppermute | solution.py:52
  8.6 14.6 %collective-permute-start.2 = (bf16[96,1024]{1,0:T(8,128)(2,1)S(1)}, bf16[96,1024]{1,0:T(8,128)(2,1)S(1)}, u32[]{:S(2)}, u32[]{:S(2)}) collective-permute-start(bf16[96,1024]{1,0:T(8,128)(2,1)S(1)} %get-tuple-element.214.refs_0_), channel_id=1, source_target_pairs={{0,24},{4,28},{8,16},{12,20},{16,8},{20,12},{24,0},{28,4},{1,25},{... | collective-permute-start | bytes 589832 | tf_op jit(solution)/shard_map/ppermute | solution.py:52
  8.6 18.1 %collective-permute-start.3 = (bf16[96,1024]{1,0:T(8,128)(2,1)S(1)}, bf16[96,1024]{1,0:T(8,128)(2,1)S(1)}, u32[]{:S(2)}, u32[]{:S(2)}) collective-permute-start(bf16[96,1024]{1,0:T(8,128)(2,1)S(1)} %get-tuple-element.214.refs_0_), channel_id=1, source_target_pairs={{0,4},{4,0},{8,12},{12,8},{16,20},{20,16},{24,28},{28,24},{1,5},{5... | collective-permute-start | bytes 589832 | tf_op jit(solution)/shard_map/ppermute | solution.py:52
  36.5 16.8 %collective-permute-start.10 = (bf16[768,192]{1,0:T(8,128)(2,1)S(1)}, bf16[768,192]{1,0:T(8,128)(2,1)S(1)}, u32[]{:S(2)}, u32[]{:S(2)}) collective-permute-start(bf16[768,192]{1,0:T(8,128)(2,1)S(1)} %bitcast.49), channel_id=1, source_target_pairs={{0,2},{1,3},{2,0},{3,1},{4,6},{5,7},{6,4},{7,5},{8,10},{9,11},{10,... | collective-permute-start | bytes 884744 | tf_op jit(solution)/shard_map/ppermute | solution.py:47
  38.1 13.2 %collective-permute-start.9 = (bf16[96,768]{1,0:T(8,128)(2,1)S(1)}, bf16[96,768]{1,0:T(8,128)(2,1)S(1)}, u32[]{:S(2)}, u32[]{:S(2)}) collective-permute-start(bf16[96,768]{1,0:T(8,128)(2,1)S(1)} %get-tuple-element.242.refs_0_), channel_id=1, source_target_pairs={{0,24},{4,28},{8,16},{12,20},{16,8},{20,12},{24,0},{28,4},{1,25},{... | collective-permute-start | bytes 442376 | tf_op jit(solution)/shard_map/ppermute | solution.py:52
  39.5 13.9 %collective-permute-start.8 = (bf16[96,768]{1,0:T(8,128)(2,1)S(1)}, bf16[96,768]{1,0:T(8,128)(2,1)S(1)}, u32[]{:S(2)}, u32[]{:S(2)}) collective-permute-start(bf16[96,768]{1,0:T(8,128)(2,1)S(1)} %get-tuple-element.242.refs_0_), channel_id=1, source_target_pairs={{0,16},{4,20},{8,24},{12,28},{16,0},{20,4},{24,8},{28,12},{1,17},{... | collective-permute-start | bytes 442376 | tf_op jit(solution)/shard_map/ppermute | solution.py:52
  60.3 19.6 %collective-permute-start.14 = (bf16[512,768]{1,0:T(8,128)(2,1)S(1)}, bf16[512,768]{1,0:T(8,128)(2,1)S(1)}, u32[]{:S(2)}, u32[]{:S(2)}) collective-permute-start(bf16[512,768]{1,0:T(8,128)(2,1)S(1)} %time_out.1.part_ref), channel_id=1, source_target_pairs={{0,2},{1,3},{2,0},{3,1},{4,6},{5,7},{6,4},{7,5},{8,10},{9,11},{10,... | collective-permute-start | bytes 2359304 | tf_op jit(solution)/shard_map/ppermute | solution.py:47
  61.0 15.2 %collective-permute-start.18 = (bf16[4,96,768]{2,1,0:T(8,128)(2,1)S(1)}, bf16[4,96,768]{2,1,0:T(8,128)(2,1)S(1)}, u32[]{:S(2)}, u32[]{:S(2)}) collective-permute-start(bf16[4,96,768]{2,1,0:T(8,128)(2,1)S(1)} %pad_maximum_fusion.2), channel_id=1, source_target_pairs={{0,4},{4,0},{8,12},{12,8},{16,20},{20,16},{24,28},{28,24},{1,5},{5... | collective-permute-start | bytes 1769480 | tf_op jit(solution)/shard_map/ppermute | solution.py:52
  62.6 19.9 %collective-permute-start.17 = (bf16[96,768]{1,0:T(8,128)(2,1)S(1)}, bf16[96,768]{1,0:T(8,128)(2,1)S(1)}, u32[]{:S(2)}, u32[]{:S(2)}) collective-permute-start(bf16[96,768]{1,0:T(8,128)(2,1)S(1)} %get-tuple-element.250.refs_0_), channel_id=1, source_target_pairs={{0,24},{4,28},{8,16},{12,20},{16,8},{20,12},{24,0},{28,4},{1,25},{... | collective-permute-start | bytes 442376 | tf_op jit(solution)/shard_map/ppermute | solution.py:52
  65.0 17.4 %collective-permute-start.16 = (bf16[96,768]{1,0:T(8,128)(2,1)S(1)}, bf16[96,768]{1,0:T(8,128)(2,1)S(1)}, u32[]{:S(2)}, u32[]{:S(2)}) collective-permute-start(bf16[96,768]{1,0:T(8,128)(2,1)S(1)} %get-tuple-element.250.refs_0_), channel_id=1, source_target_pairs={{0,16},{4,20},{8,24},{12,28},{16,0},{20,4},{24,8},{28,12},{1,17},{... | collective-permute-start | bytes 442376 | tf_op jit(solution)/shard_map/ppermute | solution.py:52
  65.0 17.4 %collective-permute-start.15 = (bf16[96,768]{1,0:T(8,128)(2,1)S(1)}, bf16[96,768]{1,0:T(8,128)(2,1)S(1)}, u32[]{:S(2)}, u32[]{:S(2)}) collective-permute-start(bf16[96,768]{1,0:T(8,128)(2,1)S(1)} %get-tuple-element.250.refs_0_), channel_id=1, source_target_pairs={{0,8},{4,12},{8,0},{12,4},{16,24},{20,28},{24,16},{28,20},{1,9},{5... | collective-permute-start | bytes 442376 | tf_op jit(solution)/shard_map/ppermute | solution.py:52
  82.6 16.4 %collective-permute-start.20 = (bf16[4,96,768]{2,1,0:T(8,128)(2,1)S(1)}, bf16[4,96,768]{2,1,0:T(8,128)(2,1)S(1)}, u32[]{:S(2)}, u32[]{:S(2)}) collective-permute-start(bf16[4,96,768]{2,1,0:T(8,128)(2,1)S(1)} %pad_maximum_fusion.3), channel_id=1, source_target_pairs={{0,4},{4,0},{8,12},{12,8},{16,20},{20,16},{24,28},{28,24},{1,5},{5... | collective-permute-start | bytes 1769480 | tf_op jit(solution)/shard_map/ppermute | solution.py:52
  86.7 12.4 %collective-permute-start.22 = (bf16[96,768]{1,0:T(8,128)(2,1)S(1)}, bf16[96,768]{1,0:T(8,128)(2,1)S(1)}, u32[]{:S(2)}, u32[]{:S(2)}) collective-permute-start(bf16[96,768]{1,0:T(8,128)(2,1)S(1)} %get-tuple-element.265.refs_0_), channel_id=1, source_target_pairs={{0,16},{4,20},{8,24},{12,28},{16,0},{20,4},{24,8},{28,12},{1,17},{... | collective-permute-start | bytes 442376 | tf_op jit(solution)/shard_map/ppermute | solution.py:52
  86.7 12.4 %collective-permute-start.21 = (bf16[96,768]{1,0:T(8,128)(2,1)S(1)}, bf16[96,768]{1,0:T(8,128)(2,1)S(1)}, u32[]{:S(2)}, u32[]{:S(2)}) collective-permute-start(bf16[96,768]{1,0:T(8,128)(2,1)S(1)} %get-tuple-element.265.refs_0_), channel_id=1, source_target_pairs={{0,8},{4,12},{8,0},{12,4},{16,24},{20,28},{24,16},{28,20},{1,9},{5... | collective-permute-start | bytes 442376 | tf_op jit(solution)/shard_map/ppermute | solution.py:52
  99.1 19.0 %collective-permute-start.25 = (bf16[512,768]{1,0:T(8,128)(2,1)S(1)}, bf16[512,768]{1,0:T(8,128)(2,1)S(1)}, u32[]{:S(2)}, u32[]{:S(2)}) collective-permute-start(bf16[512,768]{1,0:T(8,128)(2,1)S(1)} %get-tuple-element.261.part_ref), channel_id=1, source_target_pairs={{0,2},{1,3},{2,0},{3,1},{4,6},{5,7},{6,4},{7,5},{8,10},{9,11},{10,... | collective-permute-start | bytes 2359304 | tf_op jit(solution)/shard_map/ppermute | solution.py:47
  99.7 14.6 %collective-permute-start.27 = (bf16[4,96,768]{2,1,0:T(8,128)(2,1)S(1)}, bf16[4,96,768]{2,1,0:T(8,128)(2,1)S(1)}, u32[]{:S(2)}, u32[]{:S(2)}) collective-permute-start(bf16[4,96,768]{2,1,0:T(8,128)(2,1)S(1)} %pad_maximum_fusion.4), channel_id=1, source_target_pairs={{0,4},{4,0},{8,12},{12,8},{16,20},{20,16},{24,28},{28,24},{1,5},{5... | collective-permute-start | bytes 1769480 | tf_op jit(solution)/shard_map/ppermute | solution.py:52
  101.3 17.5 %collective-permute-start.26 = (bf16[768,768]{1,0:T(8,128)(2,1)S(1)}, bf16[768,768]{1,0:T(8,128)(2,1)S(1)}, u32[]{:S(2)}, u32[]{:S(2)}) collective-permute-start(bf16[768,768]{1,0:T(8,128)(2,1)S(1)} %bitcast.41), channel_id=1, source_target_pairs={{0,1},{1,0},{2,3},{3,2},{4,5},{5,4},{6,7},{7,6},{8,9},{9,8},{10,11... | collective-permute-start | bytes 3538952 | tf_op jit(solution)/shard_map/ppermute | solution.py:43
  125.0 20.0 %collective-permute-start.31 = (bf16[512,768]{1,0:T(8,128)(2,1)S(1)}, bf16[512,768]{1,0:T(8,128)(2,1)S(1)}, u32[]{:S(2)}, u32[]{:S(2)}) collective-permute-start(bf16[512,768]{1,0:T(8,128)(2,1)S(1)} %get-tuple-element.274.part_ref), channel_id=1, source_target_pairs={{0,2},{1,3},{2,0},{3,1},{4,6},{5,7},{6,4},{7,5},{8,10},{9,11},{10,... | collective-permute-start | bytes 2359304 | tf_op jit(solution)/shard_map/ppermute | solution.py:47
  130.6 25.9 %collective-permute-start.30 = (bf16[4,96,768]{2,1,0:T(8,128)(2,1)S(1)}, bf16[4,96,768]{2,1,0:T(8,128)(2,1)S(1)}, u32[]{:S(2)}, u32[]{:S(2)}) collective-permute-start(bf16[4,96,768]{2,1,0:T(8,128)(2,1)S(1)} %get-tuple-element.273), channel_id=1, source_target_pairs={{0,4},{4,0},{8,12},{12,8},{16,20},{20,16},{24,28},{28,24},{1,5},{5... | collective-permute-start | bytes 1769480 | tf_op jit(solution)/shard_map/ppermute | solution.py:52
  162.1 19.8 %collective-permute-start.37 = (bf16[512,768]{1,0:T(8,128)(2,1)S(1)}, bf16[512,768]{1,0:T(8,128)(2,1)S(1)}, u32[]{:S(2)}, u32[]{:S(2)}) collective-permute-start(bf16[512,768]{1,0:T(8,128)(2,1)S(1)} %get-tuple-element.286.part_ref), channel_id=1, source_target_pairs={{0,2},{1,3},{2,0},{3,1},{4,6},{5,7},{6,4},{7,5},{8,10},{9,11},{10,... | collective-permute-start | bytes 2359304 | tf_op jit(solution)/shard_map/ppermute | solution.py:47
  162.6 21.5 %collective-permute-start.32 = (bf16[4,96,768]{2,1,0:T(8,128)(2,1)S(1)}, bf16[4,96,768]{2,1,0:T(8,128)(2,1)S(1)}, u32[]{:S(2)}, u32[]{:S(2)}) collective-permute-start(bf16[4,96,768]{2,1,0:T(8,128)(2,1)S(1)} %get-tuple-element.282), channel_id=1, source_target_pairs={{0,4},{4,0},{8,12},{12,8},{16,20},{20,16},{24,28},{28,24},{1,5},{5... | collective-permute-start | bytes 1769480 | tf_op jit(solution)/shard_map/ppermute | solution.py:52
  163.9 14.1 %collective-permute-start.35 = (bf16[96,768]{1,0:T(8,128)(2,1)S(1)}, bf16[96,768]{1,0:T(8,128)(2,1)S(1)}, u32[]{:S(2)}, u32[]{:S(2)}) collective-permute-start(bf16[96,768]{1,0:T(8,128)(2,1)S(1)} %get-tuple-element.290), channel_id=1, source_target_pairs={{0,16},{4,20},{8,24},{12,28},{16,0},{20,4},{24,8},{28,12},{1,17},{... | collective-permute-start | bytes 442376 | tf_op jit(solution)/shard_map/ppermute | solution.py:52
  184.9 19.1 %collective-permute-start.42 = (bf16[4,96,768]{2,1,0:T(8,128)(2,1)S(1)}, bf16[4,96,768]{2,1,0:T(8,128)(2,1)S(1)}, u32[]{:S(2)}, u32[]{:S(2)}) collective-permute-start(bf16[4,96,768]{2,1,0:T(8,128)(2,1)S(1)} %get-tuple-element.296), channel_id=1, source_target_pairs={{0,4},{4,0},{8,12},{12,8},{16,20},{20,16},{24,28},{28,24},{1,5},{5... | collective-permute-start | bytes 1769480 | tf_op jit(solution)/shard_map/ppermute | solution.py:52
  188.6 18.3 %collective-permute-start.45 = (bf16[4,96,384]{2,1,0:T(8,128)(2,1)S(1)}, bf16[4,96,384]{2,1,0:T(8,128)(2,1)S(1)}, u32[]{:S(2)}, u32[]{:S(2)}) collective-permute-start(bf16[4,96,384]{2,1,0:T(8,128)(2,1)S(1)} %get-tuple-element.317), channel_id=1, source_target_pairs={{0,4},{4,0},{8,12},{12,8},{16,20},{20,16},{24,28},{28,24},{1,5},{5... | collective-permute-start | bytes 884744 | tf_op jit(solution)/shard_map/ppermute | solution.py:52
  189.9 14.1 %collective-permute-start.40 = (bf16[96,768]{1,0:T(8,128)(2,1)S(1)}, bf16[96,768]{1,0:T(8,128)(2,1)S(1)}, u32[]{:S(2)}, u32[]{:S(2)}) collective-permute-start(bf16[96,768]{1,0:T(8,128)(2,1)S(1)} %get-tuple-element.305), channel_id=1, source_target_pairs={{0,16},{4,20},{8,24},{12,28},{16,0},{20,4},{24,8},{28,12},{1,17},{... | collective-permute-start | bytes 442376 | tf_op jit(solution)/shard_map/ppermute | solution.py:52
  209.1 22.2 %collective-permute-start.50 = (bf16[512,768]{1,0:T(8,128)(2,1)S(1)}, bf16[512,768]{1,0:T(8,128)(2,1)S(1)}, u32[]{:S(2)}, u32[]{:S(2)}) collective-permute-start(bf16[512,768]{1,0:T(8,128)(2,1)S(1)} %feed_out.1.part_ref), channel_id=1, source_target_pairs={{0,2},{1,3},{2,0},{3,1},{4,6},{5,7},{6,4},{7,5},{8,10},{9,11},{10,... | collective-permute-start | bytes 2359304 | tf_op jit(solution)/shard_map/ppermute | solution.py:47
  209.7 21.5 %collective-permute-start.46 = (bf16[4,96,640]{2,1,0:T(8,128)(2,1)S(1)}, bf16[4,96,640]{2,1,0:T(8,128)(2,1)S(1)}, u32[]{:S(2)}, u32[]{:S(2)}) collective-permute-start(bf16[4,96,640]{2,1,0:T(8,128)(2,1)S(1)} %get-tuple-element.329), channel_id=1, source_target_pairs={{0,4},{4,0},{8,12},{12,8},{16,20},{20,16},{24,28},{28,24},{1,5},{5... | collective-permute-start | bytes 1474568 | tf_op jit(solution)/shard_map/ppermute | solution.py:52
  211.0 18.8 %collective-permute-start.48 = (bf16[96,1152]{1,0:T(8,128)(2,1)S(1)}, bf16[96,1152]{1,0:T(8,128)(2,1)S(1)}, u32[]{:S(2)}, u32[]{:S(2)}) collective-permute-start(bf16[96,1152]{1,0:T(8,128)(2,1)S(1)} %get-tuple-element.336), channel_id=1, source_target_pairs={{0,16},{4,20},{8,24},{12,28},{16,0},{20,4},{24,8},{28,12},{1,17},{... | collective-permute-start | bytes 663560 | tf_op jit(solution)/shard_map/ppermute | solution.py:52
  214.0 16.5 %collective-permute-start.49 = (bf16[96,1152]{1,0:T(8,128)(2,1)S(1)}, bf16[96,1152]{1,0:T(8,128)(2,1)S(1)}, u32[]{:S(2)}, u32[]{:S(2)}) collective-permute-start(bf16[96,1152]{1,0:T(8,128)(2,1)S(1)} %get-tuple-element.337), channel_id=1, source_target_pairs={{0,24},{4,28},{8,16},{12,20},{16,8},{20,12},{24,0},{28,4},{1,25},{... | collective-permute-start | bytes 663560 | tf_op jit(solution)/shard_map/ppermute | solution.py:52
  241.5 23.0 %collective-permute-start.62 = (bf16[512,768]{1,0:T(8,128)(2,1)S(1)}, bf16[512,768]{1,0:T(8,128)(2,1)}, u32[]{:S(2)}, u32[]{:S(2)}) collective-permute-start(bf16[512,768]{1,0:T(8,128)(2,1)S(1)} %first_part.1.part_ref), channel_id=1, source_target_pairs={{0,2},{1,3},{2,0},{3,1},{4,6},{5,7},{6,4},{7,5},{8,10},{9,11},{10,... | collective-permute-start | bytes 2359304 | tf_op jit(solution)/shard_map/ppermute | solution.py:47
  245.5 11.7 %collective-permute-start.56 = (bf16[96,640]{1,0:T(8,128)(2,1)S(1)}, bf16[96,640]{1,0:T(8,128)(2,1)S(1)}, u32[]{:S(2)}, u32[]{:S(2)}) collective-permute-start(bf16[96,640]{1,0:T(8,128)(2,1)S(1)} %get-tuple-element.361), channel_id=1, source_target_pairs={{0,16},{4,20},{8,24},{12,28},{16,0},{20,4},{24,8},{28,12},{1,17},{... | collective-permute-start | bytes 368648 | tf_op jit(solution)/shard_map/ppermute | solution.py:52
  (87 other events, 483.8 us)
